TPU v7x, 32 devices: a whole 2x2x4 slice. The times are simulated.
32 devices in a mesh: seq: 8 (over y, x, core), section: 4 (over z).
Axes of the slice: x: 2, y: 2, z: 4, core: 2. Of those that a mesh axis runs over, the one named last changes fastest.
Arguments:
- cotangent: bfloat16 [1, 1024, 768], P(None, 'seq'), may hold values from -6 to 6
- projected: bfloat16 [4, 1, 1024, 2304], P('section', None, 'seq'), may hold values from -6 to 6
- w_in: bfloat16 [4, 768, 2304], P('section'), may hold values from -0.21875 to 0.21875
- w_out: bfloat16 [4, 768, 768], P('section'), may hold values from -0.078125 to 0.078125
- short_filter: float32 [4, 3, 2304], P('section'), may hold values from -3.5 to 3.5
- long_filter: float32 [4, 1024, 768], P('section', 'seq'), may hold values from -1.1 to 1.1, as said below
- filter_bias: float32 [4, 768], P('section'), may hold values from 0.3 to 0.9
Outputs:
- grads: bfloat16 [4, 1, 1024, 768], P('section', None, 'seq')
Inputs may be any that keep to these rules, and one draw needn't show every extreme that they name: `long_filter`: row t of a section's long filter is its response at lag t.
All inputs are finite; a program needn't handle non-finite values.
Results may differ from a plain program's by a relative error of at most 0.03.
Values may be sent and summed in bfloat16 or wider, within the bound.
No kernel may reach another device: no remote copies, remote signals or barrier semaphores. Data moves between devices by JAX's collectives and lax.ppermute only.
A program may use at most 64 MiB of HBM per device.

v0:
```python
import math

import jax
import jax.numpy as jnp
from jax import lax
from jax.sharding import PartitionSpec as P

accuracy = lax.Precision.HIGH


def shifted(value, axis, by):
    count = lax.axis_size(axis)
    pairs = [(i, i + by) for i in range(count) if 0 <= i + by < count]
    return lax.ppermute(value, axis, pairs)


def phase_table(height, breadth, period):
    row_ids = lax.broadcasted_iota(jnp.int32, (height, breadth), 0)
    col_ids = lax.broadcasted_iota(jnp.int32, (height, breadth), 1)
    angle = (row_ids * col_ids % period).astype(jnp.float32) * (2.0 * math.pi / period)
    return (jnp.cos(angle), jnp.sin(angle))


def forward_spectrum(series, inner):
    length, chans = series.shape
    outer = 2 * length // inner
    blocks = series.reshape(length // inner, inner, chans)
    cos_outer, sin_outer = phase_table(outer, length // inner, outer)
    real_one = jnp.einsum("kn,nbc->cbk", cos_outer, blocks, precision=accuracy)
    imag_one = -jnp.einsum("kn,nbc->cbk", sin_outer, blocks, precision=accuracy)
    cos_twist, sin_twist = phase_table(inner, outer, 2 * length)
    real_two = real_one * cos_twist + imag_one * sin_twist
    imag_two = imag_one * cos_twist - real_one * sin_twist
    cos_inner, sin_inner = phase_table(inner, inner, inner)
    real = jnp.einsum("jb,cbk->cjk", cos_inner, real_two, precision=accuracy) + jnp.einsum(
        "jb,cbk->cjk", sin_inner, imag_two, precision=accuracy
    )
    imag = jnp.einsum("jb,cbk->cjk", cos_inner, imag_two, precision=accuracy) - jnp.einsum(
        "jb,cbk->cjk", sin_inner, real_two, precision=accuracy
    )
    return (real, imag)


def inverse_spectrum(real, imag, inner):
    chans, _, outer = real.shape
    length = outer * inner // 2
    cos_inner, sin_inner = phase_table(inner, inner, inner)
    real_one = jnp.einsum("jb,cjk->cbk", cos_inner, real, precision=accuracy) - jnp.einsum(
        "jb,cjk->cbk", sin_inner, imag, precision=accuracy
    )
    imag_one = jnp.einsum("jb,cjk->cbk", cos_inner, imag, precision=accuracy) + jnp.einsum(
        "jb,cjk->cbk", sin_inner, real, precision=accuracy
    )
    cos_twist, sin_twist = phase_table(inner, outer, 2 * length)
    real_two = real_one * cos_twist - imag_one * sin_twist
    imag_two = imag_one * cos_twist + real_one * sin_twist
    cos_outer, sin_outer = phase_table(outer, length // inner, outer)
    series = jnp.einsum("kn,cbk->nbc", cos_outer, real_two, precision=accuracy) - jnp.einsum(
        "kn,cbk->nbc", sin_outer, imag_two, precision=accuracy
    )
    return series.reshape(length, chans) / (2.0 * length)


def channel_conv(series, spectrum, bias_part, adjoint, inner):
    values = series.astype(jnp.float32)
    real, imag = forward_spectrum(values, inner)
    filter_real, filter_imag = spectrum
    if adjoint:
        prod_real = real * filter_real + imag * filter_imag
        prod_imag = imag * filter_real - real * filter_imag
    else:
        prod_real = real * filter_real - imag * filter_imag
        prod_imag = real * filter_imag + imag * filter_real
    return (inverse_spectrum(prod_real, prod_imag, inner) + bias_part * values).astype(jnp.bfloat16)


def when(active, action, *operands):

    def skipped(*inputs):
        return jax.tree.map(jnp.zeros_like, action(*inputs))

    return lax.cond(active, action, skipped, *operands)


def shards(cotangent, projected, w_in, w_out, short_filter, long_filter, filter_bias):
    seq_count = lax.axis_size("seq")
    seq_place = lax.axis_index("seq")
    section_count = lax.axis_size("section")
    section_place = lax.axis_index("section")
    micro = projected.shape[1]
    height = projected.shape[2]
    width = w_out.shape[2]
    length = height * seq_count
    inner = math.gcd(length, 32)
    chans = width // seq_count
    filter_local = lax.all_to_all(
        long_filter[0].astype(jnp.bfloat16), "seq", split_axis=1, concat_axis=0, tiled=True
    ).astype(jnp.float32)
    spectrum = forward_spectrum(filter_local, inner)
    bias_part = lax.dynamic_slice_in_dim(filter_bias[0], seq_place * chans, chans, 0)
    weight_in = w_in[0]
    weight_out = w_out[0]
    taps = short_filter[0]
    stored = projected[0]
    last_section = section_place == section_count - 1
    contract = (((1,), (1,)), ((), ()))

    def forward_part(grad_out, proj, rim):
        padded = jnp.concatenate([rim, proj], axis=0).astype(jnp.float32)
        mixed = taps[0] * padded[2:] + taps[1] * padded[1:-1] + taps[2] * padded[:-2]
        query = mixed[:, :width]
        keys = mixed[:, width : 2 * width]
        values = mixed[:, 2 * width :]
        product = (keys * values).astype(jnp.bfloat16)
        d_out = lax.dot_general(grad_out, weight_out, contract, preferred_element_type=jnp.float32)
        d_conv = (d_out * query).astype(jnp.bfloat16)
        return (product, d_conv, d_out, keys, values)

    def causal(series):
        return channel_conv(series, spectrum, bias_part, False, inner)

    def adjoint(series):
        return channel_conv(series, spectrum, bias_part, True, inner)

    def backward_part(d_out, conv, d_prod, keys, values):
        d_prod_wide = d_prod.astype(jnp.float32)
        return jnp.concatenate(
            [d_out * conv.astype(jnp.float32), d_prod_wide * values, d_prod_wide * keys], axis=1
        ).astype(jnp.bfloat16)

    def input_part(grad_out, d_mixed, rim):
        padded = jnp.concatenate([d_mixed, rim], axis=0).astype(jnp.float32)
        d_proj = (taps[0] * padded[:-2] + taps[1] * padded[1:-1] + taps[2] * padded[2:]).astype(
            jnp.bfloat16
        )
        total = grad_out.astype(jnp.float32) + lax.dot_general(
            d_proj, weight_in, contract, preferred_element_type=jnp.float32
        )
        return total.astype(jnp.bfloat16)

    def tick(step, carry):
        incoming, grads = carry
        index = step - (section_count - 1 - section_place)
        active = (index >= 0) & (index < micro)
        slot = jnp.clip(index, 0, micro - 1)
        top = lax.dynamic_index_in_dim(cotangent, slot, 0, keepdims=False)
        grad_out = jnp.where(last_section, top, incoming)
        proj = lax.dynamic_index_in_dim(stored, slot, 0, keepdims=False)
        rim = shifted(proj[height - 2 :], "seq", 1)
        product, d_conv, d_out, keys, values = when(active, forward_part, grad_out, proj, rim)
        product_local = lax.all_to_all(product, "seq", split_axis=1, concat_axis=0, tiled=True)
        conv = lax.all_to_all(
            when(active, causal, product_local), "seq", split_axis=0, concat_axis=1, tiled=True
        )
        d_conv_local = lax.all_to_all(d_conv, "seq", split_axis=1, concat_axis=0, tiled=True)
        d_prod = lax.all_to_all(
            when(active, adjoint, d_conv_local), "seq", split_axis=0, concat_axis=1, tiled=True
        )
        d_mixed = when(active, backward_part, d_out, conv, d_prod, keys, values)
        rim_below = shifted(d_mixed[:2], "seq", -1)
        d_input = when(active, input_part, grad_out, d_mixed, rim_below)
        grads = jnp.where(active, lax.dynamic_update_index_in_dim(grads, d_input, slot, 0), grads)
        incoming = shifted(d_input, "section", -1)
        return (incoming, grads)

    start = (
        jnp.zeros((height, width), jnp.bfloat16),
        jnp.zeros((micro, height, width), jnp.bfloat16),
    )
    incoming, grads = lax.fori_loop(0, micro + section_count - 1, tick, start)
    return grads[None]


def solution(mesh):
    return jax.shard_map(
        shards,
        mesh=mesh,
        in_specs=(
            P(None, "seq", None),
            P("section", None, "seq", None),
            P("section", None, None),
            P("section", None, None),
            P("section", None, None),
            P("section", "seq", None),
            P("section", None),
        ),
        out_specs=P("section", None, "seq", None),
        check_vma=False,
    )
```

profile of v0, /device:TPU:0, one launch (start us, length us, event | category | flops | bytes accessed | tf_op | source)
XLA Modules:
  0.0 429.7 jit_solution(9222052991891269948)
XLA Ops:
  5.7 5.0 %all-to-all-start.4 = ((bf16[128,8,96]{0,2,1:T(8,128)(2,1)}), bf16[128,8,96]{0,2,1:T(8,128)(2,1)S(1)}, u32[]{:S(2)}, u32[]{:S(2)}) async-start(bf16[128,8,96]{0,2,1:T(8,128)(2,1)} %bitcast.45), calls=%async_computation.4 | async-start | bytes 393216 | tf_op jit(solution)/shard_map/all_to_all | solution.py:96
  10.9 6.1 %all-to-all-done.4 = bf16[128,8,96]{0,2,1:T(8,128)(2,1)S(1)} async-done(((bf16[128,8,96]{0,2,1:T(8,128)(2,1)}), bf16[128,8,96]{0,2,1:T(8,128)(2,1)S(1)}, u32[]{:S(2)}, u32[]{:S(2)}) %all-to-all-start.4) | async-done | bytes 196640 | tf_op jit(solution)/shard_map/all_to_all | solution.py:96
  23.6 405.0 %while.18 = (s32[]{:T(128)}, bf16[128,768]{1,0:T(8,128)(2,1)S(1)}, bf16[1,128,768]{2,1,0:T(8,128)(2,1)}, s32[]{:T(128)}, pred[]{:T(512)}, /*index=5*/bf16[1,128,...) while((s32[]{:T(128)}, bf16[128,768]{1,0:T(8,128)(2,1)S(1)}, ...), condition=%wide.region_11.12_spmd.clone, body=%wide.region_0.11_spmd.clone.sunk | while | flops 1530654720 | bytes 99115448 | solution.py:170
  32.1 5.4 %all-to-all-done.2 = bf16[128,8,96]{0,2,1:T(8,128)(2,1)} async-done(((bf16[128,8,96]{0,2,1:T(8,128)(2,1)}), bf16[128,8,96]{0,2,1:T(8,128)(2,1)}, u32[]{:S(2)}, u32[]{:S(2)}) %all-to-all-start.2) | async-done | bytes 196640 | tf_op jit(solution)/shard_map/while/body/eval_jaxpr/all_to_all | solution.py:155
  41.5 9.1 %conditional.17 = (bf16[1024,96]{1,0:T(8,128)(2,1)S(1)}) conditional(s32[]{:T(128)} %convert_element_type.389, () %tuple.126, (bf16[8,128,96]{1,2,0:T(8,128)(2,1)}, f32[96,32,64]{0,1,2:T(8,128)S(1)}, f32[96,32,64]{0,1,2:T(8,128)S(1)}, f32[96]{0:T(128)S(1)}) %tuple.127), branch_computations={%region_3.3_spmd, %region_4.4_spmd} | conditional | flops 458747904 | bytes 30343560 | solution.py:82
  51.4 4.1 all-to-all-start.3
  65.3 6.2 %all-to-all-done.1 = bf16[8,128,96]{1,2,0:T(8,128)(2,1)S(1)} async-done(((bf16[8,128,96]{1,2,0:T(8,128)(2,1)}), bf16[8,128,96]{1,2,0:T(8,128)(2,1)S(1)}, u32[]{:S(2)}, u32[]{:S(2)}) %all-to-all-start.1) | async-done | bytes 196640 | tf_op jit(solution)/shard_map/while/body/eval_jaxpr/all_to_all | solution.py:152
  77.6 7.5 %collective-permute-done.1 = bf16[128,768]{1,0:T(8,128)(2,1)S(1)} collective-permute-done((bf16[128,768]{1,0:T(8,128)(2,1)}, bf16[128,768]{1,0:T(8,128)(2,1)S(1)}, u32[]{:S(2)}, u32[]{:S(2)}) %collective-permute-start.1) | collective-permute-done | bytes 196640 | tf_op jit(solution)/shard_map/while/body/eval_jaxpr/ppermute | solution.py:14
  93.7 5.4 %all-to-all-done.2 = bf16[128,8,96]{0,2,1:T(8,128)(2,1)} async-done(((bf16[128,8,96]{0,2,1:T(8,128)(2,1)}), bf16[128,8,96]{0,2,1:T(8,128)(2,1)}, u32[]{:S(2)}, u32[]{:S(2)}) %all-to-all-start.2) | async-done | bytes 196640 | tf_op jit(solution)/shard_map/while/body/eval_jaxpr/all_to_all | solution.py:155
  103.2 8.9 %conditional.17 = (bf16[1024,96]{1,0:T(8,128)(2,1)S(1)}) conditional(s32[]{:T(128)} %convert_element_type.389, () %tuple.126, (bf16[8,128,96]{1,2,0:T(8,128)(2,1)}, f32[96,32,64]{0,1,2:T(8,128)S(1)}, f32[96,32,64]{0,1,2:T(8,128)S(1)}, f32[96]{0:T(128)S(1)}) %tuple.127), branch_computations={%region_3.3_spmd, %region_4.4_spmd} | conditional | flops 458747904 | bytes 30343560 | solution.py:82
  126.7 6.2 %all-to-all-done.1 = bf16[8,128,96]{1,2,0:T(8,128)(2,1)S(1)} async-done(((bf16[8,128,96]{1,2,0:T(8,128)(2,1)}), bf16[8,128,96]{1,2,0:T(8,128)(2,1)S(1)}, u32[]{:S(2)}, u32[]{:S(2)}) %all-to-all-start.1) | async-done | bytes 196640 | tf_op jit(solution)/shard_map/while/body/eval_jaxpr/all_to_all | solution.py:152
  140.0 6.5 %collective-permute-done.1 = bf16[128,768]{1,0:T(8,128)(2,1)S(1)} collective-permute-done((bf16[128,768]{1,0:T(8,128)(2,1)}, bf16[128,768]{1,0:T(8,128)(2,1)S(1)}, u32[]{:S(2)}, u32[]{:S(2)}) %collective-permute-start.1) | collective-permute-done | bytes 196640 | tf_op jit(solution)/shard_map/while/body/eval_jaxpr/ppermute | solution.py:14
  154.9 5.4 %all-to-all-done.2 = bf16[128,8,96]{0,2,1:T(8,128)(2,1)} async-done(((bf16[128,8,96]{0,2,1:T(8,128)(2,1)}), bf16[128,8,96]{0,2,1:T(8,128)(2,1)}, u32[]{:S(2)}, u32[]{:S(2)}) %all-to-all-start.2) | async-done | bytes 196640 | tf_op jit(solution)/shard_map/while/body/eval_jaxpr/all_to_all | solution.py:155
  164.3 8.9 %conditional.17 = (bf16[1024,96]{1,0:T(8,128)(2,1)S(1)}) conditional(s32[]{:T(128)} %convert_element_type.389, () %tuple.126, (bf16[8,128,96]{1,2,0:T(8,128)(2,1)}, f32[96,32,64]{0,1,2:T(8,128)S(1)}, f32[96,32,64]{0,1,2:T(8,128)S(1)}, f32[96]{0:T(128)S(1)}) %tuple.127), branch_computations={%region_3.3_spmd, %region_4.4_spmd} | conditional | flops 458747904 | bytes 30343560 | solution.py:82
  187.9 6.2 %all-to-all-done.1 = bf16[8,128,96]{1,2,0:T(8,128)(2,1)S(1)} async-done(((bf16[8,128,96]{1,2,0:T(8,128)(2,1)}), bf16[8,128,96]{1,2,0:T(8,128)(2,1)S(1)}, u32[]{:S(2)}, u32[]{:S(2)}) %all-to-all-start.1) | async-done | bytes 196640 | tf_op jit(solution)/shard_map/while/body/eval_jaxpr/all_to_all | solution.py:152
  201.2 125.0 %collective-permute-done.1 = bf16[128,768]{1,0:T(8,128)(2,1)S(1)} collective-permute-done((bf16[128,768]{1,0:T(8,128)(2,1)}, bf16[128,768]{1,0:T(8,128)(2,1)S(1)}, u32[]{:S(2)}, u32[]{:S(2)}) %collective-permute-start.1) | collective-permute-done | bytes 196640 | tf_op jit(solution)/shard_map/while/body/eval_jaxpr/ppermute | solution.py:14
  327.8 5.9 %conditional.15 = (bf16[128,768]{1,0:T(8,128)(2,1)S(1)}, bf16[128,768]{1,0:T(8,128)(2,1)S(1)}, f32[128,768]{1,0:T(8,128)}, f32[128,768]{1,0:T(8,128)S(1)}, f32[128,768]{1,0:T(8,128)S(1)}) conditional(s32[]{:T(128)} %convert_element_type.389, () %tuple.123, (f32[3,2304]{1,0:T(4,128)S(1)}, bf16[1,128,2304]{2,1,0:T(8,128)(2,1)}, ...), branch_computations={%region_1.1_spmd, %region_2.2_spmd} | conditional | flops 154060800 | bytes 15839300 | solution.py:82
  339.4 5.4 %all-to-all-done.2 = bf16[128,8,96]{0,2,1:T(8,128)(2,1)} async-done(((bf16[128,8,96]{0,2,1:T(8,128)(2,1)}), bf16[128,8,96]{0,2,1:T(8,128)(2,1)}, u32[]{:S(2)}, u32[]{:S(2)}) %all-to-all-start.2) | async-done | bytes 196640 | tf_op jit(solution)/shard_map/while/body/eval_jaxpr/all_to_all | solution.py:155
  348.8 22.8 %conditional.17 = (bf16[1024,96]{1,0:T(8,128)(2,1)S(1)}) conditional(s32[]{:T(128)} %convert_element_type.389, () %tuple.126, (bf16[8,128,96]{1,2,0:T(8,128)(2,1)}, f32[96,32,64]{0,1,2:T(8,128)S(1)}, f32[96,32,64]{0,1,2:T(8,128)S(1)}, f32[96]{0:T(128)S(1)}) %tuple.127), branch_computations={%region_3.3_spmd, %region_4.4_spmd} | conditional | flops 458747904 | bytes 30343560 | solution.py:82
  376.5 18.3 %conditional.16 = (bf16[1024,96]{1,0:T(8,128)(2,1)S(1)}) conditional(s32[]{:T(128)} %convert_element_type.389, () %tuple.122, (bf16[8,128,96]{1,2,0:T(8,128)(2,1)}, f32[96,32,64]{0,1,2:T(8,128)S(1)}, f32[96,32,64]{0,1,2:T(8,128)S(1)}, f32[96]{0:T(128)S(1)}) %tuple.125), branch_computations={%region_5.5_spmd, %region_6.6_spmd} | conditional | flops 458747904 | bytes 30343560 | solution.py:82
  395.7 4.2 all-to-all-start.1
  399.9 6.2 %all-to-all-done.1 = bf16[8,128,96]{1,2,0:T(8,128)(2,1)S(1)} async-done(((bf16[8,128,96]{1,2,0:T(8,128)(2,1)}), bf16[8,128,96]{1,2,0:T(8,128)(2,1)S(1)}, u32[]{:S(2)}, u32[]{:S(2)}) %all-to-all-start.1) | async-done | bytes 196640 | tf_op jit(solution)/shard_map/while/body/eval_jaxpr/all_to_all | solution.py:152
  412.9 5.3 %conditional.19 = (bf16[128,768]{1,0:T(8,128)(2,1)}, bf16[1,128,768]{2,1,0:T(8,128)(2,1)S(1)}) conditional(s32[]{:T(128)} %convert_element_type.389, () %tuple.120, (bf16[128,768]{1,0:T(8,128)(2,1)}, f32[3,2304]{1,0:T(4,128)S(1)}, bf16[128,2304]{0,1:T(8,128)(2,1)S(1)}, bf16[2,2304]{1,0:T(2,128)(2,1)S(1)}, bf16[768,2304]{1,0:T(8,128)(2,1)}) %tuple.129), branch_computations={%region_9.9_spmd, %region_10.10_spmd} | conditional | flops 456247296 | bytes 10933264 | solution.py:82
  421.1 6.5 %collective-permute-done.1 = bf16[128,768]{1,0:T(8,128)(2,1)S(1)} collective-permute-done((bf16[128,768]{1,0:T(8,128)(2,1)}, bf16[128,768]{1,0:T(8,128)(2,1)S(1)}, u32[]{:S(2)}, u32[]{:S(2)}) %collective-permute-start.1) | collective-permute-done | bytes 196640 | tf_op jit(solution)/shard_map/while/body/eval_jaxpr/ppermute | solution.py:14
  (172 shorter events, 191.6 us)
Async XLA Ops:
  0.8 22.7 %collective-permute-start.2 = (bf16[2,2304]{1,0:T(2,128)(2,1)S(1)}, bf16[2,2304]{1,0:T(2,128)(2,1)S(1)}, u32[]{:S(2)}, u32[]{:S(2)}) collective-permute-start(bf16[2,2304]{1,0:T(2,128)(2,1)S(1)} %slice_bitcast_fusion), channel_id=1, source_target_pairs={{0,4},{4,8},{8,12},{12,16},{16,20},{20,24},{24,28},{1,5},{5,9},{9,... | collective-permute-start | bytes 27656 | tf_op jit(solution)/shard_map/while/body/eval_jaxpr/ppermute | solution.py:14
  5.7 11.3 %all-to-all-start.4 = ((bf16[128,8,96]{0,2,1:T(8,128)(2,1)}), bf16[128,8,96]{0,2,1:T(8,128)(2,1)S(1)}, u32[]{:S(2)}, u32[]{:S(2)}) async-start(bf16[128,8,96]{0,2,1:T(8,128)(2,1)} %bitcast.45), calls=%async_computation.4 | async-start | bytes 393216 | tf_op jit(solution)/shard_map/all_to_all | solution.py:96
  27.2 10.3 %all-to-all-start.2 = ((bf16[128,8,96]{0,2,1:T(8,128)(2,1)}), bf16[128,8,96]{0,2,1:T(8,128)(2,1)}, u32[]{:S(2)}, u32[]{:S(2)}) async-start(bf16[128,8,96]{0,2,1:T(8,128)(2,1)} %bitcast.226), calls=%async_computation.2 | async-start | bytes 393216 | tf_op jit(solution)/shard_map/while/body/eval_jaxpr/all_to_all | solution.py:155
  37.5 13.9 %all-to-all-start = ((bf16[128,8,96]{0,2,1:T(8,128)(2,1)}), bf16[128,8,96]{0,2,1:T(8,128)(2,1)}, u32[]{:S(2)}, u32[]{:S(2)}) async-start(bf16[128,8,96]{0,2,1:T(8,128)(2,1)} %bitcast.222), calls=%async_computation | async-start | bytes 393216 | tf_op jit(solution)/shard_map/while/body/eval_jaxpr/all_to_all | solution.py:151
  51.4 10.4 %all-to-all-start.3 = ((bf16[8,128,96]{1,2,0:T(8,128)(2,1)}), bf16[8,128,96]{1,2,0:T(8,128)(2,1)}, u32[]{:S(2)}, u32[]{:S(2)}) async-start(bf16[8,128,96]{1,2,0:T(8,128)(2,1)} %copy.276), calls=%async_computation.3 | async-start | bytes 393216 | tf_op jit(solution)/shard_map/while/body/eval_jaxpr/all_to_all | solution.py:156
  61.9 9.6 %all-to-all-start.1 = ((bf16[8,128,96]{1,2,0:T(8,128)(2,1)}), bf16[8,128,96]{1,2,0:T(8,128)(2,1)S(1)}, u32[]{:S(2)}, u32[]{:S(2)}) async-start(bf16[8,128,96]{1,2,0:T(8,128)(2,1)} %copy.274), calls=%async_computation.1 | async-start | bytes 393216 | tf_op jit(solution)/shard_map/while/body/eval_jaxpr/all_to_all | solution.py:152
  71.8 3.1 collective-permute-start
  75.6 9.5 %collective-permute-start.1 = (bf16[128,768]{1,0:T(8,128)(2,1)}, bf16[128,768]{1,0:T(8,128)(2,1)S(1)}, u32[]{:S(2)}, u32[]{:S(2)}) collective-permute-start(bf16[128,768]{1,0:T(8,128)(2,1)} %get-tuple-element.667), channel_id=1, source_target_pairs={{1,0},{2,1},{3,2},{5,4},{6,5},{7,6},{9,8},{10,9},{11,10},{13,12},{... | collective-permute-start | bytes 589832 | tf_op jit(solution)/shard_map/while/body/eval_jaxpr/ppermute | solution.py:14
  88.8 10.3 %all-to-all-start.2 = ((bf16[128,8,96]{0,2,1:T(8,128)(2,1)}), bf16[128,8,96]{0,2,1:T(8,128)(2,1)}, u32[]{:S(2)}, u32[]{:S(2)}) async-start(bf16[128,8,96]{0,2,1:T(8,128)(2,1)} %bitcast.226), calls=%async_computation.2 | async-start | bytes 393216 | tf_op jit(solution)/shard_map/while/body/eval_jaxpr/all_to_all | solution.py:155
  99.1 13.8 %all-to-all-start = ((bf16[128,8,96]{0,2,1:T(8,128)(2,1)}), bf16[128,8,96]{0,2,1:T(8,128)(2,1)}, u32[]{:S(2)}, u32[]{:S(2)}) async-start(bf16[128,8,96]{0,2,1:T(8,128)(2,1)} %bitcast.222), calls=%async_computation | async-start | bytes 393216 | tf_op jit(solution)/shard_map/while/body/eval_jaxpr/all_to_all | solution.py:151
  112.9 10.4 %all-to-all-start.3 = ((bf16[8,128,96]{1,2,0:T(8,128)(2,1)}), bf16[8,128,96]{1,2,0:T(8,128)(2,1)}, u32[]{:S(2)}, u32[]{:S(2)}) async-start(bf16[8,128,96]{1,2,0:T(8,128)(2,1)} %copy.276), calls=%async_computation.3 | async-start | bytes 393216 | tf_op jit(solution)/shard_map/while/body/eval_jaxpr/all_to_all | solution.py:156
  123.3 9.6 %all-to-all-start.1 = ((bf16[8,128,96]{1,2,0:T(8,128)(2,1)}), bf16[8,128,96]{1,2,0:T(8,128)(2,1)S(1)}, u32[]{:S(2)}, u32[]{:S(2)}) async-start(bf16[8,128,96]{1,2,0:T(8,128)(2,1)} %copy.274), calls=%async_computation.1 | async-start | bytes 393216 | tf_op jit(solution)/shard_map/while/body/eval_jaxpr/all_to_all | solution.py:152
  137.0 9.5 %collective-permute-start.1 = (bf16[128,768]{1,0:T(8,128)(2,1)}, bf16[128,768]{1,0:T(8,128)(2,1)S(1)}, u32[]{:S(2)}, u32[]{:S(2)}) collective-permute-start(bf16[128,768]{1,0:T(8,128)(2,1)} %get-tuple-element.667), channel_id=1, source_target_pairs={{1,0},{2,1},{3,2},{5,4},{6,5},{7,6},{9,8},{10,9},{11,10},{13,12},{... | collective-permute-start | bytes 589832 | tf_op jit(solution)/shard_map/while/body/eval_jaxpr/ppermute | solution.py:14
  150.0 10.3 %all-to-all-start.2 = ((bf16[128,8,96]{0,2,1:T(8,128)(2,1)}), bf16[128,8,96]{0,2,1:T(8,128)(2,1)}, u32[]{:S(2)}, u32[]{:S(2)}) async-start(bf16[128,8,96]{0,2,1:T(8,128)(2,1)} %bitcast.226), calls=%async_computation.2 | async-start | bytes 393216 | tf_op jit(solution)/shard_map/while/body/eval_jaxpr/all_to_all | solution.py:155
  160.3 13.8 %all-to-all-start = ((bf16[128,8,96]{0,2,1:T(8,128)(2,1)}), bf16[128,8,96]{0,2,1:T(8,128)(2,1)}, u32[]{:S(2)}, u32[]{:S(2)}) async-start(bf16[128,8,96]{0,2,1:T(8,128)(2,1)} %bitcast.222), calls=%async_computation | async-start | bytes 393216 | tf_op jit(solution)/shard_map/while/body/eval_jaxpr/all_to_all | solution.py:151
  174.1 10.4 %all-to-all-start.3 = ((bf16[8,128,96]{1,2,0:T(8,128)(2,1)}), bf16[8,128,96]{1,2,0:T(8,128)(2,1)}, u32[]{:S(2)}, u32[]{:S(2)}) async-start(bf16[8,128,96]{1,2,0:T(8,128)(2,1)} %copy.276), calls=%async_computation.3 | async-start | bytes 393216 | tf_op jit(solution)/shard_map/while/body/eval_jaxpr/all_to_all | solution.py:156
  184.5 9.6 %all-to-all-start.1 = ((bf16[8,128,96]{1,2,0:T(8,128)(2,1)}), bf16[8,128,96]{1,2,0:T(8,128)(2,1)S(1)}, u32[]{:S(2)}, u32[]{:S(2)}) async-start(bf16[8,128,96]{1,2,0:T(8,128)(2,1)} %copy.274), calls=%async_computation.1 | async-start | bytes 393216 | tf_op jit(solution)/shard_map/while/body/eval_jaxpr/all_to_all | solution.py:152
  194.4 3.1 collective-permute-start
  198.2 128.0 %collective-permute-start.1 = (bf16[128,768]{1,0:T(8,128)(2,1)}, bf16[128,768]{1,0:T(8,128)(2,1)S(1)}, u32[]{:S(2)}, u32[]{:S(2)}) collective-permute-start(bf16[128,768]{1,0:T(8,128)(2,1)} %get-tuple-element.667), channel_id=1, source_target_pairs={{1,0},{2,1},{3,2},{5,4},{6,5},{7,6},{9,8},{10,9},{11,10},{13,12},{... | collective-permute-start | bytes 589832 | tf_op jit(solution)/shard_map/while/body/eval_jaxpr/ppermute | solution.py:14
  334.5 10.3 %all-to-all-start.2 = ((bf16[128,8,96]{0,2,1:T(8,128)(2,1)}), bf16[128,8,96]{0,2,1:T(8,128)(2,1)}, u32[]{:S(2)}, u32[]{:S(2)}) async-start(bf16[128,8,96]{0,2,1:T(8,128)(2,1)} %bitcast.226), calls=%async_computation.2 | async-start | bytes 393216 | tf_op jit(solution)/shard_map/while/body/eval_jaxpr/all_to_all | solution.py:155
  344.8 27.6 %all-to-all-start = ((bf16[128,8,96]{0,2,1:T(8,128)(2,1)}), bf16[128,8,96]{0,2,1:T(8,128)(2,1)}, u32[]{:S(2)}, u32[]{:S(2)}) async-start(bf16[128,8,96]{0,2,1:T(8,128)(2,1)} %bitcast.222), calls=%async_computation | async-start | bytes 393216 | tf_op jit(solution)/shard_map/while/body/eval_jaxpr/all_to_all | solution.py:151
  372.4 23.2 %all-to-all-start.3 = ((bf16[8,128,96]{1,2,0:T(8,128)(2,1)}), bf16[8,128,96]{1,2,0:T(8,128)(2,1)}, u32[]{:S(2)}, u32[]{:S(2)}) async-start(bf16[8,128,96]{1,2,0:T(8,128)(2,1)} %copy.276), calls=%async_computation.3 | async-start | bytes 393216 | tf_op jit(solution)/shard_map/while/body/eval_jaxpr/all_to_all | solution.py:156
  395.7 10.4 %all-to-all-start.1 = ((bf16[8,128,96]{1,2,0:T(8,128)(2,1)}), bf16[8,128,96]{1,2,0:T(8,128)(2,1)S(1)}, u32[]{:S(2)}, u32[]{:S(2)}) async-start(bf16[8,128,96]{1,2,0:T(8,128)(2,1)} %copy.274), calls=%async_computation.1 | async-start | bytes 393216 | tf_op jit(solution)/shard_map/while/body/eval_jaxpr/all_to_all | solution.py:152
  418.2 9.5 %collective-permute-start.1 = (bf16[128,768]{1,0:T(8,128)(2,1)}, bf16[128,768]{1,0:T(8,128)(2,1)S(1)}, u32[]{:S(2)}, u32[]{:S(2)}) collective-permute-start(bf16[128,768]{1,0:T(8,128)(2,1)} %get-tuple-element.667), channel_id=1, source_target_pairs={{1,0},{2,1},{3,2},{5,4},{6,5},{7,6},{9,8},{10,9},{11,10},{13,12},{... | collective-permute-start | bytes 589832 | tf_op jit(solution)/shard_map/while/body/eval_jaxpr/ppermute | solution.py:14
  (4 other events, 18.2 us)
where the time goes:
time: 437 us; the launch traced here: 430 us
  waiting for transfers between devices  213 us (49%)
  starting transfers between devices  80.6 us (18%)
  matrix products  45.3 us (10%)
  loops' own time  42.3 us (10%)
  local copies, waits for them, and re-layouts  30.3 us (7%)
  other arithmetic  16.6 us (4%)
    ppermute x9, waiting for transfers between devices, shifted(): return lax.ppermute(value, axis, pairs)  153 us
    another operation x20, loops' own time, when(): return lax.cond(active, action, skipped, *operands)  40.1 us
    all_to_all x4, waiting for transfers between devices, tick(): lax.all_to_all(when(active, causal, product_local), 'seq', split_axis=0,...  24.7 us
    all_to_all x4, waiting for transfers between devices, tick(): lax.all_to_all(d_conv, 'seq', split_axis=1, concat_axis=0, tiled=True)  21.7 us
    all_to_all x4, starting transfers between devices, tick(): lax.all_to_all(when(active, adjoint, d_conv_local), 'seq', split_axis=0,...  16.3 us
    all_to_all x4, starting transfers between devices, tick(): lax.all_to_all(d_conv, 'seq', split_axis=1, concat_axis=0, tiled=True)  16.1 us
    all_to_all x4, starting transfers between devices, tick(): lax.all_to_all(product, 'seq', split_axis=1, concat_axis=0, tiled=True)  16.1 us
    all_to_all x4, starting transfers between devices, tick(): lax.all_to_all(when(active, causal, product_local), 'seq', split_axis=0,...  14.4 us
  transfers between devices with their start and end apart: 26, of which 20 were waited for; matrix products, arithmetic and copies ran while one was open for 14% of the time, Pallas kernels for 0%

commit v1 on v0

v1 whole, which is shorter than its diff:
```python
import math

import jax
import jax.numpy as jnp
import numpy as np
from jax import lax
from jax.experimental import pallas as pl
from jax.experimental.pallas import tpu as pltpu
from jax.sharding import PartitionSpec as P

f32 = jnp.float32
bf16 = jnp.bfloat16
PAD = 16
CONTRACT = (((1,), (1,)), ((), ()))


def tables(rows):
    period = 2 * rows + 2 * PAD
    half = period // 2
    freq = 2.0 * math.pi * (np.arange(half) + 0.5) / period

    def forward(index):
        angle = np.outer(freq, index)
        return np.concatenate([np.cos(angle), -np.sin(angle)], axis=0)

    series = forward(np.arange(rows + PAD))
    lags = forward(np.arange(period) - (rows + PAD))
    angle = np.outer(np.arange(rows + PAD), freq)
    inverse = np.concatenate([np.cos(angle), -np.sin(angle)], axis=1) * (2.0 / period)
    return tuple(jnp.asarray(t.astype(np.float32), dtype=bf16) for t in (series, lags, inverse))


def dot(a, b):
    return jnp.dot(a, b, preferred_element_type=f32)


def lanes(part, width, core):
    half = width // 2
    return pl.ds(pl.multiple_of(part * width + core * half, 128), half)


def call(body, outs, scratch, name, n_in, smem=1, anys=()):
    specs = []
    for i in range(n_in):
        if i < smem:
            specs.append(pl.BlockSpec(memory_space=pltpu.SMEM))
        elif i in anys:
            specs.append(pl.BlockSpec(memory_space=pl.ANY))
        else:
            specs.append(pl.BlockSpec(memory_space=pltpu.VMEM))
    return pl.pallas_call(
        body,
        out_shape=outs,
        in_specs=specs,
        out_specs=jax.tree.map(lambda _: pl.BlockSpec(memory_space=pltpu.VMEM), outs),
        scratch_shapes=scratch,
        compiler_params=pltpu.CompilerParams(vmem_limit_bytes=56 * 1024 * 1024),
        name=name,
    )


def mix_stored(place, proj_own, proj_core, rim_own, rim_core, taps, query, keys, values, product, padded):
    core = place[1]
    rows = query.shape[0]
    own = rows // 2
    width = 2 * query.shape[1]
    ext = rows + PAD
    for part in range(3):
        at = lanes(part, width, core)
        here = pl.ds(part * (width // 2), width // 2)
        before = jnp.where(core == 0, rim_own[:, at], rim_core[:, at])
        after = jnp.where(core == 0, rim_core[:, at], rim_own[:, at])
        padded[0:PAD] = before.astype(f32)
        padded[pl.ds(pl.multiple_of(PAD + core * own, 16), own)] = proj_own[:, at].astype(f32)
        padded[pl.ds(pl.multiple_of(PAD + (1 - core) * own, 16), own)] = proj_core[:, here].astype(f32)
        padded[PAD + rows : 2 * PAD + rows] = after.astype(f32)
        size = rows if part == 0 else ext
        mixed = (
            taps[0:1, at] * padded[PAD : PAD + size]
            + taps[1:2, at] * padded[PAD - 1 : PAD - 1 + size]
            + taps[2:3, at] * padded[PAD - 2 : PAD - 2 + size]
        )
        (query, keys, values)[part][...] = mixed
    product[...] = (keys[...] * values[...]).astype(bf16)


def lag_spectra(place, count, *refs):
    pieces, (table, out, padded) = refs[:count], refs[count:]
    rows, chans = pieces[0].shape
    chip = place[0]
    ext = rows + PAD
    padded[0:ext] = jnp.zeros((ext, chans), bf16)
    padded[ext + count * rows :] = jnp.zeros((PAD, chans), bf16)
    for m in range(count):
        at = pl.multiple_of(ext + (chip ^ m) * rows, 16)
        padded[pl.ds(at, rows)] = pieces[m][...]
    for d in range(count):
        out[d] = dot(table[...], padded[pl.ds(d * rows, 2 * ext)])
    out[count] = jnp.zeros(out.shape[1:], f32)


def gate_grad(place, g_own, g_core, w_out, query, send, d_out):
    core = place[1]
    rows, chans = query.shape
    own = rows // 2
    weight = w_out[pl.ds(pl.multiple_of(core * chans, 16), chans)]
    for g, side in ((g_own, core), (g_core, 1 - core)):
        at = pl.ds(pl.multiple_of(side * own, 16), own)
        wide = lax.dot_general(g[...], weight, CONTRACT, preferred_element_type=f32)
        d_out[at] = wide
        send[at] = (wide * query[at]).astype(bf16)
    send[rows : rows + PAD] = d_out[0:PAD].astype(bf16)


def spectra_of(series, out, table):
    out[...] = dot(table[...], series)


def convolve(lag_ref, slots, spectra, adjoint, total, half):
    step = 16

    def tile(i, carry):
        upper = pl.ds(pl.multiple_of(i * step, step), step)
        lower = pl.ds(pl.multiple_of(half + i * step, step), step)
        real = imag = None
        for slot, at in zip(slots, spectra):
            lag_re, lag_im = lag_ref[slot, upper], lag_ref[slot, lower]
            ser_re, ser_im = at[upper], at[lower]
            if adjoint:
                re = lag_re * ser_re + lag_im * ser_im
                im = lag_re * ser_im - lag_im * ser_re
            else:
                re = lag_re * ser_re - lag_im * ser_im
                im = lag_re * ser_im + lag_im * ser_re
            real = re if real is None else real + re
            imag = im if imag is None else imag + im
        total[upper] = real.astype(bf16)
        total[lower] = imag.astype(bf16)
        return carry

    lax.fori_loop(0, half // step, tile, 0)


def input_grad(first, count, *refs):
    refs = list(refs)
    place, own, d_out = refs[:3]
    got = refs[3 : 2 + count]
    refs = refs[2 + count :]
    product = refs.pop(0) if first else None
    conv = None if first else refs.pop(0)
    lag_ref, series_table, inverse_table, keys, values, taps, bias, w_in, keep, pass_on = refs[:10]
    refs = refs[10:]
    if first:
        conv = refs.pop(0)
    weight, spec, total, mixed, d_proj, sums, sem = refs
    chip, core = place[0], place[1]
    rows, chans = d_out.shape
    own_rows = rows // 2
    width = 2 * chans
    ext = rows + PAD
    half = ext
    copies = [
        pltpu.make_async_copy(
            w_in.at[:, lanes(part, width, core)], weight.at[:, pl.ds(part * chans, chans)], sem.at[part]
        )
        for part in range(3)
    ]
    for copy in copies:
        copy.start()
    slot_of = lambda distance, valid: jnp.where(valid, distance, count)
    row_ids = lax.broadcasted_iota(jnp.int32, (ext, chans), 0)
    bias_here = bias[0:1, pl.ds(pl.multiple_of(core * chans, 128), chans)]
    for m in range(1, count):
        spec[m] = dot(series_table[:, 0:rows], got[m - 1][0:rows])
    spec[0] = dot(series_table[:, 0:rows], own[0:rows])
    if first:
        spec[count] = dot(series_table[...], product[...])
        slots = [jnp.int32(0)] + [slot_of(chip - (chip ^ m), (chip ^ m) < chip) for m in range(1, count)]
        convolve(lag_ref, slots, [spec.at[count]] + [spec.at[m] for m in range(1, count)], False, total, half)
        whole = dot(inverse_table[...], total[...]) + bias_here * product[...].astype(f32)
        conv[...] = whole.astype(bf16)
    slots = [jnp.int32(0)] + [slot_of((chip ^ m) - chip, (chip ^ m) > chip) for m in range(1, count)]
    convolve(lag_ref, slots, [spec.at[m] for m in range(count)], True, total, half)
    rim_conv = jnp.zeros((PAD, chans), f32)
    rim_out = jnp.zeros((PAD, chans), f32)
    for m in range(1, count):
        pick = ((chip ^ m) == chip + 1).astype(f32)
        rim_conv = rim_conv + pick * got[m - 1][0:PAD].astype(f32)
        rim_out = rim_out + pick * got[m - 1][rows : rows + PAD].astype(f32)
    inside = (chip < count - 1).astype(f32)
    mixed[0:rows] = bias_here * own[0:rows].astype(f32)
    mixed[rows:ext] = bias_here * rim_conv
    d_prod = (dot(inverse_table[...], total[...]) + mixed[...]).astype(bf16).astype(f32)
    d_prod = jnp.where(row_ids < rows, d_prod, d_prod * inside)
    for part in range(3):
        at = lanes(part, width, core)
        if part == 0:
            mixed[0:rows] = (d_out[...] * conv[0:rows].astype(f32)).astype(bf16).astype(f32)
            mixed[rows:ext] = (rim_out * conv[rows:ext].astype(f32)).astype(bf16).astype(f32)
        else:
            mixed[...] = (d_prod * (values if part == 1 else keys)[...]).astype(bf16).astype(f32)
        d_proj[:, pl.ds(part * chans, chans)] = (
            taps[0:1, at] * mixed[0:rows] + taps[1:2, at] * mixed[1 : rows + 1] + taps[2:3, at] * mixed[2 : rows + 2]
        ).astype(bf16)
    for copy in copies:
        copy.wait()
    sums[...] = lax.dot_general(d_proj[...], weight[...], CONTRACT, preferred_element_type=f32)
    keep[...] = sums[pl.ds(pl.multiple_of(core * own_rows, 16), own_rows)]
    pass_on[...] = sums[pl.ds(pl.multiple_of((1 - core) * own_rows, 16), own_rows)].astype(bf16)


def shards(cotangent, projected, w_in, w_out, short_filter, long_filter, filter_bias):
    seq_count = lax.axis_size("seq")
    section_count = lax.axis_size("section")
    seq_place = lax.axis_index("seq")
    section_place = lax.axis_index("section")
    chips = seq_count // 2
    chip, core = seq_place // 2, seq_place % 2
    place = jnp.stack([chip, core]).astype(jnp.int32)
    own_rows = projected.shape[2]
    rows = 2 * own_rows
    width = w_out.shape[2]
    chans = width // 2
    ext = rows + PAD
    half = ext
    series_table, lag_table, inverse_table = tables(rows)
    weight_in, weight_out, taps, bias = w_in[0], w_out[0], short_filter[0], filter_bias

    def swap_core(value):
        return lax.ppermute(value, "seq", [(i, i ^ 1) for i in range(seq_count)])

    def swap_chip(value, m):
        return lax.ppermute(value, "seq", [(i, ((i // 2) ^ m) * 2 + i % 2) for i in range(seq_count)])

    def half_of(value, part, side):
        return lax.dynamic_slice_in_dim(value, part * width + side * chans, chans, 1)

    def to_rows(own, other):
        return jnp.where(core == 0, jnp.concatenate([own, other]), jnp.concatenate([other, own]))

    lags = long_filter[0].astype(bf16)
    lags_core = swap_core(half_of(lags, 0, 1 - core))
    stored = projected[0, 0]
    rim_pairs = [(2 * q + 1, 2 * q + 2) for q in range(chips - 1)]
    rim_pairs += [(b, a) for a, b in rim_pairs]
    rim_own = lax.ppermute(jnp.where(core == 0, stored[:PAD], stored[own_rows - PAD :]), "seq", rim_pairs)
    stored_core = swap_core(jnp.concatenate([half_of(stored, part, 1 - core) for part in range(3)], axis=1))
    lags_here = to_rows(half_of(lags, 0, core), lags_core)
    pieces = [lags_here] + [swap_chip(lags_here, m) for m in range(1, chips)]
    rim_core = swap_core(rim_own)

    wide = lambda n, kind: jax.ShapeDtypeStruct((n, chans), kind)
    query, keys, values, product = call(
        mix_stored,
        [wide(rows, f32), wide(ext, f32), wide(ext, f32), wide(ext, bf16)],
        [pltpu.VMEM((rows + 2 * PAD, chans), f32)],
        "mix_stored",
        6,
    )(place, stored, stored_core, rim_own, rim_core, taps)

    spectra = call(
        lambda place, *refs: lag_spectra(place, chips, *refs),
        jax.ShapeDtypeStruct((chips + 1, 2 * half, chans), f32),
        [pltpu.VMEM((chips * rows + ext + PAD, chans), bf16)],
        "lag_spectra",
        2 + chips,
    )(place, *pieces, lag_table)

    grad = cotangent[0]
    result = jnp.zeros((own_rows, width), bf16)
    conv = None
    for turn in range(section_count):
        grad_core = swap_core(grad)
        block, d_out = call(
            gate_grad, [wide(ext, bf16), wide(rows, f32)], [], "gate_grad", 5
        )(place, grad, grad_core, weight_out, query)
        first = turn == 0
        got = []
        for m in range(1, chips):
            send = jnp.where((chip ^ m) > chip, product, block) if first else block
            got.append(swap_chip(send, m))
        outs = [jax.ShapeDtypeStruct((own_rows, width), f32), jax.ShapeDtypeStruct((own_rows, width), bf16)]
        if first:
            outs.append(wide(ext, bf16))
        n_in = 3 + (chips - 1) + 1 + 8
        answer = call(
            lambda *refs, first=first: input_grad(first, chips, *refs),
            outs,
            [
                pltpu.VMEM((width, 3 * chans), bf16),
                pltpu.VMEM((chips + 1, 2 * half, chans), f32),
                pltpu.VMEM((2 * half, chans), bf16),
                pltpu.VMEM((ext, chans), f32),
                pltpu.VMEM((rows, 3 * chans), bf16),
                pltpu.VMEM((rows, width), f32),
                pltpu.SemaphoreType.DMA((3,)),
            ],
            "input_grad_first" if first else "input_grad",
            n_in,
            anys=(n_in - 1,),
        )(
            place, block, d_out, *got, product if first else conv, spectra, series_table, inverse_table,
            keys, values, taps, bias, weight_in,
        )
        keep, pass_on = answer[:2]
        if first:
            conv = answer[2]
        total = (grad.astype(f32) + keep + swap_core(pass_on).astype(f32)).astype(bf16)
        upper = section_count - 1 - turn
        result = jnp.where(section_place == upper, total, result)
        if turn < section_count - 1:
            grad = lax.ppermute(total, "section", [(upper, upper - 1), (upper - 1, upper)])
    return result[None, None]


def solution(mesh):
    return jax.shard_map(
        shards,
        mesh=mesh,
        in_specs=(
            P(None, "seq", None),
            P("section", None, "seq", None),
            P("section", None, None),
            P("section", None, None),
            P("section", None, None),
            P("section", "seq", None),
            P("section", None),
        ),
        out_specs=P("section", None, "seq", None),
        check_vma=False,
    )
```

time: 437 us -> 170 us (0.39); the launches traced: 430 us -> 170 us
  waiting for transfers between devices: 213 us -> 54.7 us
  Pallas kernels: 0 us -> 50.1 us
  matrix products: 45.3 us -> 0 us
  loops' own time: 42.3 us -> 0 us
  starting transfers between devices: 80.6 us -> 46.1 us
  local copies, waits for them, and re-layouts: 30.3 us -> 9.87 us
  other arithmetic: 16.6 us -> 8.71 us
    ppermute x9 -> x30, waiting for transfers between devices: 153 us -> 54.7 us  [the longest x15 38.9 us: swap_chip(): lax.ppermute(value, 'seq', [(i, (i // 2 ^ m) * 2 + i % 2) for i in range(...]
    all_to_all x17 -> x0, starting transfers between devices: 67.9 us -> none  [the longest x4 16.3 us: tick(): lax.all_to_all(when(active, adjoint, d_conv_local), 'seq', split_axis=0,...]
    all_to_all x17 -> x0, waiting for transfers between devices: 60.7 us -> none  [the longest x4 24.7 us: tick(): lax.all_to_all(when(active, causal, product_local), 'seq', split_axis=0,...]
    pallas_call x0 -> x10, Pallas kernels: none -> 50.1 us  [the longest x4 30.6 us: shards(): call(lambda *refs, first=first: input_grad(first, chips, *refs), outs, [p...]
    dot_general x32 -> x0, matrix products: 45.3 us -> none  [the longest x2 7.51 us: inverse_spectrum(): jnp.einsum('kn,cbk->nbc', cos_outer, real_two, precision=accuracy)]
    another operation x21 -> x0, loops' own time: 42.3 us -> none  [the longest x20 40.1 us: when(): return lax.cond(active, action, skipped, *operands)]
    ppermute x9 -> x30, starting transfers between devices: 12.7 us -> 46.1 us  [the longest x3 20.8 us: shards(): lax.ppermute(total, 'section', [(upper, upper - 1), (upper - 1, upper)])]
    select_n x8 -> x3, other arithmetic: 12.2 us -> 2.07 us  [the longest x1 1.1 us: shards(): send = jnp.where(chip ^ m > chip, product, block) if first else block]
  transfers between devices with their start and end apart: 26 -> 30, of which waited for: 20 -> 16; matrix products, arithmetic and copies ran while one was open for 14% -> 3% of each run, Pallas kernels for 0% -> 6%
where the time goes in v1:
time: 170 us
  waiting for transfers between devices  54.7 us (32%)
  Pallas kernels  50.1 us (29%)
  starting transfers between devices  46.1 us (27%)
  local copies, waits for them, and re-layouts  9.87 us (6%)
  other arithmetic  8.71 us (5%)
    ppermute x15, waiting for transfers between devices, swap_chip(): lax.ppermute(value, 'seq', [(i, (i // 2 ^ m) * 2 + i % 2) for i in range(...  38.9 us
    pallas_call x4, Pallas kernels, shards(): call(lambda *refs, first=first: input_grad(first, chips, *refs), outs, [p...  30.6 us
    ppermute x3, starting transfers between devices, shards(): lax.ppermute(total, 'section', [(upper, upper - 1), (upper - 1, upper)])  20.8 us
    ppermute x15, starting transfers between devices, swap_chip(): lax.ppermute(value, 'seq', [(i, (i // 2 ^ m) * 2 + i % 2) for i in range(...  18.9 us
    pallas_call x4, Pallas kernels, shards(): call(gate_grad, [wide(ext, bf16), wide(rows, f32)], [], 'gate_grad', 5)  11.4 us
    ppermute x11, waiting for transfers between devices, swap_core(): return lax.ppermute(value, 'seq', [(i, i ^ 1) for i in range(seq_count)])  10.6 us
    unnamed x61, local copies, waits for them, and re-layouts  8.82 us
    ppermute x11, starting transfers between devices, swap_core(): return lax.ppermute(value, 'seq', [(i, i ^ 1) for i in range(seq_count)])  5.73 us
  transfers between devices with their start and end apart: 30, of which 16 were waited for; matrix products, arithmetic and copies ran while one was open for 3% of the time, Pallas kernels for 6%

profile of v1, /device:TPU:0, one launch (start us, length us, event | category | flops | bytes accessed | tf_op | source)
XLA Modules:
  0.0 169.7 jit_solution(17299718294312317455)
XLA Ops:
  4.4 4.4 %collective-permute-start = (bf16[128,768]{1,0:T(8,128)(2,1)}, bf16[128,768]{1,0:T(8,128)(2,1)S(1)}, u32[]{:S(2)}, u32[]{:S(2)}) collective-permute-start(bf16[128,768]{1,0:T(8,128)(2,1)} %bitcast.38), channel_id=1, source_target_pairs={{0,4},{4,0},{8,12},{12,8},{16,20},{20,16},{24,28},{28,24},{1,5},{5... | collective-permute-start | bytes 589832 | tf_op jit(solution)/shard_map/ppermute | solution.py:230
  10.8 3.2 %collective-permute-start.10 = (bf16[256,384]{1,0:T(8,128)(2,1)S(1)}, bf16[256,384]{1,0:T(8,128)(2,1)S(1)}, u32[]{:S(2)}, u32[]{:S(2)}) collective-permute-start(bf16[256,384]{1,0:T(8,128)(2,1)S(1)} %maximum_select_fusion.refs_0_), channel_id=1, source_target_pairs={{0,24},{4,28},{8,16},{12,20},{16,8},{20,12},{24,0},{28,4},{1,25},{... | collective-permute-start | bytes 589832 | tf_op jit(solution)/shard_map/ppermute | solution.py:233
  14.8 2.8 %mix_stored.1 = (f32[256,384]{1,0:T(8,128)}, f32[272,384]{1,0:T(8,128)}, f32[272,384]{1,0:T(8,128)}, bf16[272,384]{1,0:T(8,128)(2,1)}) custom-call(s32[2]{0:T(128)} %pad_add_fusion.place.refs_0_, bf16[128,2304]{1,0:T(8,128)(2,1)} %bitcast.32, bf16[128,1152]{1,0:T(8,128)(2,1)} %copy-done.8, bf16[16,2304]{1,0:T(8,128)(2,1)} %copy-done.28, ...), custom_call_target="tpu_custom_call" | custom-call | tf_op jit(solution)/shard_map/mix_stored/pallas_call | solution.py:253
  18.2 2.9 %gate_grad.4 = (bf16[272,384]{1,0:T(8,128)(2,1)}, f32[256,384]{1,0:T(8,128)}) custom-call(s32[2]{0:T(128)} %pad_add_fusion.place.refs_0_, bf16[128,768]{1,0:T(8,128)(2,1)} %bitcast.39, bf16[128,768]{1,0:T(8,128)(2,1)} %copy-done.24, bf16[768,768]{1,0:T(8,128)(2,1)} %bitcast.28, f32[256,384]{1,0:T(8,128)} %get-tuple-element.26.query), custom_call_target="tpu_custom_call" | custom-call | tf_op jit(solution)/shard_map/gate_grad/pallas_call | solution.py:274
  24.0 1.8 %collective-permute-start.6 = (bf16[272,384]{1,0:T(8,128)(2,1)S(1)}, bf16[272,384]{1,0:T(8,128)(2,1)S(1)}, u32[]{:S(2)}, u32[]{:S(2)}) collective-permute-start(bf16[272,384]{1,0:T(8,128)(2,1)S(1)} %get-tuple-element.50), channel_id=1, source_target_pairs={{0,24},{4,28},{8,16},{12,20},{16,8},{20,12},{24,0},{28,4},{1,25},{... | collective-permute-start | bytes 626696 | tf_op jit(solution)/shard_map/ppermute | solution.py:233
  27.5 10.8 %collective-permute-done.8.refs_1_ = bf16[256,384]{1,0:T(8,128)(2,1)S(1)} collective-permute-done((bf16[256,384]{1,0:T(8,128)(2,1)S(1)}, bf16[256,384]{1,0:T(8,128)(2,1)S(1)}, u32[]{:S(2)}, u32[]{:S(2)}) %collective-permute-start.8) | collective-permute-done | bytes 196640 | tf_op jit(solution)/shard_map/ppermute | solution.py:233
  39.7 5.3 %lag_spectra.1.refs_7_ = f32[5,544,384]{2,1,0:T(8,128)} custom-call(s32[2]{0:T(128)} %pad_add_fusion.place.refs_0_, bf16[256,384]{1,0:T(8,128)(2,1)} %copy-done, bf16[256,384]{1,0:T(8,128)(2,1)} %copy-done.22, bf16[256,384]{1,0:T(8,128)(2,1)} %copy-done.23, bf16[256,384]{1,0:T(8,128)(2,1)} %copy-done.21, bf16[544,544]{1,0:T(8,128)(2,1)} %constant.63.clone.refs_4_), custom_call_target="tpu_custom_call" | custom-call | tf_op jit(solution)/shard_map/lag_spectra/pallas_call | solution.py:261
  45.9 8.6 %input_grad_first.1 = (f32[128,768]{1,0:T(8,128)}, bf16[128,768]{1,0:T(8,128)(2,1)}, bf16[272,384]{1,0:T(8,128)(2,1)}) custom-call(s32[2]{0:T(128)} %pad_add_fusion.place.refs_0_, bf16[272,384]{1,0:T(8,128)(2,1)} %get-tuple-element.27.refs_1_, f32[256,384]{1,0:T(8,128)} %get-tuple-element.28.refs_2_, bf16[272,384]{1,0:T(8,128)(2,1)} %copy-done.9, ...), custom_call_target="tpu_custom_call" | custom-call | tf_op jit(solution)/shard_map/input_grad_first/pallas_call | solution.py:286
  60.2 2.9 %gate_grad.5 = (bf16[272,384]{1,0:T(8,128)(2,1)}, f32[256,384]{1,0:T(8,128)}) custom-call(s32[2]{0:T(128)} %pad_add_fusion.place.refs_0_, bf16[128,768]{1,0:T(8,128)(2,1)} %copy-done.4, bf16[128,768]{1,0:T(8,128)(2,1)} %copy-done.26, bf16[768,768]{1,0:T(8,128)(2,1)} %bitcast.29, f32[256,384]{1,0:T(8,128)} %get-tuple-element.26.query), custom_call_target="tpu_custom_call" | custom-call | tf_op jit(solution)/shard_map/gate_grad/pallas_call | solution.py:274
  66.5 4.7 %collective-permute-done.14.refs_3_ = bf16[272,384]{1,0:T(8,128)(2,1)S(1)} collective-permute-done((bf16[272,384]{1,0:T(8,128)(2,1)}, bf16[272,384]{1,0:T(8,128)(2,1)S(1)}, u32[]{:S(2)}, u32[]{:S(2)}) %collective-permute-start.14) | collective-permute-done | bytes 208928 | tf_op jit(solution)/shard_map/ppermute | solution.py:233
  71.3 4.4 %collective-permute-done.15.refs_4_ = bf16[272,384]{1,0:T(8,128)(2,1)S(1)} collective-permute-done((bf16[272,384]{1,0:T(8,128)(2,1)}, bf16[272,384]{1,0:T(8,128)(2,1)S(1)}, u32[]{:S(2)}, u32[]{:S(2)}) %collective-permute-start.15) | collective-permute-done | bytes 208928 | tf_op jit(solution)/shard_map/ppermute | solution.py:233
  76.5 7.3 %input_grad.3 = (f32[128,768]{1,0:T(8,128)}, bf16[128,768]{1,0:T(8,128)(2,1)}) custom-call(s32[2]{0:T(128)} %pad_add_fusion.place.refs_0_, bf16[272,384]{1,0:T(8,128)(2,1)} %get-tuple-element.34.refs_1_, f32[256,384]{1,0:T(8,128)} %get-tuple-element.35.refs_2_, bf16[272,384]{1,0:T(8,128)(2,1)} %copy-done.15, bf16[272,384]{1,0:T(8,128)(2,1)} %copy-done.17, ...), custom_call_target="tpu_custom_call" | custom-call | tf_op jit(solution)/shard_map/input_grad/pallas_call | solution.py:286
  83.9 1.6 collective-permute-done.17
  89.6 2.9 %gate_grad.6 = (bf16[272,384]{1,0:T(8,128)(2,1)}, f32[256,384]{1,0:T(8,128)}) custom-call(s32[2]{0:T(128)} %pad_add_fusion.place.refs_0_, bf16[128,768]{1,0:T(8,128)(2,1)} %copy-done.6, bf16[128,768]{1,0:T(8,128)(2,1)} %copy-done.27, bf16[768,768]{1,0:T(8,128)(2,1)} %bitcast.30, f32[256,384]{1,0:T(8,128)} %get-tuple-element.26.query), custom_call_target="tpu_custom_call" | custom-call | tf_op jit(solution)/shard_map/gate_grad/pallas_call | solution.py:274
  96.0 4.7 %collective-permute-done.20.refs_3_ = bf16[272,384]{1,0:T(8,128)(2,1)S(1)} collective-permute-done((bf16[272,384]{1,0:T(8,128)(2,1)}, bf16[272,384]{1,0:T(8,128)(2,1)S(1)}, u32[]{:S(2)}, u32[]{:S(2)}) %collective-permute-start.20) | collective-permute-done | bytes 208928 | tf_op jit(solution)/shard_map/ppermute | solution.py:233
  100.7 4.4 %collective-permute-done.21.refs_4_ = bf16[272,384]{1,0:T(8,128)(2,1)S(1)} collective-permute-done((bf16[272,384]{1,0:T(8,128)(2,1)}, bf16[272,384]{1,0:T(8,128)(2,1)S(1)}, u32[]{:S(2)}, u32[]{:S(2)}) %collective-permute-start.21) | collective-permute-done | bytes 208928 | tf_op jit(solution)/shard_map/ppermute | solution.py:233
  105.9 7.3 %input_grad.4 = (f32[128,768]{1,0:T(8,128)}, bf16[128,768]{1,0:T(8,128)(2,1)}) custom-call(s32[2]{0:T(128)} %pad_add_fusion.place.refs_0_, bf16[272,384]{1,0:T(8,128)(2,1)} %get-tuple-element.39.refs_1_, f32[256,384]{1,0:T(8,128)} %get-tuple-element.40.refs_2_, bf16[272,384]{1,0:T(8,128)(2,1)} %copy-done.16, bf16[272,384]{1,0:T(8,128)(2,1)} %copy-done.18, ...), custom_call_target="tpu_custom_call" | custom-call | tf_op jit(solution)/shard_map/input_grad/pallas_call | solution.py:286
  116.0 19.3 %collective-permute-start.24 = (bf16[128,768]{1,0:T(8,128)(2,1)S(1)}, bf16[128,768]{1,0:T(8,128)(2,1)S(1)}, u32[]{:S(2)}, u32[]{:S(2)}) collective-permute-start(bf16[128,768]{1,0:T(8,128)(2,1)S(1)} %add_convert_fusion.1), channel_id=1, source_target_pairs={{1,0},{0,1},{5,4},{4,5},{9,8},{8,9},{13,12},{12,13},{17,16},{16,17... | collective-permute-start | bytes 589832 | tf_op jit(solution)/shard_map/ppermute | solution.py:312
  135.3 5.2 %collective-permute-done.24.g_own = bf16[128,768]{1,0:T(8,128)(2,1)S(1)} collective-permute-done((bf16[128,768]{1,0:T(8,128)(2,1)S(1)}, bf16[128,768]{1,0:T(8,128)(2,1)S(1)}, u32[]{:S(2)}, u32[]{:S(2)}) %collective-permute-start.24) | collective-permute-done | bytes 196640 | tf_op jit(solution)/shard_map/ppermute | solution.py:312
  142.6 2.9 %gate_grad.7 = (bf16[272,384]{1,0:T(8,128)(2,1)}, f32[256,384]{1,0:T(8,128)}) custom-call(s32[2]{0:T(128)} %pad_add_fusion.place.refs_0_, bf16[128,768]{1,0:T(8,128)(2,1)} %copy-done.1, bf16[128,768]{1,0:T(8,128)(2,1)} %copy-done.25, bf16[768,768]{1,0:T(8,128)(2,1)} %bitcast.31, f32[256,384]{1,0:T(8,128)} %get-tuple-element.26.query), custom_call_target="tpu_custom_call" | custom-call | tf_op jit(solution)/shard_map/gate_grad/pallas_call | solution.py:274
  148.9 4.7 %collective-permute-done.26.refs_3_ = bf16[272,384]{1,0:T(8,128)(2,1)S(1)} collective-permute-done((bf16[272,384]{1,0:T(8,128)(2,1)}, bf16[272,384]{1,0:T(8,128)(2,1)S(1)}, u32[]{:S(2)}, u32[]{:S(2)}) %collective-permute-start.26) | collective-permute-done | bytes 208928 | tf_op jit(solution)/shard_map/ppermute | solution.py:233
  153.7 4.4 %collective-permute-done.27.refs_4_ = bf16[272,384]{1,0:T(8,128)(2,1)S(1)} collective-permute-done((bf16[272,384]{1,0:T(8,128)(2,1)}, bf16[272,384]{1,0:T(8,128)(2,1)S(1)}, u32[]{:S(2)}, u32[]{:S(2)}) %collective-permute-start.27) | collective-permute-done | bytes 208928 | tf_op jit(solution)/shard_map/ppermute | solution.py:233
  158.8 7.3 %input_grad.5 = (f32[128,768]{1,0:T(8,128)}, bf16[128,768]{1,0:T(8,128)(2,1)}) custom-call(s32[2]{0:T(128)} %pad_add_fusion.place.refs_0_, bf16[272,384]{1,0:T(8,128)(2,1)} %get-tuple-element.43.refs_1_, f32[256,384]{1,0:T(8,128)} %get-tuple-element.44.refs_2_, bf16[272,384]{1,0:T(8,128)(2,1)} %copy-done.12, bf16[272,384]{1,0:T(8,128)(2,1)} %copy-done.13, ...), custom_call_target="tpu_custom_call" | custom-call | tf_op jit(solution)/shard_map/input_grad/pallas_call | solution.py:286
  167.9 1.8 %fusion.1 = bf16[1,1,128,768]{3,2,1,0:T(8,128)(2,1)} fusion(bf16[128,768]{1,0:T(8,128)(2,1)S(1)} %collective-permute-done.29, f32[128,768]{1,0:T(8,128)} %get-tuple-element.45, bf16[128,768]{1,0:T(8,128)(2,1)S(1)} %copy-done.2, bf16[128,768]{1,0:T(8,128)(2,1)S(1)} %add_convert_fusion.1, bf16[128,768]{1,0:T(8,128)(2,1)S(1)} %add_convert_fusion.2, ...), kind=kLoop, calls=%fused_computation.9 | loop fusion | flops 884736 | bytes 1572868 | tf_op jit(solution)/shard_map/broadcast_in_dim | solution.py:313
  (119 shorter events, 43.8 us)
Async XLA Ops:
  1.1 9.7 %collective-permute-start.7 = (bf16[128,384]{1,0:T(8,128)(2,1)S(1)}, bf16[128,384]{1,0:T(8,128)(2,1)S(1)}, u32[]{:S(2)}, u32[]{:S(2)}) collective-permute-start(bf16[128,384]{1,0:T(8,128)(2,1)S(1)} %get-tuple-element.54), channel_id=1, source_target_pairs={{0,4},{4,0},{8,12},{12,8},{16,20},{20,16},{24,28},{28,24},{1,5},{5... | collective-permute-start | bytes 294920 | tf_op jit(solution)/shard_map/ppermute | solution.py:230
  2.6 11.4 %collective-permute-start.1 = (bf16[128,1152]{1,0:T(8,128)(2,1)S(1)}, bf16[128,1152]{1,0:T(8,128)(2,1)S(1)}, u32[]{:S(2)}, u32[]{:S(2)}) collective-permute-start(bf16[128,1152]{1,0:T(8,128)(2,1)S(1)} %pad_maximum_fusion), channel_id=1, source_target_pairs={{0,4},{4,0},{8,12},{12,8},{16,20},{20,16},{24,28},{28,24},{1,5},{5... | collective-permute-start | bytes 884744 | tf_op jit(solution)/shard_map/ppermute | solution.py:230
  3.7 7.0 %collective-permute-start.2 = (bf16[16,2304]{1,0:T(8,128)(2,1)S(1)}, bf16[16,2304]{1,0:T(8,128)(2,1)S(1)}, u32[]{:S(2)}, u32[]{:S(2)}) collective-permute-start(bf16[16,2304]{1,0:T(8,128)(2,1)S(1)} %select_bitcast_fusion), channel_id=1, source_target_pairs={{4,8},{12,16},{20,24},{8,4},{16,12},{24,20},{5,9},{13,17},{21,25},... | collective-permute-start | bytes 221192 | tf_op jit(solution)/shard_map/ppermute | solution.py:246
  4.4 13.2 %collective-permute-start = (bf16[128,768]{1,0:T(8,128)(2,1)}, bf16[128,768]{1,0:T(8,128)(2,1)S(1)}, u32[]{:S(2)}, u32[]{:S(2)}) collective-permute-start(bf16[128,768]{1,0:T(8,128)(2,1)} %bitcast.38), channel_id=1, source_target_pairs={{0,4},{4,0},{8,12},{12,8},{16,20},{20,16},{24,28},{28,24},{1,5},{5... | collective-permute-start | bytes 589832 | tf_op jit(solution)/shard_map/ppermute | solution.py:230
  10.7 3.3 %collective-permute-start.3 = (bf16[16,2304]{1,0:T(8,128)(2,1)S(1)}, bf16[16,2304]{1,0:T(8,128)(2,1)S(1)}, u32[]{:S(2)}, u32[]{:S(2)}) collective-permute-start(bf16[16,2304]{1,0:T(8,128)(2,1)S(1)} %collective-permute-done.2.rim_own), channel_id=1, source_target_pairs={{0,4},{4,0},{8,12},{12,8},{16,20},{20,16},{24,28},{28,24},{1,5},{5... | collective-permute-start | bytes 221192 | tf_op jit(solution)/shard_map/ppermute | solution.py:230
  10.8 15.8 %collective-permute-start.10 = (bf16[256,384]{1,0:T(8,128)(2,1)S(1)}, bf16[256,384]{1,0:T(8,128)(2,1)S(1)}, u32[]{:S(2)}, u32[]{:S(2)}) collective-permute-start(bf16[256,384]{1,0:T(8,128)(2,1)S(1)} %maximum_select_fusion.refs_0_), channel_id=1, source_target_pairs={{0,24},{4,28},{8,16},{12,20},{16,8},{20,12},{24,0},{28,4},{1,25},{... | collective-permute-start | bytes 589832 | tf_op jit(solution)/shard_map/ppermute | solution.py:233
  22.2 22.8 %collective-permute-start.4 = (bf16[272,384]{1,0:T(8,128)(2,1)S(1)}, bf16[272,384]{1,0:T(8,128)(2,1)S(1)}, u32[]{:S(2)}, u32[]{:S(2)}) collective-permute-start(bf16[272,384]{1,0:T(8,128)(2,1)S(1)} %get-tuple-element.52), channel_id=1, source_target_pairs={{0,8},{4,12},{8,0},{12,4},{16,24},{20,28},{24,16},{28,20},{1,9},{5... | collective-permute-start | bytes 626696 | tf_op jit(solution)/shard_map/ppermute | solution.py:233
  23.1 21.9 %collective-permute-start.5 = (bf16[272,384]{1,0:T(8,128)(2,1)S(1)}, bf16[272,384]{1,0:T(8,128)(2,1)S(1)}, u32[]{:S(2)}, u32[]{:S(2)}) collective-permute-start(bf16[272,384]{1,0:T(8,128)(2,1)S(1)} %get-tuple-element.51), channel_id=1, source_target_pairs={{0,16},{4,20},{8,24},{12,28},{16,0},{20,4},{24,8},{28,12},{1,17},{... | collective-permute-start | bytes 626696 | tf_op jit(solution)/shard_map/ppermute | solution.py:233
  24.0 21.0 %collective-permute-start.6 = (bf16[272,384]{1,0:T(8,128)(2,1)S(1)}, bf16[272,384]{1,0:T(8,128)(2,1)S(1)}, u32[]{:S(2)}, u32[]{:S(2)}) collective-permute-start(bf16[272,384]{1,0:T(8,128)(2,1)S(1)} %get-tuple-element.50), channel_id=1, source_target_pairs={{0,24},{4,28},{8,16},{12,20},{16,8},{20,12},{24,0},{28,4},{1,25},{... | collective-permute-start | bytes 626696 | tf_op jit(solution)/shard_map/ppermute | solution.py:233
  25.8 12.5 %collective-permute-start.8 = (bf16[256,384]{1,0:T(8,128)(2,1)S(1)}, bf16[256,384]{1,0:T(8,128)(2,1)S(1)}, u32[]{:S(2)}, u32[]{:S(2)}) collective-permute-start(bf16[256,384]{1,0:T(8,128)(2,1)S(1)} %maximum_select_fusion.refs_0_), channel_id=1, source_target_pairs={{0,8},{4,12},{8,0},{12,4},{16,24},{20,28},{24,16},{28,20},{1,9},{5... | collective-permute-start | bytes 589832 | tf_op jit(solution)/shard_map/ppermute | solution.py:233
  26.6 12.3 %collective-permute-start.9 = (bf16[256,384]{1,0:T(8,128)(2,1)S(1)}, bf16[256,384]{1,0:T(8,128)(2,1)S(1)}, u32[]{:S(2)}, u32[]{:S(2)}) collective-permute-start(bf16[256,384]{1,0:T(8,128)(2,1)S(1)} %maximum_select_fusion.refs_0_), channel_id=1, source_target_pairs={{0,16},{4,20},{8,24},{12,28},{16,0},{20,4},{24,8},{28,12},{1,17},{... | collective-permute-start | bytes 589832 | tf_op jit(solution)/shard_map/ppermute | solution.py:233
  54.5 1.7 %collective-permute-start.11 = (bf16[128,768]{1,0:T(8,128)(2,1)}, bf16[128,768]{1,0:T(8,128)(2,1)S(1)}, u32[]{:S(2)}, u32[]{:S(2)}) collective-permute-start(bf16[128,768]{1,0:T(8,128)(2,1)} %get-tuple-element.33), channel_id=1, source_target_pairs={{0,4},{4,0},{8,12},{12,8},{16,20},{20,16},{24,28},{28,24},{1,5},{5... | collective-permute-start | bytes 589832 | tf_op jit(solution)/shard_map/ppermute | solution.py:230
  63.0 8.2 %collective-permute-start.14 = (bf16[272,384]{1,0:T(8,128)(2,1)}, bf16[272,384]{1,0:T(8,128)(2,1)S(1)}, u32[]{:S(2)}, u32[]{:S(2)}) collective-permute-start(bf16[272,384]{1,0:T(8,128)(2,1)} %get-tuple-element.34.refs_1_), channel_id=1, source_target_pairs={{0,8},{4,12},{8,0},{12,4},{16,24},{20,28},{24,16},{28,20},{1,9},{5... | collective-permute-start | bytes 626696 | tf_op jit(solution)/shard_map/ppermute | solution.py:233
  64.1 11.6 %collective-permute-start.15 = (bf16[272,384]{1,0:T(8,128)(2,1)}, bf16[272,384]{1,0:T(8,128)(2,1)S(1)}, u32[]{:S(2)}, u32[]{:S(2)}) collective-permute-start(bf16[272,384]{1,0:T(8,128)(2,1)} %get-tuple-element.34.refs_1_), channel_id=1, source_target_pairs={{0,16},{4,20},{8,24},{12,28},{16,0},{20,4},{24,8},{28,12},{1,17},{... | collective-permute-start | bytes 626696 | tf_op jit(solution)/shard_map/ppermute | solution.py:233
  65.0 10.7 %collective-permute-start.16 = (bf16[272,384]{1,0:T(8,128)(2,1)}, bf16[272,384]{1,0:T(8,128)(2,1)S(1)}, u32[]{:S(2)}, u32[]{:S(2)}) collective-permute-start(bf16[272,384]{1,0:T(8,128)(2,1)} %get-tuple-element.34.refs_1_), channel_id=1, source_target_pairs={{0,24},{4,28},{8,16},{12,20},{16,8},{20,12},{24,0},{28,4},{1,25},{... | collective-permute-start | bytes 626696 | tf_op jit(solution)/shard_map/ppermute | solution.py:233
  83.8 1.7 %collective-permute-start.17 = (bf16[128,768]{1,0:T(8,128)(2,1)}, bf16[128,768]{1,0:T(8,128)(2,1)S(1)}, u32[]{:S(2)}, u32[]{:S(2)}) collective-permute-start(bf16[128,768]{1,0:T(8,128)(2,1)} %get-tuple-element.38), channel_id=1, source_target_pairs={{0,4},{4,0},{8,12},{12,8},{16,20},{20,16},{24,28},{28,24},{1,5},{5... | collective-permute-start | bytes 589832 | tf_op jit(solution)/shard_map/ppermute | solution.py:230
  92.5 8.2 %collective-permute-start.20 = (bf16[272,384]{1,0:T(8,128)(2,1)}, bf16[272,384]{1,0:T(8,128)(2,1)S(1)}, u32[]{:S(2)}, u32[]{:S(2)}) collective-permute-start(bf16[272,384]{1,0:T(8,128)(2,1)} %get-tuple-element.39.refs_1_), channel_id=1, source_target_pairs={{0,8},{4,12},{8,0},{12,4},{16,24},{20,28},{24,16},{28,20},{1,9},{5... | collective-permute-start | bytes 626696 | tf_op jit(solution)/shard_map/ppermute | solution.py:233
  93.5 11.6 %collective-permute-start.21 = (bf16[272,384]{1,0:T(8,128)(2,1)}, bf16[272,384]{1,0:T(8,128)(2,1)S(1)}, u32[]{:S(2)}, u32[]{:S(2)}) collective-permute-start(bf16[272,384]{1,0:T(8,128)(2,1)} %get-tuple-element.39.refs_1_), channel_id=1, source_target_pairs={{0,16},{4,20},{8,24},{12,28},{16,0},{20,4},{24,8},{28,12},{1,17},{... | collective-permute-start | bytes 626696 | tf_op jit(solution)/shard_map/ppermute | solution.py:233
  94.4 10.7 %collective-permute-start.22 = (bf16[272,384]{1,0:T(8,128)(2,1)}, bf16[272,384]{1,0:T(8,128)(2,1)S(1)}, u32[]{:S(2)}, u32[]{:S(2)}) collective-permute-start(bf16[272,384]{1,0:T(8,128)(2,1)} %get-tuple-element.39.refs_1_), channel_id=1, source_target_pairs={{0,24},{4,28},{8,16},{12,20},{16,8},{20,12},{24,0},{28,4},{1,25},{... | collective-permute-start | bytes 626696 | tf_op jit(solution)/shard_map/ppermute | solution.py:233
  113.2 1.7 %collective-permute-start.23 = (bf16[128,768]{1,0:T(8,128)(2,1)}, bf16[128,768]{1,0:T(8,128)(2,1)S(1)}, u32[]{:S(2)}, u32[]{:S(2)}) collective-permute-start(bf16[128,768]{1,0:T(8,128)(2,1)} %get-tuple-element.42), channel_id=1, source_target_pairs={{0,4},{4,0},{8,12},{12,8},{16,20},{20,16},{24,28},{28,24},{1,5},{5... | collective-permute-start | bytes 589832 | tf_op jit(solution)/shard_map/ppermute | solution.py:230
  116.0 24.5 %collective-permute-start.24 = (bf16[128,768]{1,0:T(8,128)(2,1)S(1)}, bf16[128,768]{1,0:T(8,128)(2,1)S(1)}, u32[]{:S(2)}, u32[]{:S(2)}) collective-permute-start(bf16[128,768]{1,0:T(8,128)(2,1)S(1)} %add_convert_fusion.1), channel_id=1, source_target_pairs={{1,0},{0,1},{5,4},{4,5},{9,8},{8,9},{13,12},{12,13},{17,16},{16,17... | collective-permute-start | bytes 589832 | tf_op jit(solution)/shard_map/ppermute | solution.py:312
  145.4 8.2 %collective-permute-start.26 = (bf16[272,384]{1,0:T(8,128)(2,1)}, bf16[272,384]{1,0:T(8,128)(2,1)S(1)}, u32[]{:S(2)}, u32[]{:S(2)}) collective-permute-start(bf16[272,384]{1,0:T(8,128)(2,1)} %get-tuple-element.43.refs_1_), channel_id=1, source_target_pairs={{0,8},{4,12},{8,0},{12,4},{16,24},{20,28},{24,16},{28,20},{1,9},{5... | collective-permute-start | bytes 626696 | tf_op jit(solution)/shard_map/ppermute | solution.py:233
  146.5 11.6 %collective-permute-start.27 = (bf16[272,384]{1,0:T(8,128)(2,1)}, bf16[272,384]{1,0:T(8,128)(2,1)S(1)}, u32[]{:S(2)}, u32[]{:S(2)}) collective-permute-start(bf16[272,384]{1,0:T(8,128)(2,1)} %get-tuple-element.43.refs_1_), channel_id=1, source_target_pairs={{0,16},{4,20},{8,24},{12,28},{16,0},{20,4},{24,8},{28,12},{1,17},{... | collective-permute-start | bytes 626696 | tf_op jit(solution)/shard_map/ppermute | solution.py:233
  147.4 10.7 %collective-permute-start.28 = (bf16[272,384]{1,0:T(8,128)(2,1)}, bf16[272,384]{1,0:T(8,128)(2,1)S(1)}, u32[]{:S(2)}, u32[]{:S(2)}) collective-permute-start(bf16[272,384]{1,0:T(8,128)(2,1)} %get-tuple-element.43.refs_1_), channel_id=1, source_target_pairs={{0,24},{4,28},{8,16},{12,20},{16,8},{20,12},{24,0},{28,4},{1,25},{... | collective-permute-start | bytes 626696 | tf_op jit(solution)/shard_map/ppermute | solution.py:233
  (36 other events, 118.9 us)

commit v2 on v1

v2 whole, which is shorter than its diff:
```python
import math

import jax
import jax.numpy as jnp
import numpy as np
from jax import lax
from jax.experimental import pallas as pl
from jax.experimental.pallas import tpu as pltpu
from jax.sharding import PartitionSpec as P

f32 = jnp.float32
bf16 = jnp.bfloat16
PAD = 16
CONTRACT = (((1,), (1,)), ((), ()))


def tables(rows):
    period = 2 * rows + 2 * PAD
    half = period // 2
    freq = 2.0 * math.pi * (np.arange(half) + 0.5) / period

    def forward(index):
        angle = np.outer(freq, index)
        return np.concatenate([np.cos(angle), -np.sin(angle)], axis=0)

    series = forward(np.arange(rows + PAD))
    lags = forward(np.arange(period) - (rows + PAD))
    angle = np.outer(np.arange(rows + PAD), freq)
    inverse = np.concatenate([np.cos(angle), -np.sin(angle)], axis=1) * (2.0 / period)
    return tuple(jnp.asarray(t.astype(np.float32), dtype=bf16) for t in (series, lags, inverse))


def dot(a, b):
    return jnp.dot(a, b, preferred_element_type=f32)


def dot_last(a, b):
    return lax.dot_general(a, b, CONTRACT, preferred_element_type=f32)


def lanes(part, width, core):
    half = width // 2
    return pl.ds(pl.multiple_of(part * width + core * half, 128), half)


def side_rows(side, own):
    return pl.ds(pl.multiple_of(side * own, 16), own)


def call(body, outs, scratch, name, limit, micros, place, *operands):
    vmem = pl.BlockSpec(memory_space=pltpu.VMEM)
    return pl.pallas_call(
        body,
        out_shape=outs,
        in_specs=[pl.BlockSpec(memory_space=pltpu.SMEM)] + [vmem] * len(operands),
        out_specs=jax.tree.map(lambda _: vmem, outs),
        scratch_shapes=scratch,
        compiler_params=pltpu.CompilerParams(vmem_limit_bytes=limit),
        cost_estimate=pl.CostEstimate(flops=int(micros * 1e9), bytes_accessed=0, transcendentals=0),
        name=name,
    )(place, *operands)


def split_lags(place, lags, own, other):
    core = place[1]
    own[...] = lags[:, lanes(0, lags.shape[1], core)].astype(bf16)
    other[...] = lags[:, lanes(0, lags.shape[1], 1 - core)].astype(bf16)


def split_stored(place, stored, grad, _, other, rim):
    core = place[1]
    rows, chans = other.shape[0], other.shape[1] // 3
    width = 2 * chans
    for part in range(3):
        other[:, part * chans : (part + 1) * chans] = stored[:, lanes(part, width, 1 - core)]
    edge = pl.ds(pl.multiple_of(core * (rows - PAD), 16), PAD)
    rim[:, : 3 * width] = stored[edge]
    rim[:, 3 * width :] = grad[edge]


def mix_stored(place, stored, stored_core, rim_own, rim_core, grad, taps, _, __, query, keys, values, product, grad_ext, padded):
    core = place[1]
    own, width = grad.shape
    rows = 2 * own
    ext = rows + PAD
    for part in range(3):
        at = lanes(part, width, core)
        here = pl.ds(part * (width // 2), width // 2)
        before = jnp.where(core == 0, rim_own[:, at], rim_core[:, at])
        before = jnp.where(place[0] == 0, jnp.zeros_like(before), before)
        after = jnp.where(core == 0, rim_core[:, at], rim_own[:, at])
        padded[0:PAD] = before.astype(f32)
        padded[pl.ds(pl.multiple_of(PAD + core * own, 16), own)] = stored[:, at].astype(f32)
        padded[pl.ds(pl.multiple_of(PAD + (1 - core) * own, 16), own)] = stored_core[:, here].astype(f32)
        padded[PAD + rows : 2 * PAD + rows] = after.astype(f32)
        mixed = (
            taps[0, :, at] * padded[PAD : PAD + ext]
            + taps[1, :, at] * padded[PAD - 1 : PAD - 1 + ext]
            + taps[2, :, at] * padded[PAD - 2 : PAD - 2 + ext]
        )
        (query, keys, values)[part][...] = mixed
    product[...] = (keys[...] * values[...]).astype(bf16)
    grad_ext[0:own] = grad[...]
    grad_ext[own:] = jnp.where(core == 0, rim_core[:, 3 * width :], rim_own[:, 3 * width :])


def lag_spectra(place, count, *refs):
    pieces, (table, out, padded) = refs[:count], refs[count:]
    rows, chans = pieces[0].shape
    chip = place[0]
    ext = rows + PAD
    padded[0:ext] = jnp.zeros((ext, chans), bf16)
    padded[ext + count * rows :] = jnp.zeros((PAD, chans), bf16)
    for m in range(count):
        at = pl.multiple_of(ext + (chip ^ m) * rows, 16)
        padded[pl.ds(at, rows)] = pieces[m][...]
    for d in range(count):
        out[d] = dot(table[...], padded[pl.ds(d * rows, 2 * ext)])
    out[count] = jnp.zeros(out.shape[1:], f32)


def gate_grad(place, g_own, g_core, w_out, query, block, upper, lower, rim, d_out):
    core = place[1]
    rows, chans = block.shape
    own = rows // 2
    weight = w_out[pl.ds(pl.multiple_of(core * chans, 16), chans)]
    wide = dot_last(g_own[...], weight)
    d_out[side_rows(core, own)] = wide[:own]
    d_out[rows:] = wide[own:]
    d_out[side_rows(1 - core, own)] = dot_last(g_core[0:own], weight)
    upper[...] = (d_out[0:own] * query[0:own]).astype(bf16)
    lower[...] = (d_out[own:rows] * query[own:rows]).astype(bf16)
    block[0:own] = upper[...]
    block[own:rows] = lower[...]
    rim[...] = (d_out[rows:] * query[rows:]).astype(bf16)


def slot_of(place, m, count, adjoint):
    chip, other = place[0], place[0] ^ m
    distance = other - chip if adjoint else chip - other
    return jnp.where(distance >= 0, distance, count)


def accumulate(lag_ref, pairs, adjoint, start, total):
    step = 16
    half = total.shape[0] // 2

    def tile(i, carry):
        upper = pl.ds(pl.multiple_of(i * step, step), step)
        lower = pl.ds(pl.multiple_of(half + i * step, step), step)
        real, imag = (None, None) if start is None else (start[upper], start[lower])
        for slot, at in pairs:
            lag_re, lag_im = lag_ref[slot, upper], lag_ref[slot, lower]
            ser_re, ser_im = at[upper], at[lower]
            if adjoint:
                re = lag_re * ser_re + lag_im * ser_im
                im = lag_re * ser_im - lag_im * ser_re
            else:
                re = lag_re * ser_re - lag_im * ser_im
                im = lag_re * ser_im + lag_im * ser_re
            real = re if real is None else real + re
            imag = im if imag is None else imag + im
        total[upper] = real.astype(total.dtype)
        total[lower] = imag.astype(total.dtype)
        return carry

    lax.fori_loop(0, half // step, tile, 0)


def short_adjoint(taps, at, mixed, ext):
    mixed[ext:] = jnp.zeros((PAD, mixed.shape[1]), f32)
    return (
        taps[0, :, at] * mixed[0:ext] + taps[1, :, at] * mixed[1 : ext + 1] + taps[2, :, at] * mixed[2 : ext + 2]
    ).astype(bf16)


def inside_rows(place, count, rows, ext, chans):
    ids = lax.broadcasted_iota(jnp.int32, (ext, chans), 0)
    return jnp.where((ids < rows) | (place[0] < count - 1), 1.0, 0.0)


def query_part(place, count, d_out, conv, taps, w_in, mixed, share):
    ext, chans = d_out.shape
    rows, width = ext - PAD, 2 * chans
    inside = inside_rows(place, count, rows, ext, chans)
    at = lanes(0, width, place[1])
    mixed[0:ext] = (d_out[...] * conv[...].astype(f32) * inside).astype(bf16).astype(f32)
    share[...] = dot_last(short_adjoint(taps, at, mixed, ext), w_in[:, at])


def gated_part(place, count, total, inverse, block, rim, keys, values, bias, taps, w_in, share, mixed, keep, pass_on):
    core = place[1]
    rows, chans = block.shape
    own, ext, width = rows // 2, rows + PAD, 2 * chans
    inside = inside_rows(place, count, rows, ext, chans)
    bias_here = bias[0:1, lanes(0, width, core)]
    mixed[0:rows] = bias_here * block[...].astype(f32)
    mixed[rows:ext] = bias_here * rim[...].astype(f32)
    d_prod = (dot(inverse[...], total[...]) + mixed[0:ext]).astype(bf16).astype(f32) * inside
    sums = share[...]
    for part, other in ((1, values), (2, keys)):
        at = lanes(part, width, core)
        mixed[0:ext] = (d_prod * other[...]).astype(bf16).astype(f32)
        sums = sums + dot_last(short_adjoint(taps, at, mixed, ext), w_in[:, at])
    share[...] = sums
    keep[0:own] = share[side_rows(core, own)]
    keep[own:] = share[rows:]
    pass_on[0:own] = share[side_rows(1 - core, own)].astype(bf16)
    pass_on[own:] = share[rows:].astype(bf16)


def early(place, count, block, d_out, conv, lag_ref, table, taps, w_in, total, share, spec, mixed):
    rows = block.shape[0]
    spec[...] = dot(table[:, 0:rows], block[...])
    accumulate(lag_ref, [(slot_of(place, 0, count, True), spec)], True, None, total)
    query_part(place, count, d_out, conv, taps, w_in, mixed, share)


def middle(place, count, ms, *refs):
    got, (start, lag_ref, table, total, spec) = refs[: len(ms)], refs[len(ms) :]
    pairs = []
    for i, m in enumerate(ms):
        spec[i] = dot(table[:, 0 : got[i].shape[0]], got[i][...])
        pairs.append((slot_of(place, m, count, True), spec.at[i]))
    accumulate(lag_ref, pairs, True, start, total)


def late_pairs(place, count, got, spec, table):
    rows = got[0].shape[0] if len(got) > 2 else 2 * got[0].shape[0]
    first = count - (len(got) - 1)
    pairs = []
    for i in range(len(got) - 1):
        if i < len(got) - 2:
            spec[i] = dot(table[:, 0:rows], got[i][...])
        else:
            half = rows // 2
            spec[i] = dot(table[:, 0:half], got[i][...]) + dot(table[:, half:rows], got[i + 1][...])
        pairs.append((first + i, spec.at[i]))
    return [[(slot_of(place, m, count, adjoint), at) for m, at in pairs] for adjoint in (False, True)]


def late(place, count, n_got, *refs):
    got, refs = refs[:n_got], refs[n_got:]
    start, part_share, block, rim, lag_ref, table, inverse, keys, values, bias, taps, w_in = refs[:12]
    keep, pass_on, spec, total, mixed, share = refs[12:]
    _, pairs = late_pairs(place, count, got, spec, table)
    accumulate(lag_ref, pairs, True, start, total)
    share[...] = part_share[...]
    gated_part(
        place, count, total, inverse, block, rim, keys, values, bias, taps, w_in, share, mixed, keep, pass_on
    )


def early_first(place, count, block, product, lag_ref, table, total, total_conv, spec):
    rows = block.shape[0]
    spec[...] = dot(table[:, 0:rows], block[...])
    accumulate(lag_ref, [(slot_of(place, 0, count, True), spec)], True, None, total)
    spec[...] = dot(table[...], product[...])
    accumulate(lag_ref, [(slot_of(place, 0, count, False), spec)], False, None, total_conv)


def middle_first(place, count, ms, *refs):
    got, (start, start_conv, lag_ref, table, total, total_conv, spec) = refs[: len(ms)], refs[len(ms) :]
    for i, m in enumerate(ms):
        spec[i] = dot(table[:, 0 : got[i].shape[0]], got[i][...])
    for adjoint, begin, end in ((True, start, total), (False, start_conv, total_conv)):
        pairs = [(slot_of(place, m, count, adjoint), spec.at[i]) for i, m in enumerate(ms)]
        accumulate(lag_ref, pairs, adjoint, begin, end)


def late_first(place, count, n_got, *refs):
    got, refs = refs[:n_got], refs[n_got:]
    start, start_conv, d_out, product, block, rim, lag_ref, table, inverse, keys, values, bias, taps, w_in = refs[:14]
    keep, pass_on, conv, spec, total, mixed, share = refs[14:]
    width = 2 * block.shape[1]
    pairs_conv, pairs = late_pairs(place, count, got, spec, table)
    accumulate(lag_ref, pairs_conv, False, start_conv, total)
    whole = dot(inverse[...], total[...]) + bias[0:1, lanes(0, width, place[1])] * product[...].astype(f32)
    conv[...] = whole.astype(bf16)
    query_part(place, count, d_out, conv, taps, w_in, mixed, share)
    accumulate(lag_ref, pairs, True, start, total)
    gated_part(
        place, count, total, inverse, block, rim, keys, values, bias, taps, w_in, share, mixed, keep, pass_on
    )


def shards(cotangent, projected, w_in, w_out, short_filter, long_filter, filter_bias):
    seq_count = lax.axis_size("seq")
    section_count = lax.axis_size("section")
    seq_place = lax.axis_index("seq")
    section_place = lax.axis_index("section")
    chips = seq_count // 2
    core = seq_place % 2
    place = jnp.stack([seq_place // 2, core]).astype(jnp.int32)
    own_rows = projected.shape[2]
    rows = 2 * own_rows
    width = w_out.shape[2]
    chans = width // 2
    ext = rows + PAD
    limit = (8 + 3 * chips) * 1024 * 1024
    table, lag_table, inverse = tables(rows)
    weight_in, weight_out, bias = w_in[0], w_out[0], filter_bias
    taps = jnp.transpose(short_filter, (1, 0, 2))

    def swap_core(value):
        return lax.ppermute(value, "seq", [(i, i ^ 1) for i in range(seq_count)])

    def swap_chip(value, m):
        return lax.ppermute(value, "seq", [(i, ((i // 2) ^ m) * 2 + i % 2) for i in range(seq_count)])

    def swap_section(value, upper):
        pairs = []
        for i in range(seq_count):
            for s in range(section_count):
                t = s - 1 if (s - upper) % 2 == 0 else s + 1
                j, t = (i, t) if 0 <= t < section_count else (i ^ 1, s)
                pairs.append((i * section_count + s, j * section_count + t))
        return lax.ppermute(value, ("seq", "section"), pairs)

    def shape(n, kind, across=chans):
        return jax.ShapeDtypeStruct((n, across), kind)

    def run(body, outs, scratch, name, micros, *operands):
        return call(body, outs, scratch, name, limit, micros, place, *operands)

    stored, grad = projected[0, 0], cotangent[0]
    lags_own, lags_other = run(
        split_lags, [shape(own_rows, bf16), shape(own_rows, bf16)], [], "split_lags", 0.4, long_filter[0]
    )
    stored_other, rim_send = run(
        split_stored, [shape(own_rows, bf16, 3 * chans), shape(PAD, bf16, 4 * width)], [], "split_stored", 0.6,
        stored, grad, lags_other,
    )
    lags_core = swap_core(lags_other)
    rim_pairs = [(2 * q + 1, (2 * q + 2) % seq_count) for q in range(chips)]
    rim_own = lax.ppermute(rim_send, "seq", rim_pairs + [(b, a) for a, b in rim_pairs])
    lags_here = jnp.where(
        core == 0, jnp.concatenate([lags_own, lags_core]), jnp.concatenate([lags_core, lags_own])
    )
    pieces = [lags_here] + [swap_chip(lags_here, m) for m in range(1, chips)]
    stored_core = swap_core(stored_other)
    grad_core = swap_core(grad)
    rim_core = swap_core(rim_own)
    query, keys, values, product, grad = run(
        mix_stored,
        [shape(ext, f32), shape(ext, f32), shape(ext, f32), shape(ext, bf16), shape(own_rows + PAD, bf16, width)],
        [pltpu.VMEM((rows + 2 * PAD, chans), f32)],
        "mix_stored", 1.3,
        stored, stored_core, rim_own, rim_core, grad, taps, pieces[1], pieces[2],
    )
    spectra = run(
        lambda place, *refs: lag_spectra(place, chips, *refs),
        jax.ShapeDtypeStruct((chips + 1, 2 * ext, chans), f32),
        [pltpu.VMEM((chips * rows + ext + PAD, chans), bf16)],
        "lag_spectra", 2.4,
        *pieces, lag_table,
    )

    spec = pltpu.VMEM((2 * ext, chans), f32)
    total_wide = shape(2 * ext, f32)
    total_scratch = pltpu.VMEM((2 * ext, chans), bf16)
    mixed = pltpu.VMEM((ext + PAD, chans), f32)
    share = pltpu.VMEM((ext, width), f32)
    ms = list(range(1, chips // 2))
    specs = pltpu.VMEM((len(ms), 2 * ext, chans), f32)
    late_specs = pltpu.VMEM((chips - 1 - len(ms), 2 * ext, chans), f32)
    ends = [shape(own_rows + PAD, f32, width), shape(own_rows + PAD, bf16, width)]
    result = jnp.zeros((own_rows, width), bf16)
    conv = None
    for turn in range(section_count):
        first = turn == 0
        block, upper_half, lower_half, rim, d_out = run(
            gate_grad,
            [shape(rows, bf16), shape(own_rows, bf16), shape(own_rows, bf16), shape(PAD, bf16), shape(ext, f32)],
            [],
            "gate_grad", 1.0,
            grad, grad_core if first else swap_core(grad), weight_out, query,
        )

        def send(value, at, m):
            if first:
                value = jnp.where(((seq_place // 2) ^ m) > seq_place // 2, product[at], value)
            return swap_chip(value, m)

        got = [send(block, slice(0, rows), m) for m in range(1, chips - 1)]
        got.append(send(upper_half, slice(0, own_rows), chips - 1))
        got.append(send(lower_half, slice(own_rows, rows), chips - 1))
        soon, last = got[: len(ms)], got[len(ms) :]
        if first:
            start, start_conv = run(
                lambda place, *refs: early_first(place, chips, *refs),
                [total_wide, total_wide], [spec], "early_first", 1.8, block, product, spectra, table,
            )
            start, start_conv = run(
                lambda place, *refs: middle_first(place, chips, ms, *refs),
                [total_wide, total_wide], [specs], "middle_first", 1.0, *soon, start, start_conv, spectra, table,
            )
            keep, pass_on, conv = run(
                lambda place, *refs: late_first(place, chips, len(last), *refs),
                ends + [shape(ext, bf16)], [late_specs, total_scratch, mixed, share], "late_first", 4.0,
                *last, start, start_conv, d_out, product, block, rim, spectra, table, inverse, keys, values, bias,
                taps, weight_in,
            )
        else:
            start, part_share = run(
                lambda place, *refs: early(place, chips, *refs),
                [total_wide, shape(ext, f32, width)], [spec, mixed], "early", 1.6,
                block, d_out, conv, spectra, table, taps, weight_in,
            )
            start = run(
                lambda place, *refs: middle(place, chips, ms, *refs),
                total_wide, [specs], "middle", 0.8, *soon, start, spectra, table,
            )
            keep, pass_on = run(
                lambda place, *refs: late(place, chips, len(last), *refs),
                ends, [late_specs, total_scratch, mixed, share], "late", 3.0,
                *last, start, part_share, block, rim, spectra, table, inverse, keys, values, bias, taps, weight_in,
            )
        summed = (grad.astype(f32) + keep + swap_core(pass_on).astype(f32)).astype(bf16)
        upper = section_count - 1 - turn
        result = jnp.where(section_place == upper, summed[:own_rows], result)
        if turn < section_count - 1:
            grad = swap_section(summed, upper)
    return result[None, None]


def solution(mesh):
    return jax.shard_map(
        shards,
        mesh=mesh,
        in_specs=(
            P(None, "seq", None),
            P("section", None, "seq", None),
            P("section", None, None),
            P("section", None, None),
            P("section", None, None),
            P("section", "seq", None),
            P("section", None),
        ),
        out_specs=P("section", None, "seq", None),
        check_vma=False,
    )
```

time: 170 us -> 119 us (0.70)
  Pallas kernels: 50.1 us -> 33.8 us
  waiting for transfers between devices: 54.7 us -> 40.4 us
  other arithmetic: 8.71 us -> 1.28 us
  local copies, waits for them, and re-layouts: 9.87 us -> 3.08 us
  starting transfers between devices: 46.1 us -> 40.3 us
    ppermute x15 -> x19, waiting for transfers between devices: 38.9 us -> 14.4 us  [swap_chip(): lax.ppermute(value, 'seq', [(i, (i // 2 ^ m) * 2 + i % 2) for i in range(...]
    pallas_call x10 -> x20, Pallas kernels: 50.1 us -> 33.8 us  [call(): pl.pallas_call(body, out_shape=outs, in_specs=[pl.BlockSpec(memory_space=...]
    ppermute x4, waiting for transfers between devices: 5.2 us -> 14.8 us  [the longest x3 12.9 us: swap_section(): return lax.ppermute(value, ('seq', 'section'), pairs)]
    ppermute x4, starting transfers between devices: 21.5 us -> 13.1 us  [the longest x3 9.53 us: swap_section(): return lax.ppermute(value, ('seq', 'section'), pairs)]
    ppermute x15 -> x19, starting transfers between devices: 18.9 us -> 25.6 us  [swap_chip(): lax.ppermute(value, 'seq', [(i, (i // 2 ^ m) * 2 + i % 2) for i in range(...]
    unnamed x61 -> x24, local copies, waits for them, and re-layouts: 8.82 us -> 3.08 us
    ppermute x11, starting transfers between devices: 5.73 us -> 1.58 us  [swap_core(): return lax.ppermute(value, 'seq', [(i, i ^ 1) for i in range(seq_count)])]
    convert_element_type x3, other arithmetic: 3.17 us -> 0.24 us  [shards(): (grad.astype(f32) + keep + swap_core(pass_on).astype(f32)).astype(bf16)]
  transfers between devices with their start and end apart: 30 -> 34, of which waited for: 16 -> 24; matrix products, arithmetic and copies ran while one was open for 3% -> 0% of each run, Pallas kernels for 6% -> 14%
where the time goes in v2:
time: 119 us
  waiting for transfers between devices  40.4 us (34%)
  starting transfers between devices  40.3 us (34%)
  Pallas kernels  33.8 us (28%)
  local copies, waits for them, and re-layouts  3.08 us (3%)
  other arithmetic  1.28 us (1%)
    pallas_call x20, Pallas kernels, call(): pl.pallas_call(body, out_shape=outs, in_specs=[pl.BlockSpec(memory_space=...  33.8 us
    ppermute x19, starting transfers between devices, swap_chip(): lax.ppermute(value, 'seq', [(i, (i // 2 ^ m) * 2 + i % 2) for i in range(...  25.6 us
    ppermute x19, waiting for transfers between devices, swap_chip(): lax.ppermute(value, 'seq', [(i, (i // 2 ^ m) * 2 + i % 2) for i in range(...  14.4 us
    ppermute x3, waiting for transfers between devices, swap_section(): return lax.ppermute(value, ('seq', 'section'), pairs)  12.9 us
    ppermute x11, waiting for transfers between devices, swap_core(): return lax.ppermute(value, 'seq', [(i, i ^ 1) for i in range(seq_count)])  11.2 us
    ppermute x3, starting transfers between devices, swap_section(): return lax.ppermute(value, ('seq', 'section'), pairs)  9.53 us
    ppermute x1, starting transfers between devices, shards(): lax.ppermute(rim_send, 'seq', rim_pairs + [(b, a) for a, b in rim_pairs])  3.58 us
    unnamed x24, local copies, waits for them, and re-layouts  3.08 us
  transfers between devices with their start and end apart: 34, of which 24 were waited for; matrix products, arithmetic and copies ran while one was open for 0% of the time, Pallas kernels for 14%

profile of v2, /device:TPU:0, one launch (start us, length us, event | category | flops | bytes accessed | tf_op | source)
XLA Modules:
  0.0 119.2 jit_solution(3201546873703992545)
XLA Ops:
  4.9 3.6 %collective-permute-start.1 = (bf16[16,3072]{1,0:T(8,128)(2,1)S(1)}, bf16[16,3072]{1,0:T(8,128)(2,1)}, u32[]{:S(2)}, u32[]{:S(2)}) collective-permute-start(bf16[16,3072]{1,0:T(8,128)(2,1)S(1)} %get-tuple-element.55), channel_id=1, source_target_pairs={{4,8},{12,16},{20,24},{28,0},{8,4},{16,12},{24,20},{0,28},{5,9},{1... | collective-permute-start | bytes 294920 | tf_op jit(solution)/shard_map/ppermute | solution.py:336
  9.7 1.9 %collective-permute-done.1.rim_own = bf16[16,3072]{1,0:T(8,128)(2,1)} collective-permute-done((bf16[16,3072]{1,0:T(8,128)(2,1)S(1)}, bf16[16,3072]{1,0:T(8,128)(2,1)}, u32[]{:S(2)}, u32[]{:S(2)}) %collective-permute-start.1) | collective-permute-done | bytes 98336 | tf_op jit(solution)/shard_map/ppermute | solution.py:336
  13.2 2.9 %collective-permute-start.11 = (bf16[256,384]{1,0:T(8,128)(2,1)S(1)}, bf16[256,384]{1,0:T(8,128)(2,1)S(1)}, u32[]{:S(2)}, u32[]{:S(2)}) collective-permute-start(bf16[256,384]{1,0:T(8,128)(2,1)S(1)} %maximum_select_fusion.refs_0_), channel_id=1, source_target_pairs={{0,24},{4,28},{8,16},{12,20},{16,8},{20,12},{24,0},{28,4},{1,25},{... | collective-permute-start | bytes 589832 | tf_op jit(solution)/shard_map/ppermute | solution.py:309
  16.1 1.7 %mix_stored.1 = (f32[272,384]{1,0:T(8,128)S(1)}, f32[272,384]{1,0:T(8,128)S(1)}, f32[272,384]{1,0:T(8,128)S(1)}, bf16[272,384]{1,0:T(8,128)(2,1)S(1)}, bf16[144,768]{1,0:T(8,128)(2,1)S(1)}) custom-call(s32[2]{0:T(128)S(1)} %pad_add_fusion.place, bf16[128,2304]{1,0:T(8,128)(2,1)S(1)} %bitcast.30, bf16[128,1152]{1,0:T(8,128)(2,1)S(1)} %collective-permute-done.stored_core, ...), custom_call_target="tpu_custom_call" | custom-call | flops 1300000000 | tf_op jit(solution)/shard_map/mix_stored/pallas_call | solution.py:52
  20.1 1.8 %collective-permute-start.8 = (bf16[128,384]{1,0:T(8,128)(2,1)S(1)}, bf16[128,384]{1,0:T(8,128)(2,1)S(1)}, u32[]{:S(2)}, u32[]{:S(2)}) collective-permute-start(bf16[128,384]{1,0:T(8,128)(2,1)S(1)} %get-tuple-element.104), channel_id=1, source_target_pairs={{0,24},{4,28},{8,16},{12,20},{16,8},{20,12},{24,0},{28,4},{1,25},{... | collective-permute-start | bytes 294920 | tf_op jit(solution)/shard_map/ppermute | solution.py:309
  23.1 1.8 %collective-permute-start.10 = (bf16[256,384]{1,0:T(8,128)(2,1)S(1)}, bf16[256,384]{1,0:T(8,128)(2,1)S(1)}, u32[]{:S(2)}, u32[]{:S(2)}) collective-permute-start(bf16[256,384]{1,0:T(8,128)(2,1)S(1)} %get-tuple-element.101), channel_id=1, source_target_pairs={{0,8},{4,12},{8,0},{12,4},{16,24},{20,28},{24,16},{28,20},{1,9},{5... | collective-permute-start | bytes 589832 | tf_op jit(solution)/shard_map/ppermute | solution.py:309
  24.9 2.4 %lag_spectra.1.refs_2_.refs_3_.refs_9_.refs_7_ = f32[5,544,384]{2,1,0:T(8,128)S(1)} custom-call(s32[2]{0:T(128)S(1)} %pad_add_fusion.place, bf16[256,384]{1,0:T(8,128)(2,1)S(1)} %maximum_select_fusion.refs_0_, bf16[256,384]{1,0:T(8,128)(2,1)S(1)} %collective-permute-done.4._.refs_1_, bf16[256,384]{1,0:T(8,128)(2,1)S(1)} %collective-permute-done.5.__.refs_2_, ...), custom_call_target="tpu_custom_call" | custom-call | flops 2400000000 | tf_op jit(solution)/shard_map/lag_spectra/pallas_call | solution.py:52
  27.3 1.9 %early_first.1 = (f32[544,384]{1,0:T(8,128)S(1)}, f32[544,384]{1,0:T(8,128)S(1)}) custom-call(s32[2]{0:T(128)S(1)} %pad_add_fusion.place, bf16[256,384]{1,0:T(8,128)(2,1)S(1)} %get-tuple-element.60.refs_0_.refs_7_, bf16[272,384]{1,0:T(8,128)(2,1)S(1)} %get-tuple-element.58.refs_1_.refs_6_, f32[5,544,384]{2,1,0:T(8,128)S(1)} %lag_spectra.1.refs_2_.refs_3_.refs_9_.refs_7_, ...), custom_call_target="tpu_custom_call" | custom-call | flops 1800000000 | tf_op jit(solution)/shard_map/early_first/pallas_call | solution.py:52
  29.3 2.3 %collective-permute-done.10.refs_0_ = bf16[256,384]{1,0:T(8,128)(2,1)S(1)} collective-permute-done((bf16[256,384]{1,0:T(8,128)(2,1)S(1)}, bf16[256,384]{1,0:T(8,128)(2,1)S(1)}, u32[]{:S(2)}, u32[]{:S(2)}) %collective-permute-start.10) | collective-permute-done | bytes 196640 | tf_op jit(solution)/shard_map/ppermute | solution.py:309
  33.0 4.2 %late_first.1 = (f32[144,768]{1,0:T(8,128)S(1)}, bf16[144,768]{1,0:T(8,128)(2,1)S(1)}, bf16[272,384]{1,0:T(8,128)(2,1)S(1)}) custom-call(s32[2]{0:T(128)S(1)} %pad_add_fusion.place, bf16[256,384]{1,0:T(8,128)(2,1)S(1)} %collective-permute-done.7.refs_0_, bf16[128,384]{1,0:T(8,128)(2,1)S(1)} %collective-permute-done.8.refs_1_, ...), custom_call_target="tpu_custom_call" | custom-call | flops 4000000000 | tf_op jit(solution)/shard_map/late_first/pallas_call | solution.py:52
  38.8 1.7 %collective-permute-start.13 = (bf16[144,768]{1,0:T(8,128)(2,1)S(1)}, bf16[144,768]{1,0:T(8,128)(2,1)S(1)}, u32[]{:S(2)}, u32[]{:S(2)}) collective-permute-start(bf16[144,768]{1,0:T(8,128)(2,1)S(1)} %add_convert_fusion.2), channel_id=1, source_target_pairs={{0,1},{1,0},{2,3},{3,2},{4,5},{5,4},{6,7},{7,6},{8,9},{9,8},{10,11... | collective-permute-start | bytes 663560 | tf_op jit(solution)/shard_map/ppermute | solution.py:318
  40.5 5.8 %collective-permute-done.13.g_own = bf16[144,768]{1,0:T(8,128)(2,1)S(1)} collective-permute-done((bf16[144,768]{1,0:T(8,128)(2,1)S(1)}, bf16[144,768]{1,0:T(8,128)(2,1)S(1)}, u32[]{:S(2)}, u32[]{:S(2)}) %collective-permute-start.13) | collective-permute-done | bytes 221216 | tf_op jit(solution)/shard_map/ppermute | solution.py:318
  52.5 1.9 %collective-permute-start.17 = (bf16[128,384]{1,0:T(8,128)(2,1)S(1)}, bf16[128,384]{1,0:T(8,128)(2,1)S(1)}, u32[]{:S(2)}, u32[]{:S(2)}) collective-permute-start(bf16[128,384]{1,0:T(8,128)(2,1)S(1)} %get-tuple-element.75), channel_id=1, source_target_pairs={{0,24},{4,28},{8,16},{12,20},{16,8},{20,12},{24,0},{28,4},{1,25},{... | collective-permute-start | bytes 294920 | tf_op jit(solution)/shard_map/ppermute | solution.py:309
  54.4 1.6 %early.3 = (f32[544,384]{1,0:T(8,128)S(1)}, f32[272,768]{1,0:T(8,128)S(1)}) custom-call(s32[2]{0:T(128)S(1)} %pad_add_fusion.place, bf16[256,384]{1,0:T(8,128)(2,1)S(1)} %get-tuple-element.73.refs_0_.refs_5_, f32[272,384]{1,0:T(8,128)S(1)} %get-tuple-element.76.refs_1_, bf16[272,384]{1,0:T(8,128)(2,1)S(1)} %get-tuple-element.77.refs_2_, ...), custom_call_target="tpu_custom_call" | custom-call | flops 1600000000 | tf_op jit(solution)/shard_map/early/pallas_call | solution.py:52
  60.8 2.9 %late.3 = (f32[144,768]{1,0:T(8,128)S(1)}, bf16[144,768]{1,0:T(8,128)(2,1)S(1)}) custom-call(s32[2]{0:T(128)S(1)} %pad_add_fusion.place, bf16[256,384]{1,0:T(8,128)(2,1)S(1)} %collective-permute-done.15.refs_0_, bf16[128,384]{1,0:T(8,128)(2,1)S(1)} %collective-permute-done.16.refs_1_, bf16[128,384]{1,0:T(8,128)(2,1)S(1)} %collective-permute-done.17.refs_2_, ...), custom_call_target="tpu_custom_call" | custom-call | flops 3000000000 | tf_op jit(solution)/shard_map/late/pallas_call | solution.py:52
  71.4 1.5 %collective-permute-start.23 = (bf16[128,384]{1,0:T(8,128)(2,1)S(1)}, bf16[128,384]{1,0:T(8,128)(2,1)S(1)}, u32[]{:S(2)}, u32[]{:S(2)}) collective-permute-start(bf16[128,384]{1,0:T(8,128)(2,1)S(1)} %get-tuple-element.84), channel_id=1, source_target_pairs={{0,24},{4,28},{8,16},{12,20},{16,8},{20,12},{24,0},{28,4},{1,25},{... | collective-permute-start | bytes 294920 | tf_op jit(solution)/shard_map/ppermute | solution.py:309
  74.3 1.6 %early.4 = (f32[544,384]{1,0:T(8,128)S(1)}, f32[272,768]{1,0:T(8,128)S(1)}) custom-call(s32[2]{0:T(128)S(1)} %pad_add_fusion.place, bf16[256,384]{1,0:T(8,128)(2,1)S(1)} %get-tuple-element.83.refs_0_.refs_5_, f32[272,384]{1,0:T(8,128)S(1)} %get-tuple-element.86.refs_1_, bf16[272,384]{1,0:T(8,128)(2,1)S(1)} %get-tuple-element.77.refs_2_, ...), custom_call_target="tpu_custom_call" | custom-call | flops 1600000000 | tf_op jit(solution)/shard_map/early/pallas_call | solution.py:52
  78.3 2.0 %collective-permute-done.23.refs_1_ = bf16[128,384]{1,0:T(8,128)(2,1)S(1)} collective-permute-done((bf16[128,384]{1,0:T(8,128)(2,1)S(1)}, bf16[128,384]{1,0:T(8,128)(2,1)S(1)}, u32[]{:S(2)}, u32[]{:S(2)}) %collective-permute-start.23) | collective-permute-done | bytes 98336 | tf_op jit(solution)/shard_map/ppermute | solution.py:309
  81.6 2.9 %late.4 = (f32[144,768]{1,0:T(8,128)S(1)}, bf16[144,768]{1,0:T(8,128)(2,1)S(1)}) custom-call(s32[2]{0:T(128)S(1)} %pad_add_fusion.place, bf16[256,384]{1,0:T(8,128)(2,1)S(1)} %collective-permute-done.22.refs_0_, bf16[128,384]{1,0:T(8,128)(2,1)S(1)} %collective-permute-done.23.refs_1_, bf16[128,384]{1,0:T(8,128)(2,1)S(1)} %collective-permute-done.24.refs_2_, ...), custom_call_target="tpu_custom_call" | custom-call | flops 3000000000 | tf_op jit(solution)/shard_map/late/pallas_call | solution.py:52
  86.1 7.6 %collective-permute-start.27 = (bf16[144,768]{1,0:T(8,128)(2,1)S(1)}, bf16[144,768]{1,0:T(8,128)(2,1)S(1)}, u32[]{:S(2)}, u32[]{:S(2)}) collective-permute-start(bf16[144,768]{1,0:T(8,128)(2,1)S(1)} %add_convert_fusion), channel_id=1, source_target_pairs={{0,1},{1,0},{2,3},{3,2},{4,5},{5,4},{6,7},{7,6},{8,9},{9,8},{10,11... | collective-permute-start | bytes 663560 | tf_op jit(solution)/shard_map/ppermute | solution.py:318
  93.8 5.7 %collective-permute-done.27.g_own = bf16[144,768]{1,0:T(8,128)(2,1)S(1)} collective-permute-done((bf16[144,768]{1,0:T(8,128)(2,1)S(1)}, bf16[144,768]{1,0:T(8,128)(2,1)S(1)}, u32[]{:S(2)}, u32[]{:S(2)}) %collective-permute-start.27) | collective-permute-done | bytes 221216 | tf_op jit(solution)/shard_map/ppermute | solution.py:318
  105.6 1.7 %collective-permute-start.31 = (bf16[128,384]{1,0:T(8,128)(2,1)S(1)}, bf16[128,384]{1,0:T(8,128)(2,1)S(1)}, u32[]{:S(2)}, u32[]{:S(2)}) collective-permute-start(bf16[128,384]{1,0:T(8,128)(2,1)S(1)} %get-tuple-element.94), channel_id=1, source_target_pairs={{0,24},{4,28},{8,16},{12,20},{16,8},{20,12},{24,0},{28,4},{1,25},{... | collective-permute-start | bytes 294920 | tf_op jit(solution)/shard_map/ppermute | solution.py:309
  107.4 1.6 %early.5 = (f32[544,384]{1,0:T(8,128)S(1)}, f32[272,768]{1,0:T(8,128)S(1)}) custom-call(s32[2]{0:T(128)S(1)} %pad_add_fusion.place, bf16[256,384]{1,0:T(8,128)(2,1)S(1)} %get-tuple-element.92.refs_0_.refs_5_, f32[272,384]{1,0:T(8,128)S(1)} %get-tuple-element.95.refs_1_, bf16[272,384]{1,0:T(8,128)(2,1)S(1)} %get-tuple-element.77.refs_2_, ...), custom_call_target="tpu_custom_call" | custom-call | flops 1600000000 | tf_op jit(solution)/shard_map/early/pallas_call | solution.py:52
  113.9 2.9 %late.5 = (f32[144,768]{1,0:T(8,128)S(1)}, bf16[144,768]{1,0:T(8,128)(2,1)S(1)}) custom-call(s32[2]{0:T(128)S(1)} %pad_add_fusion.place, bf16[256,384]{1,0:T(8,128)(2,1)S(1)} %collective-permute-done.29.refs_0_, bf16[128,384]{1,0:T(8,128)(2,1)S(1)} %collective-permute-done.30.refs_1_, bf16[128,384]{1,0:T(8,128)(2,1)S(1)} %collective-permute-done.31.refs_2_, ...), custom_call_target="tpu_custom_call" | custom-call | flops 3000000000 | tf_op jit(solution)/shard_map/late/pallas_call | solution.py:52
  (96 shorter events, 52.9 us)
Async XLA Ops:
  1.7 6.8 %collective-permute-start.3 = (bf16[128,384]{1,0:T(8,128)(2,1)S(1)}, bf16[128,384]{1,0:T(8,128)(2,1)S(1)}, u32[]{:S(2)}, u32[]{:S(2)}) collective-permute-start(bf16[128,384]{1,0:T(8,128)(2,1)S(1)} %get-tuple-element.53._), channel_id=1, source_target_pairs={{0,4},{4,0},{8,12},{12,8},{16,20},{20,16},{24,28},{28,24},{1,5},{5... | collective-permute-start | bytes 294920 | tf_op jit(solution)/shard_map/ppermute | solution.py:306
  4.8 11.3 %collective-permute-start = (bf16[128,1152]{1,0:T(8,128)(2,1)S(1)}, bf16[128,1152]{1,0:T(8,128)(2,1)S(1)}, u32[]{:S(2)}, u32[]{:S(2)}) collective-permute-start(bf16[128,1152]{1,0:T(8,128)(2,1)S(1)} %get-tuple-element.54), channel_id=1, source_target_pairs={{0,4},{4,0},{8,12},{12,8},{16,20},{20,16},{24,28},{28,24},{1,5},{5... | collective-permute-start | bytes 884744 | tf_op jit(solution)/shard_map/ppermute | solution.py:306
  4.9 6.7 %collective-permute-start.1 = (bf16[16,3072]{1,0:T(8,128)(2,1)S(1)}, bf16[16,3072]{1,0:T(8,128)(2,1)}, u32[]{:S(2)}, u32[]{:S(2)}) collective-permute-start(bf16[16,3072]{1,0:T(8,128)(2,1)S(1)} %get-tuple-element.55), channel_id=1, source_target_pairs={{4,8},{12,16},{20,24},{28,0},{8,4},{16,12},{24,20},{0,28},{5,9},{1... | collective-permute-start | bytes 294920 | tf_op jit(solution)/shard_map/ppermute | solution.py:336
  8.6 7.6 %collective-permute-start.4 = (bf16[256,384]{1,0:T(8,128)(2,1)S(1)}, bf16[256,384]{1,0:T(8,128)(2,1)S(1)}, u32[]{:S(2)}, u32[]{:S(2)}) collective-permute-start(bf16[256,384]{1,0:T(8,128)(2,1)S(1)} %maximum_select_fusion.refs_0_), channel_id=1, source_target_pairs={{0,8},{4,12},{8,0},{12,4},{16,24},{20,28},{24,16},{28,20},{1,9},{5... | collective-permute-start | bytes 589832 | tf_op jit(solution)/shard_map/ppermute | solution.py:309
  8.6 7.5 %collective-permute-start.5 = (bf16[256,384]{1,0:T(8,128)(2,1)S(1)}, bf16[256,384]{1,0:T(8,128)(2,1)S(1)}, u32[]{:S(2)}, u32[]{:S(2)}) collective-permute-start(bf16[256,384]{1,0:T(8,128)(2,1)S(1)} %maximum_select_fusion.refs_0_), channel_id=1, source_target_pairs={{0,16},{4,20},{8,24},{12,28},{16,0},{20,4},{24,8},{28,12},{1,17},{... | collective-permute-start | bytes 589832 | tf_op jit(solution)/shard_map/ppermute | solution.py:309
  13.2 11.7 %collective-permute-start.11 = (bf16[256,384]{1,0:T(8,128)(2,1)S(1)}, bf16[256,384]{1,0:T(8,128)(2,1)S(1)}, u32[]{:S(2)}, u32[]{:S(2)}) collective-permute-start(bf16[256,384]{1,0:T(8,128)(2,1)S(1)} %maximum_select_fusion.refs_0_), channel_id=1, source_target_pairs={{0,24},{4,28},{8,16},{12,20},{16,8},{20,12},{24,0},{28,4},{1,25},{... | collective-permute-start | bytes 589832 | tf_op jit(solution)/shard_map/ppermute | solution.py:309
  19.0 14.0 %collective-permute-start.7 = (bf16[256,384]{1,0:T(8,128)(2,1)S(1)}, bf16[256,384]{1,0:T(8,128)(2,1)S(1)}, u32[]{:S(2)}, u32[]{:S(2)}) collective-permute-start(bf16[256,384]{1,0:T(8,128)(2,1)S(1)} %get-tuple-element.102), channel_id=1, source_target_pairs={{0,16},{4,20},{8,24},{12,28},{16,0},{20,4},{24,8},{28,12},{1,17},{... | collective-permute-start | bytes 589832 | tf_op jit(solution)/shard_map/ppermute | solution.py:309
  20.1 12.8 %collective-permute-start.8 = (bf16[128,384]{1,0:T(8,128)(2,1)S(1)}, bf16[128,384]{1,0:T(8,128)(2,1)S(1)}, u32[]{:S(2)}, u32[]{:S(2)}) collective-permute-start(bf16[128,384]{1,0:T(8,128)(2,1)S(1)} %get-tuple-element.104), channel_id=1, source_target_pairs={{0,24},{4,28},{8,16},{12,20},{16,8},{20,12},{24,0},{28,4},{1,25},{... | collective-permute-start | bytes 294920 | tf_op jit(solution)/shard_map/ppermute | solution.py:309
  22.0 11.0 %collective-permute-start.9 = (bf16[128,384]{1,0:T(8,128)(2,1)S(1)}, bf16[128,384]{1,0:T(8,128)(2,1)S(1)}, u32[]{:S(2)}, u32[]{:S(2)}) collective-permute-start(bf16[128,384]{1,0:T(8,128)(2,1)S(1)} %get-tuple-element.103), channel_id=1, source_target_pairs={{0,24},{4,28},{8,16},{12,20},{16,8},{20,12},{24,0},{28,4},{1,25},{... | collective-permute-start | bytes 294920 | tf_op jit(solution)/shard_map/ppermute | solution.py:309
  23.1 8.4 %collective-permute-start.10 = (bf16[256,384]{1,0:T(8,128)(2,1)S(1)}, bf16[256,384]{1,0:T(8,128)(2,1)S(1)}, u32[]{:S(2)}, u32[]{:S(2)}) collective-permute-start(bf16[256,384]{1,0:T(8,128)(2,1)S(1)} %get-tuple-element.101), channel_id=1, source_target_pairs={{0,8},{4,12},{8,0},{12,4},{16,24},{20,28},{24,16},{28,20},{1,9},{5... | collective-permute-start | bytes 589832 | tf_op jit(solution)/shard_map/ppermute | solution.py:309
  38.8 7.5 %collective-permute-start.13 = (bf16[144,768]{1,0:T(8,128)(2,1)S(1)}, bf16[144,768]{1,0:T(8,128)(2,1)S(1)}, u32[]{:S(2)}, u32[]{:S(2)}) collective-permute-start(bf16[144,768]{1,0:T(8,128)(2,1)S(1)} %add_convert_fusion.2), channel_id=1, source_target_pairs={{0,1},{1,0},{2,3},{3,2},{4,5},{5,4},{6,7},{7,6},{8,9},{9,8},{10,11... | collective-permute-start | bytes 663560 | tf_op jit(solution)/shard_map/ppermute | solution.py:318
  48.9 7.8 %collective-permute-start.18 = (bf16[256,384]{1,0:T(8,128)(2,1)S(1)}, bf16[256,384]{1,0:T(8,128)(2,1)S(1)}, u32[]{:S(2)}, u32[]{:S(2)}) collective-permute-start(bf16[256,384]{1,0:T(8,128)(2,1)S(1)} %get-tuple-element.73.refs_0_.refs_5_), channel_id=1, source_target_pairs={{0,8},{4,12},{8,0},{12,4},{16,24},{20,28},{24,16},{28,20},{1,9},{5... | collective-permute-start | bytes 589832 | tf_op jit(solution)/shard_map/ppermute | solution.py:309
  49.9 10.9 %collective-permute-start.15 = (bf16[256,384]{1,0:T(8,128)(2,1)S(1)}, bf16[256,384]{1,0:T(8,128)(2,1)S(1)}, u32[]{:S(2)}, u32[]{:S(2)}) collective-permute-start(bf16[256,384]{1,0:T(8,128)(2,1)S(1)} %get-tuple-element.73.refs_0_.refs_5_), channel_id=1, source_target_pairs={{0,16},{4,20},{8,24},{12,28},{16,0},{20,4},{24,8},{28,12},{1,17},{... | collective-permute-start | bytes 589832 | tf_op jit(solution)/shard_map/ppermute | solution.py:309
  51.4 7.8 %collective-permute-start.16 = (bf16[128,384]{1,0:T(8,128)(2,1)S(1)}, bf16[128,384]{1,0:T(8,128)(2,1)S(1)}, u32[]{:S(2)}, u32[]{:S(2)}) collective-permute-start(bf16[128,384]{1,0:T(8,128)(2,1)S(1)} %get-tuple-element.74), channel_id=1, source_target_pairs={{0,24},{4,28},{8,16},{12,20},{16,8},{20,12},{24,0},{28,4},{1,25},{... | collective-permute-start | bytes 294920 | tf_op jit(solution)/shard_map/ppermute | solution.py:309
  52.5 8.0 %collective-permute-start.17 = (bf16[128,384]{1,0:T(8,128)(2,1)S(1)}, bf16[128,384]{1,0:T(8,128)(2,1)S(1)}, u32[]{:S(2)}, u32[]{:S(2)}) collective-permute-start(bf16[128,384]{1,0:T(8,128)(2,1)S(1)} %get-tuple-element.75), channel_id=1, source_target_pairs={{0,24},{4,28},{8,16},{12,20},{16,8},{20,12},{24,0},{28,4},{1,25},{... | collective-permute-start | bytes 294920 | tf_op jit(solution)/shard_map/ppermute | solution.py:309
  69.4 7.8 %collective-permute-start.25 = (bf16[256,384]{1,0:T(8,128)(2,1)S(1)}, bf16[256,384]{1,0:T(8,128)(2,1)S(1)}, u32[]{:S(2)}, u32[]{:S(2)}) collective-permute-start(bf16[256,384]{1,0:T(8,128)(2,1)S(1)} %get-tuple-element.83.refs_0_.refs_5_), channel_id=1, source_target_pairs={{0,8},{4,12},{8,0},{12,4},{16,24},{20,28},{24,16},{28,20},{1,9},{5... | collective-permute-start | bytes 589832 | tf_op jit(solution)/shard_map/ppermute | solution.py:309
  70.7 10.9 %collective-permute-start.22 = (bf16[256,384]{1,0:T(8,128)(2,1)S(1)}, bf16[256,384]{1,0:T(8,128)(2,1)S(1)}, u32[]{:S(2)}, u32[]{:S(2)}) collective-permute-start(bf16[256,384]{1,0:T(8,128)(2,1)S(1)} %get-tuple-element.83.refs_0_.refs_5_), channel_id=1, source_target_pairs={{0,16},{4,20},{8,24},{12,28},{16,0},{20,4},{24,8},{28,12},{1,17},{... | collective-permute-start | bytes 589832 | tf_op jit(solution)/shard_map/ppermute | solution.py:309
  71.4 8.9 %collective-permute-start.23 = (bf16[128,384]{1,0:T(8,128)(2,1)S(1)}, bf16[128,384]{1,0:T(8,128)(2,1)S(1)}, u32[]{:S(2)}, u32[]{:S(2)}) collective-permute-start(bf16[128,384]{1,0:T(8,128)(2,1)S(1)} %get-tuple-element.84), channel_id=1, source_target_pairs={{0,24},{4,28},{8,16},{12,20},{16,8},{20,12},{24,0},{28,4},{1,25},{... | collective-permute-start | bytes 294920 | tf_op jit(solution)/shard_map/ppermute | solution.py:309
  73.0 8.6 %collective-permute-start.24 = (bf16[128,384]{1,0:T(8,128)(2,1)S(1)}, bf16[128,384]{1,0:T(8,128)(2,1)S(1)}, u32[]{:S(2)}, u32[]{:S(2)}) collective-permute-start(bf16[128,384]{1,0:T(8,128)(2,1)S(1)} %get-tuple-element.85), channel_id=1, source_target_pairs={{0,24},{4,28},{8,16},{12,20},{16,8},{20,12},{24,0},{28,4},{1,25},{... | collective-permute-start | bytes 294920 | tf_op jit(solution)/shard_map/ppermute | solution.py:309
  86.1 13.4 %collective-permute-start.27 = (bf16[144,768]{1,0:T(8,128)(2,1)S(1)}, bf16[144,768]{1,0:T(8,128)(2,1)S(1)}, u32[]{:S(2)}, u32[]{:S(2)}) collective-permute-start(bf16[144,768]{1,0:T(8,128)(2,1)S(1)} %add_convert_fusion), channel_id=1, source_target_pairs={{0,1},{1,0},{2,3},{3,2},{4,5},{5,4},{6,7},{7,6},{8,9},{9,8},{10,11... | collective-permute-start | bytes 663560 | tf_op jit(solution)/shard_map/ppermute | solution.py:318
  102.1 7.8 %collective-permute-start.32 = (bf16[256,384]{1,0:T(8,128)(2,1)S(1)}, bf16[256,384]{1,0:T(8,128)(2,1)S(1)}, u32[]{:S(2)}, u32[]{:S(2)}) collective-permute-start(bf16[256,384]{1,0:T(8,128)(2,1)S(1)} %get-tuple-element.92.refs_0_.refs_5_), channel_id=1, source_target_pairs={{0,8},{4,12},{8,0},{12,4},{16,24},{20,28},{24,16},{28,20},{1,9},{5... | collective-permute-start | bytes 589832 | tf_op jit(solution)/shard_map/ppermute | solution.py:309
  103.1 10.9 %collective-permute-start.29 = (bf16[256,384]{1,0:T(8,128)(2,1)S(1)}, bf16[256,384]{1,0:T(8,128)(2,1)S(1)}, u32[]{:S(2)}, u32[]{:S(2)}) collective-permute-start(bf16[256,384]{1,0:T(8,128)(2,1)S(1)} %get-tuple-element.92.refs_0_.refs_5_), channel_id=1, source_target_pairs={{0,16},{4,20},{8,24},{12,28},{16,0},{20,4},{24,8},{28,12},{1,17},{... | collective-permute-start | bytes 589832 | tf_op jit(solution)/shard_map/ppermute | solution.py:309
  104.4 8.0 %collective-permute-start.30 = (bf16[128,384]{1,0:T(8,128)(2,1)S(1)}, bf16[128,384]{1,0:T(8,128)(2,1)S(1)}, u32[]{:S(2)}, u32[]{:S(2)}) collective-permute-start(bf16[128,384]{1,0:T(8,128)(2,1)S(1)} %get-tuple-element.93), channel_id=1, source_target_pairs={{0,24},{4,28},{8,16},{12,20},{16,8},{20,12},{24,0},{28,4},{1,25},{... | collective-permute-start | bytes 294920 | tf_op jit(solution)/shard_map/ppermute | solution.py:309
  105.6 8.1 %collective-permute-start.31 = (bf16[128,384]{1,0:T(8,128)(2,1)S(1)}, bf16[128,384]{1,0:T(8,128)(2,1)S(1)}, u32[]{:S(2)}, u32[]{:S(2)}) collective-permute-start(bf16[128,384]{1,0:T(8,128)(2,1)S(1)} %get-tuple-element.94), channel_id=1, source_target_pairs={{0,24},{4,28},{8,16},{12,20},{16,8},{20,12},{24,0},{28,4},{1,25},{... | collective-permute-start | bytes 294920 | tf_op jit(solution)/shard_map/ppermute | solution.py:309
  (22 other events, 101.8 us)

commit v3 on v2

--- a/solution.py
+++ b/solution.py
@@ -47,18 +47,23 @@
     return pl.ds(pl.multiple_of(side * own, 16), own)
 
 
-def call(body, outs, scratch, name, limit, micros, place, *operands):
+def call(body, outs, scratch, name, limit, micros, *operands):
     vmem = pl.BlockSpec(memory_space=pltpu.VMEM)
+
+    def placed(*refs):
+        seq = lax.axis_index("seq")
+        body((seq // 2, seq % 2), *refs)
+
     return pl.pallas_call(
-        body,
+        placed,
         out_shape=outs,
-        in_specs=[pl.BlockSpec(memory_space=pltpu.SMEM)] + [vmem] * len(operands),
+        in_specs=[vmem] * len(operands),
         out_specs=jax.tree.map(lambda _: vmem, outs),
         scratch_shapes=scratch,
         compiler_params=pltpu.CompilerParams(vmem_limit_bytes=limit),
         cost_estimate=pl.CostEstimate(flops=int(micros * 1e9), bytes_accessed=0, transcendentals=0),
         name=name,
-    )(place, *operands)
+    )(*operands)
 
 
 def split_lags(place, lags, own, other):
@@ -135,6 +140,43 @@
     rim[...] = (d_out[rows:] * query[rows:]).astype(bf16)
 
 
+def gate_only(place, d_out, query, _, block, upper, lower, rim):
+    rows = block.shape[0]
+    own = rows // 2
+    d_conv = (d_out[...].astype(f32) * query[...]).astype(bf16)
+    upper[...] = d_conv[0:own]
+    lower[...] = d_conv[own:rows]
+    block[...] = d_conv[0:rows]
+    rim[...] = d_conv[rows:]
+
+
+def carry_grad(place, g_own, g_core, below, _, out):
+    core = place[1]
+    rows = out.shape[0] - PAD
+    own = rows // 2
+    wide = dot_last(g_own[...], below[...])
+    out[side_rows(core, own)] = wide[:own]
+    out[rows:] = wide[own:]
+    out[side_rows(1 - core, own)] = dot_last(g_core[0:own], below[...])
+
+
+def split_rows(place, share, _, keep, pass_on):
+    rows = share.shape[0] - PAD
+    own = rows // 2
+    keep[0:own] = share[side_rows(place[1], own)]
+    keep[own:] = share[rows:]
+    pass_on[0:own] = share[side_rows(1 - place[1], own)].astype(bf16)
+    pass_on[own:] = share[rows:].astype(bf16)
+
+
+def keep_half(place, short_share, below, carried, keep):
+    keep[...] = carried[...] + dot_last(short_share[...], below[...])
+
+
+def pass_half(place, short_share, below_core, pass_on):
+    pass_on[...] = dot_last(short_share[...], below_core[...]).astype(bf16)
+
+
 def slot_of(place, m, count, adjoint):
     chip, other = place[0], place[0] ^ m
     distance = other - chip if adjoint else chip - other
@@ -179,41 +221,42 @@
     return jnp.where((ids < rows) | (place[0] < count - 1), 1.0, 0.0)
 
 
-def query_part(place, count, d_out, conv, taps, w_in, mixed, share):
+def query_part(place, count, d_out, conv, taps, mixed, proj_query):
     ext, chans = d_out.shape
     rows, width = ext - PAD, 2 * chans
     inside = inside_rows(place, count, rows, ext, chans)
     at = lanes(0, width, place[1])
-    mixed[0:ext] = (d_out[...] * conv[...].astype(f32) * inside).astype(bf16).astype(f32)
-    share[...] = dot_last(short_adjoint(taps, at, mixed, ext), w_in[:, at])
-
-
-def gated_part(place, count, total, inverse, block, rim, keys, values, bias, taps, w_in, share, mixed, keep, pass_on):
+    mixed[0:ext] = (d_out[...].astype(f32) * conv[...].astype(f32) * inside).astype(bf16).astype(f32)
+    proj_query[...] = short_adjoint(taps, at, mixed, ext)
+
+
+def gated_part(
+    place, count, total, inverse, block, rim, keys, values, bias, taps, mixed, proj, w_in, part_share, share, short_share
+):
     core = place[1]
     rows, chans = block.shape
-    own, ext, width = rows // 2, rows + PAD, 2 * chans
+    ext, width = rows + PAD, 2 * chans
     inside = inside_rows(place, count, rows, ext, chans)
     bias_here = bias[0:1, lanes(0, width, core)]
     mixed[0:rows] = bias_here * block[...].astype(f32)
     mixed[rows:ext] = bias_here * rim[...].astype(f32)
     d_prod = (dot(inverse[...], total[...]) + mixed[0:ext]).astype(bf16).astype(f32) * inside
-    sums = share[...]
+    sums = part_share[...]
     for part, other in ((1, values), (2, keys)):
         at = lanes(part, width, core)
         mixed[0:ext] = (d_prod * other[...]).astype(bf16).astype(f32)
-        sums = sums + dot_last(short_adjoint(taps, at, mixed, ext), w_in[:, at])
+        proj[...] = short_adjoint(taps, at, mixed, ext)
+        sums = sums + dot_last(proj[...], w_in[:, at])
     share[...] = sums
-    keep[0:own] = share[side_rows(core, own)]
-    keep[own:] = share[rows:]
-    pass_on[0:own] = share[side_rows(1 - core, own)].astype(bf16)
-    pass_on[own:] = share[rows:].astype(bf16)
-
-
-def early(place, count, block, d_out, conv, lag_ref, table, taps, w_in, total, share, spec, mixed):
+    short_share[...] = sums.astype(bf16)
+
+
+def early(place, count, block, d_out, conv, lag_ref, table, taps, w_in, total, share, spec, mixed, proj):
     rows = block.shape[0]
     spec[...] = dot(table[:, 0:rows], block[...])
     accumulate(lag_ref, [(slot_of(place, 0, count, True), spec)], True, None, total)
-    query_part(place, count, d_out, conv, taps, w_in, mixed, share)
+    query_part(place, count, d_out, conv, taps, mixed, proj)
+    share[...] = dot_last(proj[...], w_in[:, lanes(0, w_in.shape[0], place[1])])
 
 
 def middle(place, count, ms, *refs):
@@ -239,16 +282,20 @@
     return [[(slot_of(place, m, count, adjoint), at) for m, at in pairs] for adjoint in (False, True)]
 
 
-def late(place, count, n_got, *refs):
+def late(place, count, n_got, final, *refs):
     got, refs = refs[:n_got], refs[n_got:]
-    start, part_share, block, rim, lag_ref, table, inverse, keys, values, bias, taps, w_in = refs[:12]
-    keep, pass_on, spec, total, mixed, share = refs[12:]
+    start, part_share, block, rim, lag_ref, table, inverse, keys, values, bias, taps, w_in, below_core, _ = refs[:14]
+    share, short_share, pass_on, spec, total, mixed, proj = refs[14:]
     _, pairs = late_pairs(place, count, got, spec, table)
     accumulate(lag_ref, pairs, True, start, total)
-    share[...] = part_share[...]
     gated_part(
-        place, count, total, inverse, block, rim, keys, values, bias, taps, w_in, share, mixed, keep, pass_on
-    )
+        place, count, total, inverse, block, rim, keys, values, bias, taps, mixed, proj, w_in, part_share, share,
+        short_share,
+    )
+    if final:
+        pass_on[...] = jnp.zeros(pass_on.shape, bf16)
+    else:
+        pass_half(place, short_share, below_core, pass_on)
 
 
 def early_first(place, count, block, product, lag_ref, table, total, total_conv, spec):
@@ -270,17 +317,19 @@
 
 def late_first(place, count, n_got, *refs):
     got, refs = refs[:n_got], refs[n_got:]
-    start, start_conv, d_out, product, block, rim, lag_ref, table, inverse, keys, values, bias, taps, w_in = refs[:14]
-    keep, pass_on, conv, spec, total, mixed, share = refs[14:]
+    start, start_conv, d_out, product, block, rim, lag_ref, table, inverse = refs[:9]
+    keys, values, bias, taps, w_in, _ = refs[9:15]
+    share, short_share, conv, spec, total, mixed, proj = refs[15:]
     width = 2 * block.shape[1]
     pairs_conv, pairs = late_pairs(place, count, got, spec, table)
     accumulate(lag_ref, pairs_conv, False, start_conv, total)
     whole = dot(inverse[...], total[...]) + bias[0:1, lanes(0, width, place[1])] * product[...].astype(f32)
     conv[...] = whole.astype(bf16)
-    query_part(place, count, d_out, conv, taps, w_in, mixed, share)
+    query_part(place, count, d_out, conv, taps, mixed, proj)
+    share[...] = dot_last(proj[...], w_in[:, lanes(0, width, place[1])])
     accumulate(lag_ref, pairs, True, start, total)
     gated_part(
-        place, count, total, inverse, block, rim, keys, values, bias, taps, w_in, share, mixed, keep, pass_on
+        place, count, total, inverse, block, rim, keys, values, bias, taps, mixed, proj, w_in, share, share, short_share
     )
 
 
@@ -291,7 +340,6 @@
     section_place = lax.axis_index("section")
     chips = seq_count // 2
     core = seq_place % 2
-    place = jnp.stack([seq_place // 2, core]).astype(jnp.int32)
     own_rows = projected.shape[2]
     rows = 2 * own_rows
     width = w_out.shape[2]
@@ -321,7 +369,7 @@
         return jax.ShapeDtypeStruct((n, across), kind)
 
     def run(body, outs, scratch, name, micros, *operands):
-        return call(body, outs, scratch, name, limit, micros, place, *operands)
+        return call(body, outs, scratch, name, limit, micros, *operands)
 
     stored, grad = projected[0, 0], cotangent[0]
     lags_own, lags_other = run(
@@ -356,26 +404,34 @@
         *pieces, lag_table,
     )
 
+    weight_half = lax.dynamic_slice_in_dim(weight_out, core * chans, chans, 0)
+    below = lax.ppermute(
+        weight_half, "section", [(s, (s + 1) % section_count) for s in range(section_count)]
+    )
+    below_core = swap_core(below)
+
     spec = pltpu.VMEM((2 * ext, chans), f32)
     total_wide = shape(2 * ext, f32)
     total_scratch = pltpu.VMEM((2 * ext, chans), bf16)
     mixed = pltpu.VMEM((ext + PAD, chans), f32)
-    share = pltpu.VMEM((ext, width), f32)
     ms = list(range(1, chips // 2))
     specs = pltpu.VMEM((len(ms), 2 * ext, chans), f32)
     late_specs = pltpu.VMEM((chips - 1 - len(ms), 2 * ext, chans), f32)
+    gates = [shape(rows, bf16), shape(own_rows, bf16), shape(own_rows, bf16), shape(PAD, bf16)]
+    proj = pltpu.VMEM((ext, chans), bf16)
+    late_outs = [shape(ext, f32, width), shape(ext, bf16, width)]
     ends = [shape(own_rows + PAD, f32, width), shape(own_rows + PAD, bf16, width)]
     result = jnp.zeros((own_rows, width), bf16)
-    conv = None
+    conv = d_out = ready = None
     for turn in range(section_count):
-        first = turn == 0
-        block, upper_half, lower_half, rim, d_out = run(
-            gate_grad,
-            [shape(rows, bf16), shape(own_rows, bf16), shape(own_rows, bf16), shape(PAD, bf16), shape(ext, f32)],
-            [],
-            "gate_grad", 1.0,
-            grad, grad_core if first else swap_core(grad), weight_out, query,
-        )
+        first, final = turn == 0, turn == section_count - 1
+        upper = section_count - 1 - turn
+        if first:
+            block, upper_half, lower_half, rim, d_out = run(
+                gate_grad, gates + [shape(ext, f32)], [], "gate_grad", 1.0, grad, grad_core, weight_out, query
+            )
+        else:
+            block, upper_half, lower_half, rim = run(gate_only, gates, [], "gate_only", 0.3, d_out, query, ready)
 
         def send(value, at, m):
             if first:
@@ -386,41 +442,54 @@
         got.append(send(upper_half, slice(0, own_rows), chips - 1))
         got.append(send(lower_half, slice(own_rows, rows), chips - 1))
         soon, last = got[: len(ms)], got[len(ms) :]
+        if not first:
+            grad_core = swap_core(grad)
         if first:
             start, start_conv = run(
                 lambda place, *refs: early_first(place, chips, *refs),
                 [total_wide, total_wide], [spec], "early_first", 1.8, block, product, spectra, table,
             )
+            carried = run(carry_grad, shape(ext, f32), [], "carry_grad", 1.0, grad, grad_core, below, start)
             start, start_conv = run(
                 lambda place, *refs: middle_first(place, chips, ms, *refs),
                 [total_wide, total_wide], [specs], "middle_first", 1.0, *soon, start, start_conv, spectra, table,
             )
-            keep, pass_on, conv = run(
+            share, short_share, conv = run(
                 lambda place, *refs: late_first(place, chips, len(last), *refs),
-                ends + [shape(ext, bf16)], [late_specs, total_scratch, mixed, share], "late_first", 4.0,
+                late_outs + [shape(ext, bf16)], [late_specs, total_scratch, mixed, proj], "late_first", 4.0,
                 *last, start, start_conv, d_out, product, block, rim, spectra, table, inverse, keys, values, bias,
-                taps, weight_in,
-            )
+                taps, weight_in, carried,
+            )
+            pass_on = run(pass_half, shape(ext, bf16), [], "pass_half", 0.5, short_share, below_core)
         else:
             start, part_share = run(
                 lambda place, *refs: early(place, chips, *refs),
-                [total_wide, shape(ext, f32, width)], [spec, mixed], "early", 1.6,
+                [total_wide, shape(ext, f32, width)], [spec, mixed, proj], "early", 1.6,
                 block, d_out, conv, spectra, table, taps, weight_in,
             )
             start = run(
                 lambda place, *refs: middle(place, chips, ms, *refs),
                 total_wide, [specs], "middle", 0.8, *soon, start, spectra, table,
             )
-            keep, pass_on = run(
-                lambda place, *refs: late(place, chips, len(last), *refs),
-                ends, [late_specs, total_scratch, mixed, share], "late", 3.0,
+            carried = start
+            if not final:
+                carried = run(carry_grad, shape(ext, f32), [], "carry_grad", 1.0, grad, grad_core, below, start)
+            share, short_share, pass_on = run(
+                lambda place, *refs, final=final: late(place, chips, len(last), final, *refs),
+                late_outs + [shape(ext, bf16)], [late_specs, total_scratch, mixed, proj], "late", 2.5,
                 *last, start, part_share, block, rim, spectra, table, inverse, keys, values, bias, taps, weight_in,
-            )
-        summed = (grad.astype(f32) + keep + swap_core(pass_on).astype(f32)).astype(bf16)
-        upper = section_count - 1 - turn
-        result = jnp.where(section_place == upper, summed[:own_rows], result)
-        if turn < section_count - 1:
-            grad = swap_section(summed, upper)
+                below_core, carried,
+            )
+        half = pass_on
+        if not final:
+            keep = run(keep_half, shape(ext, f32), [], "keep_half", 0.6, short_share, below, carried)
+            half = (keep + swap_core(pass_on).astype(f32)).astype(bf16)
+            d_out = swap_section(half, upper)
+        keep_rows, pass_rows = run(split_rows, ends, [], "split_rows", 0.3, share, half)
+        ready = (grad.astype(f32) + keep_rows + swap_core(pass_rows).astype(f32)).astype(bf16)
+        result = jnp.where(section_place == upper, ready[:own_rows], result)
+        if not final:
+            grad = swap_section(ready, upper)
     return result[None, None]
 
 

time: 119 us -> 112 us (0.941)
  Pallas kernels: 33.8 us -> 27.8 us
  waiting for transfers between devices: 40.4 us -> 36.8 us
    pallas_call x20 -> x31, Pallas kernels: 33.8 us -> 27.8 us  [call(): pl.pallas_call(placed, out_shape=outs, in_specs=[vmem] * len(operands), o...]
    ppermute x11 -> x14, waiting for transfers between devices: 11.2 us -> 6.84 us  [swap_core(): return lax.ppermute(value, 'seq', [(i, i ^ 1) for i in range(seq_count)])]
    ppermute x0 -> x1, waiting for transfers between devices: none -> 3.96 us  [shards(): lax.ppermute(weight_half, 'section', [(s, (s + 1) % section_count) for s...]
    ppermute x19, waiting for transfers between devices: 14.4 us -> 12.4 us  [swap_chip(): lax.ppermute(value, 'seq', [(i, (i // 2 ^ m) * 2 + i % 2) for i in range(...]
    ppermute x19, starting transfers between devices: 25.6 us -> 23.9 us  [swap_chip(): lax.ppermute(value, 'seq', [(i, (i // 2 ^ m) * 2 + i % 2) for i in range(...]
    ppermute x3 -> x6, waiting for transfers between devices: 12.9 us -> 11.3 us  [swap_section(): return lax.ppermute(value, ('seq', 'section'), pairs)]
    ppermute x0 -> x1, starting transfers between devices: none -> 1.58 us  [shards(): lax.ppermute(weight_half, 'section', [(s, (s + 1) % section_count) for s...]
    ppermute x3 -> x6, starting transfers between devices: 9.53 us -> 10.1 us  [swap_section(): return lax.ppermute(value, ('seq', 'section'), pairs)]
  transfers between devices with their start and end apart: 34 -> 41, of which waited for: 24 -> 23; matrix products, arithmetic and copies ran while one was open for 0% -> 0% of each run, Pallas kernels for 14% -> 19%
where the time goes in v3:
time: 112 us; the launch traced here: 111 us
  starting transfers between devices  41.3 us (37%)
  waiting for transfers between devices  36.8 us (33%)
  Pallas kernels  27.8 us (25%)
  local copies, waits for them, and re-layouts  3.65 us (3%)
  other arithmetic  1.35 us (1%)
    pallas_call x31, Pallas kernels, call(): pl.pallas_call(placed, out_shape=outs, in_specs=[vmem] * len(operands), o...  27.8 us
    ppermute x19, starting transfers between devices, swap_chip(): lax.ppermute(value, 'seq', [(i, (i // 2 ^ m) * 2 + i % 2) for i in range(...  23.9 us
    ppermute x19, waiting for transfers between devices, swap_chip(): lax.ppermute(value, 'seq', [(i, (i // 2 ^ m) * 2 + i % 2) for i in range(...  12.4 us
    ppermute x6, waiting for transfers between devices, swap_section(): return lax.ppermute(value, ('seq', 'section'), pairs)  11.3 us
    ppermute x6, starting transfers between devices, swap_section(): return lax.ppermute(value, ('seq', 'section'), pairs)  10.1 us
    ppermute x14, waiting for transfers between devices, swap_core(): return lax.ppermute(value, 'seq', [(i, i ^ 1) for i in range(seq_count)])  6.84 us
    ppermute x1, waiting for transfers between devices, shards(): lax.ppermute(weight_half, 'section', [(s, (s + 1) % section_count) for s...  3.96 us
    unnamed x24, local copies, waits for them, and re-layouts  3.61 us
  transfers between devices with their start and end apart: 41, of which 23 were waited for; matrix products, arithmetic and copies ran while one was open for 0% of the time, Pallas kernels for 19%

profile of v3, /device:TPU:0, one launch (start us, length us, event | category | flops | bytes accessed | tf_op | source)
XLA Modules:
  0.0 111.3 jit_solution(770780008067756269)
XLA Ops:
  4.3 3.6 %collective-permute-start.1 = (bf16[16,3072]{1,0:T(8,128)(2,1)}, bf16[16,3072]{1,0:T(8,128)(2,1)}, u32[]{:S(2)}, u32[]{:S(2)}) collective-permute-start(bf16[16,3072]{1,0:T(8,128)(2,1)} %get-tuple-element.62), channel_id=1, source_target_pairs={{4,8},{12,16},{20,24},{28,0},{8,4},{16,12},{24,20},{0,28},{5,9},{1... | collective-permute-start | bytes 294920 | tf_op jit(solution)/shard_map/ppermute | solution.py:384
  9.1 2.3 %collective-permute-done.1.refs_2_ = bf16[16,3072]{1,0:T(8,128)(2,1)} collective-permute-done((bf16[16,3072]{1,0:T(8,128)(2,1)}, bf16[16,3072]{1,0:T(8,128)(2,1)}, u32[]{:S(2)}, u32[]{:S(2)}) %collective-permute-start.1) | collective-permute-done | bytes 98336 | tf_op jit(solution)/shard_map/ppermute | solution.py:384
  12.9 1.6 %collective-permute-start.12 = (bf16[384,768]{1,0:T(8,128)(2,1)S(1)}, bf16[384,768]{1,0:T(8,128)(2,1)S(1)}, u32[]{:S(2)}, u32[]{:S(2)}) collective-permute-start(bf16[384,768]{1,0:T(8,128)(2,1)S(1)} %dynamic-slice_bitcast_fusion), channel_id=1, source_target_pairs={{0,1},{1,2},{2,3},{3,0},{4,5},{5,6},{6,7},{7,4},{8,9},{9,10},{10,1... | collective-permute-start | bytes 1769480 | tf_op jit(solution)/shard_map/ppermute | solution.py:408
  15.3 2.0 %collective-permute-start.11 = (bf16[256,384]{1,0:T(8,128)(2,1)S(1)}, bf16[256,384]{1,0:T(8,128)(2,1)S(1)}, u32[]{:S(2)}, u32[]{:S(2)}) collective-permute-start(bf16[256,384]{1,0:T(8,128)(2,1)S(1)} %maximum_select_fusion.refs_0_), channel_id=1, source_target_pairs={{0,24},{4,28},{8,16},{12,20},{16,8},{20,12},{24,0},{28,4},{1,25},{... | collective-permute-start | bytes 589832 | tf_op jit(solution)/shard_map/ppermute | solution.py:357
  17.3 1.7 %mix_stored.1 = (f32[272,384]{1,0:T(8,128)S(1)}, f32[272,384]{1,0:T(8,128)S(1)}, f32[272,384]{1,0:T(8,128)S(1)}, bf16[272,384]{1,0:T(8,128)(2,1)S(1)}, bf16[144,768]{1,0:T(8,128)(2,1)S(1)}) custom-call(bf16[128,2304]{1,0:T(8,128)(2,1)S(1)} %bitcast.27, bf16[128,1152]{1,0:T(8,128)(2,1)S(1)} %collective-permute-done.refs_1_, ...), custom_call_target="tpu_custom_call" | custom-call | flops 1300000000 | tf_op jit(solution)/shard_map/mix_stored/pallas_call | solution.py:57
  20.2 2.0 %collective-permute-start.8 = (bf16[128,384]{1,0:T(8,128)(2,1)S(1)}, bf16[128,384]{1,0:T(8,128)(2,1)S(1)}, u32[]{:S(2)}, u32[]{:S(2)}) collective-permute-start(bf16[128,384]{1,0:T(8,128)(2,1)S(1)} %get-tuple-element.118), channel_id=1, source_target_pairs={{0,24},{4,28},{8,16},{12,20},{16,8},{20,12},{24,0},{28,4},{1,25},{... | collective-permute-start | bytes 294920 | tf_op jit(solution)/shard_map/ppermute | solution.py:357
  24.3 1.9 %lag_spectra.1.refs_2_.refs_3_.refs_9_.refs_7_ = f32[5,544,384]{2,1,0:T(8,128)S(1)} custom-call(bf16[256,384]{1,0:T(8,128)(2,1)S(1)} %maximum_select_fusion.refs_0_, bf16[256,384]{1,0:T(8,128)(2,1)S(1)} %collective-permute-done.4.refs_6_.refs_1_, bf16[256,384]{1,0:T(8,128)(2,1)S(1)} %collective-permute-done.5.refs_7_.refs_2_, ...), custom_call_target="tpu_custom_call" | custom-call | flops 2400000000 | tf_op jit(solution)/shard_map/lag_spectra/pallas_call | solution.py:57
  26.2 4.0 %collective-permute-done.12.refs_2_.refs_1_ = bf16[384,768]{1,0:T(8,128)(2,1)S(1)} collective-permute-done((bf16[384,768]{1,0:T(8,128)(2,1)S(1)}, bf16[384,768]{1,0:T(8,128)(2,1)S(1)}, u32[]{:S(2)}, u32[]{:S(2)}) %collective-permute-start.12) | collective-permute-done | bytes 589856 | tf_op jit(solution)/shard_map/ppermute | solution.py:408
  33.6 3.7 %late_first.1 = (f32[272,768]{1,0:T(8,128)S(1)}, bf16[272,768]{1,0:T(8,128)(2,1)S(1)}, bf16[272,384]{1,0:T(8,128)(2,1)S(1)}) custom-call(bf16[256,384]{1,0:T(8,128)(2,1)S(1)} %collective-permute-done.7.refs_0_, bf16[128,384]{1,0:T(8,128)(2,1)S(1)} %collective-permute-done.8.refs_1_, bf16[128,384]{1,0:T(8,128)(2,1)S(1)} %collective-permute-done.9.refs_2_, ...), custom_call_target="tpu_custom_call" | custom-call | flops 4000000000 | tf_op jit(solution)/shard_map/late_first/pallas_call | solution.py:57
  42.2 5.6 %collective-permute-done.17.refs_0_.refs_1_ = bf16[272,384]{1,0:T(8,128)(2,1)S(1)} collective-permute-done((bf16[272,384]{1,0:T(8,128)(2,1)S(1)}, bf16[272,384]{1,0:T(8,128)(2,1)S(1)}, u32[]{:S(2)}, u32[]{:S(2)}) %collective-permute-start.17) | collective-permute-done | bytes 208928 | tf_op jit(solution)/shard_map/ppermute | solution.py:366
  47.9 2.1 %collective-permute-start.21 = (bf16[256,384]{1,0:T(8,128)(2,1)S(1)}, bf16[256,384]{1,0:T(8,128)(2,1)S(1)}, u32[]{:S(2)}, u32[]{:S(2)}) collective-permute-start(bf16[256,384]{1,0:T(8,128)(2,1)S(1)} %get-tuple-element.82.refs_0_.refs_5_), channel_id=1, source_target_pairs={{0,8},{4,12},{8,0},{12,4},{16,24},{20,28},{24,16},{28,20},{1,9},{5... | collective-permute-start | bytes 589832 | tf_op jit(solution)/shard_map/ppermute | solution.py:357
  50.0 1.6 %collective-permute-start.18 = (bf16[256,384]{1,0:T(8,128)(2,1)S(1)}, bf16[256,384]{1,0:T(8,128)(2,1)S(1)}, u32[]{:S(2)}, u32[]{:S(2)}) collective-permute-start(bf16[256,384]{1,0:T(8,128)(2,1)S(1)} %get-tuple-element.82.refs_0_.refs_5_), channel_id=1, source_target_pairs={{0,16},{4,20},{8,24},{12,28},{16,0},{20,4},{24,8},{28,12},{1,17},{... | collective-permute-start | bytes 589832 | tf_op jit(solution)/shard_map/ppermute | solution.py:357
  51.6 2.9 %collective-permute-start.20 = (bf16[128,384]{1,0:T(8,128)(2,1)S(1)}, bf16[128,384]{1,0:T(8,128)(2,1)S(1)}, u32[]{:S(2)}, u32[]{:S(2)}) collective-permute-start(bf16[128,384]{1,0:T(8,128)(2,1)S(1)} %get-tuple-element.84), channel_id=1, source_target_pairs={{0,24},{4,28},{8,16},{12,20},{16,8},{20,12},{24,0},{28,4},{1,25},{... | collective-permute-start | bytes 294920 | tf_op jit(solution)/shard_map/ppermute | solution.py:357
  59.6 2.7 %late.3 = (f32[272,768]{1,0:T(8,128)S(1)}, bf16[272,768]{1,0:T(8,128)(2,1)S(1)}, bf16[272,384]{1,0:T(8,128)(2,1)S(1)}) custom-call(bf16[256,384]{1,0:T(8,128)(2,1)S(1)} %collective-permute-done.18.refs_0_, bf16[128,384]{1,0:T(8,128)(2,1)S(1)} %collective-permute-done.19.refs_1_, bf16[128,384]{1,0:T(8,128)(2,1)S(1)} %collective-permute-done.20.refs_2_, ...), custom_call_target="tpu_custom_call" | custom-call | flops 2500000000 | tf_op jit(solution)/shard_map/late/pallas_call | solution.py:57
  67.5 1.9 %collective-permute-start.28 = (bf16[128,384]{1,0:T(8,128)(2,1)S(1)}, bf16[128,384]{1,0:T(8,128)(2,1)S(1)}, u32[]{:S(2)}, u32[]{:S(2)}) collective-permute-start(bf16[128,384]{1,0:T(8,128)(2,1)S(1)} %get-tuple-element.95), channel_id=1, source_target_pairs={{0,24},{4,28},{8,16},{12,20},{16,8},{20,12},{24,0},{28,4},{1,25},{... | collective-permute-start | bytes 294920 | tf_op jit(solution)/shard_map/ppermute | solution.py:357
  71.5 2.1 %collective-permute-done.30.refs_0_ = bf16[256,384]{1,0:T(8,128)(2,1)S(1)} collective-permute-done((bf16[256,384]{1,0:T(8,128)(2,1)S(1)}, bf16[256,384]{1,0:T(8,128)(2,1)S(1)}, u32[]{:S(2)}, u32[]{:S(2)}) %collective-permute-start.30) | collective-permute-done | bytes 196640 | tf_op jit(solution)/shard_map/ppermute | solution.py:357
  74.7 1.7 %collective-permute-done.28.refs_1_ = bf16[128,384]{1,0:T(8,128)(2,1)S(1)} collective-permute-done((bf16[128,384]{1,0:T(8,128)(2,1)S(1)}, bf16[128,384]{1,0:T(8,128)(2,1)S(1)}, u32[]{:S(2)}, u32[]{:S(2)}) %collective-permute-start.28) | collective-permute-done | bytes 98336 | tf_op jit(solution)/shard_map/ppermute | solution.py:357
  76.4 1.5 %collective-permute-done.29.refs_2_ = bf16[128,384]{1,0:T(8,128)(2,1)S(1)} collective-permute-done((bf16[128,384]{1,0:T(8,128)(2,1)S(1)}, bf16[128,384]{1,0:T(8,128)(2,1)S(1)}, u32[]{:S(2)}, u32[]{:S(2)}) %collective-permute-start.29) | collective-permute-done | bytes 98336 | tf_op jit(solution)/shard_map/ppermute | solution.py:357
  78.0 2.9 %late.4 = (f32[272,768]{1,0:T(8,128)S(1)}, bf16[272,768]{1,0:T(8,128)(2,1)S(1)}, bf16[272,384]{1,0:T(8,128)(2,1)S(1)}) custom-call(bf16[256,384]{1,0:T(8,128)(2,1)S(1)} %collective-permute-done.27.refs_0_, bf16[128,384]{1,0:T(8,128)(2,1)S(1)} %collective-permute-done.28.refs_1_, bf16[128,384]{1,0:T(8,128)(2,1)S(1)} %collective-permute-done.29.refs_2_, ...), custom_call_target="tpu_custom_call" | custom-call | flops 2500000000 | tf_op jit(solution)/shard_map/late/pallas_call | solution.py:57
  82.7 5.7 %collective-permute-start.35 = (bf16[272,384]{1,0:T(8,128)(2,1)S(1)}, bf16[272,384]{1,0:T(8,128)(2,1)S(1)}, u32[]{:S(2)}, u32[]{:S(2)}) collective-permute-start(bf16[272,384]{1,0:T(8,128)(2,1)S(1)} %add_convert_fusion.3.refs_1_), channel_id=1, source_target_pairs={{0,1},{1,0},{2,3},{3,2},{4,5},{5,4},{6,7},{7,6},{8,9},{9,8},{10,11... | collective-permute-start | bytes 626696 | tf_op jit(solution)/shard_map/ppermute | solution.py:366
  88.5 5.6 %collective-permute-done.35.refs_0_.refs_1_ = bf16[272,384]{1,0:T(8,128)(2,1)S(1)} collective-permute-done((bf16[272,384]{1,0:T(8,128)(2,1)S(1)}, bf16[272,384]{1,0:T(8,128)(2,1)S(1)}, u32[]{:S(2)}, u32[]{:S(2)}) %collective-permute-start.35) | collective-permute-done | bytes 208928 | tf_op jit(solution)/shard_map/ppermute | solution.py:366
  96.4 1.7 %collective-permute-start.34 = (bf16[144,768]{1,0:T(8,128)(2,1)S(1)}, bf16[144,768]{1,0:T(8,128)(2,1)S(1)}, u32[]{:S(2)}, u32[]{:S(2)}) collective-permute-start(bf16[144,768]{1,0:T(8,128)(2,1)S(1)} %add_convert_fusion.refs_2_), channel_id=1, source_target_pairs={{0,1},{1,0},{2,3},{3,2},{4,5},{5,4},{6,7},{7,6},{8,9},{9,8},{10,11... | collective-permute-start | bytes 663560 | tf_op jit(solution)/shard_map/ppermute | solution.py:366
  99.5 1.6 %collective-permute-start.38 = (bf16[128,384]{1,0:T(8,128)(2,1)S(1)}, bf16[128,384]{1,0:T(8,128)(2,1)S(1)}, u32[]{:S(2)}, u32[]{:S(2)}) collective-permute-start(bf16[128,384]{1,0:T(8,128)(2,1)S(1)} %get-tuple-element.107), channel_id=1, source_target_pairs={{0,24},{4,28},{8,16},{12,20},{16,8},{20,12},{24,0},{28,4},{1,25},{... | collective-permute-start | bytes 294920 | tf_op jit(solution)/shard_map/ppermute | solution.py:357
  105.7 3.2 %late.5 = (f32[272,768]{1,0:T(8,128)S(1)}, bf16[272,768]{1,0:T(8,128)(2,1)}, bf16[272,384]{1,0:T(8,128)(2,1)S(1)}) custom-call(bf16[256,384]{1,0:T(8,128)(2,1)S(1)} %collective-permute-done.36.refs_0_, bf16[128,384]{1,0:T(8,128)(2,1)S(1)} %collective-permute-done.37.refs_1_, bf16[128,384]{1,0:T(8,128)(2,1)S(1)} %collective-permute-done.38.refs_2_, ...), custom_call_target="tpu_custom_call" | custom-call | flops 2500000000 | tf_op jit(solution)/shard_map/late/pallas_call | solution.py:57
  (124 shorter events, 45.4 us)
Async XLA Ops:
  7.9 9.5 %collective-permute-start = (bf16[128,1152]{1,0:T(8,128)(2,1)S(1)}, bf16[128,1152]{1,0:T(8,128)(2,1)S(1)}, u32[]{:S(2)}, u32[]{:S(2)}) collective-permute-start(bf16[128,1152]{1,0:T(8,128)(2,1)S(1)} %get-tuple-element.61), channel_id=1, source_target_pairs={{0,4},{4,0},{8,12},{12,8},{16,20},{20,16},{24,28},{28,24},{1,5},{5... | collective-permute-start | bytes 884744 | tf_op jit(solution)/shard_map/ppermute | solution.py:354
  7.9 7.4 %collective-permute-start.4 = (bf16[256,384]{1,0:T(8,128)(2,1)S(1)}, bf16[256,384]{1,0:T(8,128)(2,1)S(1)}, u32[]{:S(2)}, u32[]{:S(2)}) collective-permute-start(bf16[256,384]{1,0:T(8,128)(2,1)S(1)} %maximum_select_fusion.refs_0_), channel_id=1, source_target_pairs={{0,8},{4,12},{8,0},{12,4},{16,24},{20,28},{24,16},{28,20},{1,9},{5... | collective-permute-start | bytes 589832 | tf_op jit(solution)/shard_map/ppermute | solution.py:357
  8.5 8.8 %collective-permute-start.5 = (bf16[256,384]{1,0:T(8,128)(2,1)S(1)}, bf16[256,384]{1,0:T(8,128)(2,1)S(1)}, u32[]{:S(2)}, u32[]{:S(2)}) collective-permute-start(bf16[256,384]{1,0:T(8,128)(2,1)S(1)} %maximum_select_fusion.refs_0_), channel_id=1, source_target_pairs={{0,16},{4,20},{8,24},{12,28},{16,0},{20,4},{24,8},{28,12},{1,17},{... | collective-permute-start | bytes 589832 | tf_op jit(solution)/shard_map/ppermute | solution.py:357
  9.1 9.9 %collective-permute-start.6 = (bf16[128,768]{1,0:T(8,128)(2,1)S(1)}, bf16[128,768]{1,0:T(8,128)(2,1)S(1)}, u32[]{:S(2)}, u32[]{:S(2)}) collective-permute-start(bf16[128,768]{1,0:T(8,128)(2,1)S(1)} %bitcast.30), channel_id=1, source_target_pairs={{0,4},{4,0},{8,12},{12,8},{16,20},{20,16},{24,28},{28,24},{1,5},{5... | collective-permute-start | bytes 589832 | tf_op jit(solution)/shard_map/ppermute | solution.py:354
  12.9 17.2 %collective-permute-start.12 = (bf16[384,768]{1,0:T(8,128)(2,1)S(1)}, bf16[384,768]{1,0:T(8,128)(2,1)S(1)}, u32[]{:S(2)}, u32[]{:S(2)}) collective-permute-start(bf16[384,768]{1,0:T(8,128)(2,1)S(1)} %dynamic-slice_bitcast_fusion), channel_id=1, source_target_pairs={{0,1},{1,2},{2,3},{3,0},{4,5},{5,6},{6,7},{7,4},{8,9},{9,10},{10,1... | collective-permute-start | bytes 1769480 | tf_op jit(solution)/shard_map/ppermute | solution.py:408
  15.3 8.1 %collective-permute-start.11 = (bf16[256,384]{1,0:T(8,128)(2,1)S(1)}, bf16[256,384]{1,0:T(8,128)(2,1)S(1)}, u32[]{:S(2)}, u32[]{:S(2)}) collective-permute-start(bf16[256,384]{1,0:T(8,128)(2,1)S(1)} %maximum_select_fusion.refs_0_), channel_id=1, source_target_pairs={{0,24},{4,28},{8,16},{12,20},{16,8},{20,12},{24,0},{28,4},{1,25},{... | collective-permute-start | bytes 589832 | tf_op jit(solution)/shard_map/ppermute | solution.py:357
  19.7 11.8 %collective-permute-start.10 = (bf16[256,384]{1,0:T(8,128)(2,1)S(1)}, bf16[256,384]{1,0:T(8,128)(2,1)S(1)}, u32[]{:S(2)}, u32[]{:S(2)}) collective-permute-start(bf16[256,384]{1,0:T(8,128)(2,1)S(1)} %get-tuple-element.115), channel_id=1, source_target_pairs={{0,8},{4,12},{8,0},{12,4},{16,24},{20,28},{24,16},{28,20},{1,9},{5... | collective-permute-start | bytes 589832 | tf_op jit(solution)/shard_map/ppermute | solution.py:357
  20.2 12.7 %collective-permute-start.8 = (bf16[128,384]{1,0:T(8,128)(2,1)S(1)}, bf16[128,384]{1,0:T(8,128)(2,1)S(1)}, u32[]{:S(2)}, u32[]{:S(2)}) collective-permute-start(bf16[128,384]{1,0:T(8,128)(2,1)S(1)} %get-tuple-element.118), channel_id=1, source_target_pairs={{0,24},{4,28},{8,16},{12,20},{16,8},{20,12},{24,0},{28,4},{1,25},{... | collective-permute-start | bytes 294920 | tf_op jit(solution)/shard_map/ppermute | solution.py:357
  22.1 10.8 %collective-permute-start.9 = (bf16[128,384]{1,0:T(8,128)(2,1)S(1)}, bf16[128,384]{1,0:T(8,128)(2,1)S(1)}, u32[]{:S(2)}, u32[]{:S(2)}) collective-permute-start(bf16[128,384]{1,0:T(8,128)(2,1)S(1)} %get-tuple-element.117), channel_id=1, source_target_pairs={{0,24},{4,28},{8,16},{12,20},{16,8},{20,12},{24,0},{28,4},{1,25},{... | collective-permute-start | bytes 294920 | tf_op jit(solution)/shard_map/ppermute | solution.py:357
  23.4 9.7 %collective-permute-start.7 = (bf16[256,384]{1,0:T(8,128)(2,1)S(1)}, bf16[256,384]{1,0:T(8,128)(2,1)S(1)}, u32[]{:S(2)}, u32[]{:S(2)}) collective-permute-start(bf16[256,384]{1,0:T(8,128)(2,1)S(1)} %get-tuple-element.116), channel_id=1, source_target_pairs={{0,16},{4,20},{8,24},{12,28},{16,0},{20,4},{24,8},{28,12},{1,17},{... | collective-permute-start | bytes 589832 | tf_op jit(solution)/shard_map/ppermute | solution.py:357
  30.1 7.1 %collective-permute-start.13 = (bf16[384,768]{1,0:T(8,128)(2,1)S(1)}, bf16[384,768]{1,0:T(8,128)(2,1)S(1)}, u32[]{:S(2)}, u32[]{:S(2)}) collective-permute-start(bf16[384,768]{1,0:T(8,128)(2,1)S(1)} %collective-permute-done.12.refs_2_.refs_1_), channel_id=1, source_target_pairs={{0,4},{4,0},{8,12},{12,8},{16,20},{20,16},{24,28},{28,24},{1,5},{5... | collective-permute-start | bytes 1769480 | tf_op jit(solution)/shard_map/ppermute | solution.py:354
  39.9 8.0 %collective-permute-start.17 = (bf16[272,384]{1,0:T(8,128)(2,1)S(1)}, bf16[272,384]{1,0:T(8,128)(2,1)S(1)}, u32[]{:S(2)}, u32[]{:S(2)}) collective-permute-start(bf16[272,384]{1,0:T(8,128)(2,1)S(1)} %add_convert_fusion.5.refs_1_), channel_id=1, source_target_pairs={{0,1},{1,0},{2,3},{3,2},{4,5},{5,4},{6,7},{7,6},{8,9},{9,8},{10,11... | collective-permute-start | bytes 626696 | tf_op jit(solution)/shard_map/ppermute | solution.py:366
  41.1 13.5 %collective-permute-start.16 = (bf16[144,768]{1,0:T(8,128)(2,1)S(1)}, bf16[144,768]{1,0:T(8,128)(2,1)S(1)}, u32[]{:S(2)}, u32[]{:S(2)}) collective-permute-start(bf16[144,768]{1,0:T(8,128)(2,1)S(1)} %add_convert_fusion.2.refs_2_), channel_id=1, source_target_pairs={{0,1},{1,0},{2,3},{3,2},{4,5},{5,4},{6,7},{7,6},{8,9},{9,8},{10,11... | collective-permute-start | bytes 663560 | tf_op jit(solution)/shard_map/ppermute | solution.py:366
  47.9 7.7 %collective-permute-start.21 = (bf16[256,384]{1,0:T(8,128)(2,1)S(1)}, bf16[256,384]{1,0:T(8,128)(2,1)S(1)}, u32[]{:S(2)}, u32[]{:S(2)}) collective-permute-start(bf16[256,384]{1,0:T(8,128)(2,1)S(1)} %get-tuple-element.82.refs_0_.refs_5_), channel_id=1, source_target_pairs={{0,8},{4,12},{8,0},{12,4},{16,24},{20,28},{24,16},{28,20},{1,9},{5... | collective-permute-start | bytes 589832 | tf_op jit(solution)/shard_map/ppermute | solution.py:357
  50.0 9.6 %collective-permute-start.18 = (bf16[256,384]{1,0:T(8,128)(2,1)S(1)}, bf16[256,384]{1,0:T(8,128)(2,1)S(1)}, u32[]{:S(2)}, u32[]{:S(2)}) collective-permute-start(bf16[256,384]{1,0:T(8,128)(2,1)S(1)} %get-tuple-element.82.refs_0_.refs_5_), channel_id=1, source_target_pairs={{0,16},{4,20},{8,24},{12,28},{16,0},{20,4},{24,8},{28,12},{1,17},{... | collective-permute-start | bytes 589832 | tf_op jit(solution)/shard_map/ppermute | solution.py:357
  51.6 7.4 %collective-permute-start.20 = (bf16[128,384]{1,0:T(8,128)(2,1)S(1)}, bf16[128,384]{1,0:T(8,128)(2,1)S(1)}, u32[]{:S(2)}, u32[]{:S(2)}) collective-permute-start(bf16[128,384]{1,0:T(8,128)(2,1)S(1)} %get-tuple-element.84), channel_id=1, source_target_pairs={{0,24},{4,28},{8,16},{12,20},{16,8},{20,12},{24,0},{28,4},{1,25},{... | collective-permute-start | bytes 294920 | tf_op jit(solution)/shard_map/ppermute | solution.py:357
  65.8 7.8 %collective-permute-start.30 = (bf16[256,384]{1,0:T(8,128)(2,1)S(1)}, bf16[256,384]{1,0:T(8,128)(2,1)S(1)}, u32[]{:S(2)}, u32[]{:S(2)}) collective-permute-start(bf16[256,384]{1,0:T(8,128)(2,1)S(1)} %get-tuple-element.94.refs_0_.refs_5_), channel_id=1, source_target_pairs={{0,8},{4,12},{8,0},{12,4},{16,24},{20,28},{24,16},{28,20},{1,9},{5... | collective-permute-start | bytes 589832 | tf_op jit(solution)/shard_map/ppermute | solution.py:357
  66.9 11.1 %collective-permute-start.27 = (bf16[256,384]{1,0:T(8,128)(2,1)S(1)}, bf16[256,384]{1,0:T(8,128)(2,1)S(1)}, u32[]{:S(2)}, u32[]{:S(2)}) collective-permute-start(bf16[256,384]{1,0:T(8,128)(2,1)S(1)} %get-tuple-element.94.refs_0_.refs_5_), channel_id=1, source_target_pairs={{0,16},{4,20},{8,24},{12,28},{16,0},{20,4},{24,8},{28,12},{1,17},{... | collective-permute-start | bytes 589832 | tf_op jit(solution)/shard_map/ppermute | solution.py:357
  67.5 8.9 %collective-permute-start.28 = (bf16[128,384]{1,0:T(8,128)(2,1)S(1)}, bf16[128,384]{1,0:T(8,128)(2,1)S(1)}, u32[]{:S(2)}, u32[]{:S(2)}) collective-permute-start(bf16[128,384]{1,0:T(8,128)(2,1)S(1)} %get-tuple-element.95), channel_id=1, source_target_pairs={{0,24},{4,28},{8,16},{12,20},{16,8},{20,12},{24,0},{28,4},{1,25},{... | collective-permute-start | bytes 294920 | tf_op jit(solution)/shard_map/ppermute | solution.py:357
  69.4 8.6 %collective-permute-start.29 = (bf16[128,384]{1,0:T(8,128)(2,1)S(1)}, bf16[128,384]{1,0:T(8,128)(2,1)S(1)}, u32[]{:S(2)}, u32[]{:S(2)}) collective-permute-start(bf16[128,384]{1,0:T(8,128)(2,1)S(1)} %get-tuple-element.96), channel_id=1, source_target_pairs={{0,24},{4,28},{8,16},{12,20},{16,8},{20,12},{24,0},{28,4},{1,25},{... | collective-permute-start | bytes 294920 | tf_op jit(solution)/shard_map/ppermute | solution.py:357
  82.7 11.4 %collective-permute-start.35 = (bf16[272,384]{1,0:T(8,128)(2,1)S(1)}, bf16[272,384]{1,0:T(8,128)(2,1)S(1)}, u32[]{:S(2)}, u32[]{:S(2)}) collective-permute-start(bf16[272,384]{1,0:T(8,128)(2,1)S(1)} %add_convert_fusion.3.refs_1_), channel_id=1, source_target_pairs={{0,1},{1,0},{2,3},{3,2},{4,5},{5,4},{6,7},{7,6},{8,9},{9,8},{10,11... | collective-permute-start | bytes 626696 | tf_op jit(solution)/shard_map/ppermute | solution.py:366
  94.2 8.0 %collective-permute-start.39 = (bf16[256,384]{1,0:T(8,128)(2,1)S(1)}, bf16[256,384]{1,0:T(8,128)(2,1)S(1)}, u32[]{:S(2)}, u32[]{:S(2)}) collective-permute-start(bf16[256,384]{1,0:T(8,128)(2,1)S(1)} %get-tuple-element.105.refs_0_.refs_5_), channel_id=1, source_target_pairs={{0,8},{4,12},{8,0},{12,4},{16,24},{20,28},{24,16},{28,20},{1,9},{5... | collective-permute-start | bytes 589832 | tf_op jit(solution)/shard_map/ppermute | solution.py:357
  95.1 10.5 %collective-permute-start.36 = (bf16[256,384]{1,0:T(8,128)(2,1)S(1)}, bf16[256,384]{1,0:T(8,128)(2,1)S(1)}, u32[]{:S(2)}, u32[]{:S(2)}) collective-permute-start(bf16[256,384]{1,0:T(8,128)(2,1)S(1)} %get-tuple-element.105.refs_0_.refs_5_), channel_id=1, source_target_pairs={{0,16},{4,20},{8,24},{12,28},{16,0},{20,4},{24,8},{28,12},{1,17},{... | collective-permute-start | bytes 589832 | tf_op jit(solution)/shard_map/ppermute | solution.py:357
  96.4 12.6 %collective-permute-start.34 = (bf16[144,768]{1,0:T(8,128)(2,1)S(1)}, bf16[144,768]{1,0:T(8,128)(2,1)S(1)}, u32[]{:S(2)}, u32[]{:S(2)}) collective-permute-start(bf16[144,768]{1,0:T(8,128)(2,1)S(1)} %add_convert_fusion.refs_2_), channel_id=1, source_target_pairs={{0,1},{1,0},{2,3},{3,2},{4,5},{5,4},{6,7},{7,6},{8,9},{9,8},{10,11... | collective-permute-start | bytes 663560 | tf_op jit(solution)/shard_map/ppermute | solution.py:366
  (29 other events, 132.4 us)

commit v4 on v3

--- a/solution.py
+++ b/solution.py
@@ -66,16 +66,12 @@
     )(*operands)
 
 
-def split_lags(place, lags, own, other):
+def split_inputs(place, lags, stored, grad, lags_own, lags_other, other, rim):
     core = place[1]
-    own[...] = lags[:, lanes(0, lags.shape[1], core)].astype(bf16)
-    other[...] = lags[:, lanes(0, lags.shape[1], 1 - core)].astype(bf16)
-
-
-def split_stored(place, stored, grad, _, other, rim):
-    core = place[1]
-    rows, chans = other.shape[0], other.shape[1] // 3
+    rows, chans = lags_own.shape
     width = 2 * chans
+    lags_own[...] = lags[:, lanes(0, width, core)].astype(bf16)
+    lags_other[...] = lags[:, lanes(0, width, 1 - core)].astype(bf16)
     for part in range(3):
         other[:, part * chans : (part + 1) * chans] = stored[:, lanes(part, width, 1 - core)]
     edge = pl.ds(pl.multiple_of(core * (rows - PAD), 16), PAD)
@@ -193,7 +189,11 @@
         real, imag = (None, None) if start is None else (start[upper], start[lower])
         for slot, at in pairs:
             lag_re, lag_im = lag_ref[slot, upper], lag_ref[slot, lower]
-            ser_re, ser_im = at[upper], at[lower]
+            if isinstance(at, tuple):
+                across = slice(at[1], at[1] + lag_ref.shape[2])
+                ser_re, ser_im = at[0][upper, across], at[0][lower, across]
+            else:
+                ser_re, ser_im = at[upper], at[lower]
             if adjoint:
                 re = lag_re * ser_re + lag_im * ser_im
                 im = lag_re * ser_im - lag_im * ser_re
@@ -216,17 +216,16 @@
     ).astype(bf16)
 
 
-def inside_rows(place, count, rows, ext, chans):
-    ids = lax.broadcasted_iota(jnp.int32, (ext, chans), 0)
-    return jnp.where((ids < rows) | (place[0] < count - 1), 1.0, 0.0)
+def inside(place, count):
+    return jnp.where(place[0] < count - 1, 1.0, 0.0)
 
 
 def query_part(place, count, d_out, conv, taps, mixed, proj_query):
     ext, chans = d_out.shape
     rows, width = ext - PAD, 2 * chans
-    inside = inside_rows(place, count, rows, ext, chans)
     at = lanes(0, width, place[1])
-    mixed[0:ext] = (d_out[...].astype(f32) * conv[...].astype(f32) * inside).astype(bf16).astype(f32)
+    mixed[0:ext] = (d_out[...].astype(f32) * conv[...].astype(f32)).astype(bf16).astype(f32)
+    mixed[rows:ext] = mixed[rows:ext] * inside(place, count)
     proj_query[...] = short_adjoint(taps, at, mixed, ext)
 
 
@@ -236,15 +235,15 @@
     core = place[1]
     rows, chans = block.shape
     ext, width = rows + PAD, 2 * chans
-    inside = inside_rows(place, count, rows, ext, chans)
     bias_here = bias[0:1, lanes(0, width, core)]
     mixed[0:rows] = bias_here * block[...].astype(f32)
     mixed[rows:ext] = bias_here * rim[...].astype(f32)
-    d_prod = (dot(inverse[...], total[...]) + mixed[0:ext]).astype(bf16).astype(f32) * inside
+    d_prod = (dot(inverse[...], total[...]) + mixed[0:ext]).astype(bf16).astype(f32)
     sums = part_share[...]
     for part, other in ((1, values), (2, keys)):
         at = lanes(part, width, core)
         mixed[0:ext] = (d_prod * other[...]).astype(bf16).astype(f32)
+        mixed[rows:ext] = mixed[rows:ext] * inside(place, count)
         proj[...] = short_adjoint(taps, at, mixed, ext)
         sums = sums + dot_last(proj[...], w_in[:, at])
     share[...] = sums
@@ -268,25 +267,31 @@
     accumulate(lag_ref, pairs, True, start, total)
 
 
-def late_pairs(place, count, got, spec, table):
-    rows = got[0].shape[0] if len(got) > 2 else 2 * got[0].shape[0]
-    first = count - (len(got) - 1)
-    pairs = []
-    for i in range(len(got) - 1):
-        if i < len(got) - 2:
-            spec[i] = dot(table[:, 0:rows], got[i][...])
+def late_pairs(place, count, got, spec, table, side):
+    rows, chans = side.shape[0], got[0].shape[1]
+    blocks = side.shape[1] // chans
+    first = count - blocks
+    at = 0
+    for i in range(blocks):
+        here = slice(i * chans, (i + 1) * chans)
+        if got[at].shape[0] == rows:
+            side[:, here] = got[at][...]
+            at += 1
         else:
             half = rows // 2
-            spec[i] = dot(table[:, 0:half], got[i][...]) + dot(table[:, half:rows], got[i + 1][...])
-        pairs.append((first + i, spec.at[i]))
+            side[0:half, here] = got[at][...]
+            side[half:rows, here] = got[at + 1][...]
+            at += 2
+    spec[...] = dot(table[:, 0:rows], side[...])
+    pairs = [(first + i, (spec, i * chans)) for i in range(blocks)]
     return [[(slot_of(place, m, count, adjoint), at) for m, at in pairs] for adjoint in (False, True)]
 
 
 def late(place, count, n_got, final, *refs):
     got, refs = refs[:n_got], refs[n_got:]
     start, part_share, block, rim, lag_ref, table, inverse, keys, values, bias, taps, w_in, below_core, _ = refs[:14]
-    share, short_share, pass_on, spec, total, mixed, proj = refs[14:]
-    _, pairs = late_pairs(place, count, got, spec, table)
+    share, short_share, pass_on, spec, total, mixed, proj, side = refs[14:]
+    _, pairs = late_pairs(place, count, got, spec, table, side)
     accumulate(lag_ref, pairs, True, start, total)
     gated_part(
         place, count, total, inverse, block, rim, keys, values, bias, taps, mixed, proj, w_in, part_share, share,
@@ -318,10 +323,10 @@
 def late_first(place, count, n_got, *refs):
     got, refs = refs[:n_got], refs[n_got:]
     start, start_conv, d_out, product, block, rim, lag_ref, table, inverse = refs[:9]
-    keys, values, bias, taps, w_in, _ = refs[9:15]
-    share, short_share, conv, spec, total, mixed, proj = refs[15:]
+    keys, values, bias, taps, w_in = refs[9:14]
+    share, short_share, conv, spec, total, mixed, proj, side = refs[14:]
     width = 2 * block.shape[1]
-    pairs_conv, pairs = late_pairs(place, count, got, spec, table)
+    pairs_conv, pairs = late_pairs(place, count, got, spec, table, side)
     accumulate(lag_ref, pairs_conv, False, start_conv, total)
     whole = dot(inverse[...], total[...]) + bias[0:1, lanes(0, width, place[1])] * product[...].astype(f32)
     conv[...] = whole.astype(bf16)
@@ -372,12 +377,10 @@
         return call(body, outs, scratch, name, limit, micros, *operands)
 
     stored, grad = projected[0, 0], cotangent[0]
-    lags_own, lags_other = run(
-        split_lags, [shape(own_rows, bf16), shape(own_rows, bf16)], [], "split_lags", 0.4, long_filter[0]
-    )
-    stored_other, rim_send = run(
-        split_stored, [shape(own_rows, bf16, 3 * chans), shape(PAD, bf16, 4 * width)], [], "split_stored", 0.6,
-        stored, grad, lags_other,
+    lags_own, lags_other, stored_other, rim_send = call(
+        split_inputs,
+        [shape(own_rows, bf16), shape(own_rows, bf16), shape(own_rows, bf16, 3 * chans), shape(PAD, bf16, 4 * width)],
+        [], "split_inputs", 56 * 1024 * 1024, 1.0, long_filter[0], stored, grad,
     )
     lags_core = swap_core(lags_other)
     rim_pairs = [(2 * q + 1, (2 * q + 2) % seq_count) for q in range(chips)]
@@ -408,6 +411,7 @@
     below = lax.ppermute(
         weight_half, "section", [(s, (s + 1) % section_count) for s in range(section_count)]
     )
+    below, _ = lax.optimization_barrier((below, spectra))
     below_core = swap_core(below)
 
     spec = pltpu.VMEM((2 * ext, chans), f32)
@@ -416,7 +420,9 @@
     mixed = pltpu.VMEM((ext + PAD, chans), f32)
     ms = list(range(1, chips // 2))
     specs = pltpu.VMEM((len(ms), 2 * ext, chans), f32)
-    late_specs = pltpu.VMEM((chips - 1 - len(ms), 2 * ext, chans), f32)
+    late_count = chips - 1 - len(ms)
+    late_specs = pltpu.VMEM((2 * ext, late_count * chans), f32)
+    side = pltpu.VMEM((rows, late_count * chans), bf16)
     gates = [shape(rows, bf16), shape(own_rows, bf16), shape(own_rows, bf16), shape(PAD, bf16)]
     proj = pltpu.VMEM((ext, chans), bf16)
     late_outs = [shape(ext, f32, width), shape(ext, bf16, width)]
@@ -439,8 +445,11 @@
             return swap_chip(value, m)
 
         got = [send(block, slice(0, rows), m) for m in range(1, chips - 1)]
-        got.append(send(upper_half, slice(0, own_rows), chips - 1))
-        got.append(send(lower_half, slice(own_rows, rows), chips - 1))
+        if first:
+            got.append(send(block, slice(0, rows), chips - 1))
+        else:
+            got.append(send(upper_half, slice(0, own_rows), chips - 1))
+            got.append(send(lower_half, slice(own_rows, rows), chips - 1))
         soon, last = got[: len(ms)], got[len(ms) :]
         if not first:
             grad_core = swap_core(grad)
@@ -449,17 +458,17 @@
                 lambda place, *refs: early_first(place, chips, *refs),
                 [total_wide, total_wide], [spec], "early_first", 1.8, block, product, spectra, table,
             )
-            carried = run(carry_grad, shape(ext, f32), [], "carry_grad", 1.0, grad, grad_core, below, start)
             start, start_conv = run(
                 lambda place, *refs: middle_first(place, chips, ms, *refs),
                 [total_wide, total_wide], [specs], "middle_first", 1.0, *soon, start, start_conv, spectra, table,
             )
             share, short_share, conv = run(
                 lambda place, *refs: late_first(place, chips, len(last), *refs),
-                late_outs + [shape(ext, bf16)], [late_specs, total_scratch, mixed, proj], "late_first", 4.0,
+                late_outs + [shape(ext, bf16)], [late_specs, total_scratch, mixed, proj, side], "late_first", 4.0,
                 *last, start, start_conv, d_out, product, block, rim, spectra, table, inverse, keys, values, bias,
-                taps, weight_in, carried,
-            )
+                taps, weight_in,
+            )
+            carried = run(carry_grad, shape(ext, f32), [], "carry_grad", 1.0, grad, grad_core, below, start)
             pass_on = run(pass_half, shape(ext, bf16), [], "pass_half", 0.5, short_share, below_core)
         else:
             start, part_share = run(
@@ -476,7 +485,7 @@
                 carried = run(carry_grad, shape(ext, f32), [], "carry_grad", 1.0, grad, grad_core, below, start)
             share, short_share, pass_on = run(
                 lambda place, *refs, final=final: late(place, chips, len(last), final, *refs),
-                late_outs + [shape(ext, bf16)], [late_specs, total_scratch, mixed, proj], "late", 2.5,
+                late_outs + [shape(ext, bf16)], [late_specs, total_scratch, mixed, proj, side], "late", 2.5,
                 *last, start, part_share, block, rim, spectra, table, inverse, keys, values, bias, taps, weight_in,
                 below_core, carried,
             )

time: 112 us -> 108 us (0.964)
  local copies, waits for them, and re-layouts: 3.65 us -> 1.2 us
  starting transfers between devices: 41.3 us -> 39.4 us
    ppermute x19 -> x18, waiting for transfers between devices: 12.4 us -> 15 us  [swap_chip(): lax.ppermute(value, 'seq', [(i, (i // 2 ^ m) * 2 + i % 2) for i in range(...]
    unnamed x24 -> x18, local copies, waits for them, and re-layouts: 3.61 us -> 1.16 us
    ppermute x1, waiting for transfers between devices: 2.27 us -> 0.01 us  [shards(): lax.ppermute(rim_send, 'seq', rim_pairs + [(b, a) for a, b in rim_pairs])]
    ppermute x19 -> x18, starting transfers between devices: 23.9 us -> 22.5 us  [swap_chip(): lax.ppermute(value, 'seq', [(i, (i // 2 ^ m) * 2 + i % 2) for i in range(...]
    pallas_call x31 -> x30, Pallas kernels: 27.8 us -> 28.7 us  [call(): pl.pallas_call(placed, out_shape=outs, in_specs=[vmem] * len(operands), o...]
  transfers between devices with their start and end apart: 41 -> 40, of which waited for: 23 -> 22; matrix products, arithmetic and copies ran while one was open for 0% -> 1% of each run, Pallas kernels for 19% -> 19%
where the time goes in v4:
time: 108 us
  starting transfers between devices  39.4 us (36%)
  waiting for transfers between devices  36.2 us (34%)
  Pallas kernels  28.7 us (27%)
  other arithmetic  2.32 us (2%)
  local copies, waits for them, and re-layouts  1.2 us (1%)
    pallas_call x30, Pallas kernels, call(): pl.pallas_call(placed, out_shape=outs, in_specs=[vmem] * len(operands), o...  28.7 us
    ppermute x18, starting transfers between devices, swap_chip(): lax.ppermute(value, 'seq', [(i, (i // 2 ^ m) * 2 + i % 2) for i in range(...  22.5 us
    ppermute x18, waiting for transfers between devices, swap_chip(): lax.ppermute(value, 'seq', [(i, (i // 2 ^ m) * 2 + i % 2) for i in range(...  15 us
    ppermute x6, waiting for transfers between devices, swap_section(): return lax.ppermute(value, ('seq', 'section'), pairs)  11.5 us
    ppermute x6, starting transfers between devices, swap_section(): return lax.ppermute(value, ('seq', 'section'), pairs)  9.13 us
    ppermute x14, waiting for transfers between devices, swap_core(): return lax.ppermute(value, 'seq', [(i, i ^ 1) for i in range(seq_count)])  6.72 us
    ppermute x1, starting transfers between devices, shards(): lax.ppermute(rim_send, 'seq', rim_pairs + [(b, a) for a, b in rim_pairs])  3.56 us
    ppermute x1, waiting for transfers between devices, shards(): lax.ppermute(weight_half, 'section', [(s, (s + 1) % section_count) for s...  2.96 us
  transfers between devices with their start and end apart: 40, of which 22 were waited for; matrix products, arithmetic and copies ran while one was open for 1% of the time, Pallas kernels for 19%

profile of v4, /device:TPU:0, one launch (start us, length us, event | category | flops | bytes accessed | tf_op | source)
XLA Modules:
  0.0 108.2 jit_solution(11542164982825665004)
XLA Ops:
  0.0 2.2 %split_inputs.1 = (bf16[128,384]{1,0:T(8,128)(2,1)}, bf16[128,384]{1,0:T(8,128)(2,1)}, bf16[128,1152]{1,0:T(8,128)(2,1)}, bf16[16,3072]{1,0:T(8,128)(2,1)}) custom-call(f32[128,768]{1,0:T(8,128)} %bitcast.31, bf16[128,2304]{1,0:T(8,128)(2,1)} %bitcast.26, bf16[128,768]{1,0:T(8,128)(2,1)} %bitcast.28), custom_call_target="tpu_custom_call" | custom-call | flops 1000000000 | tf_op jit(solution)/shard_map/split_inputs/pallas_call | solution.py:57
  2.7 3.6 %collective-permute-start.1 = (bf16[16,3072]{1,0:T(8,128)(2,1)}, bf16[16,3072]{1,0:T(8,128)(2,1)S(1)}, u32[]{:S(2)}, u32[]{:S(2)}) collective-permute-start(bf16[16,3072]{1,0:T(8,128)(2,1)} %get-tuple-element.60), channel_id=1, source_target_pairs={{4,8},{12,16},{20,24},{28,0},{8,4},{16,12},{24,20},{0,28},{5,9},{1... | collective-permute-start | bytes 294920 | tf_op jit(solution)/shard_map/ppermute | solution.py:387
  10.9 1.6 %collective-permute-start.11 = (bf16[384,768]{1,0:T(8,128)(2,1)S(1)}, bf16[384,768]{1,0:T(8,128)(2,1)S(1)}, u32[]{:S(2)}, u32[]{:S(2)}) collective-permute-start(bf16[384,768]{1,0:T(8,128)(2,1)S(1)} %dynamic-slice_bitcast_fusion), channel_id=1, source_target_pairs={{0,1},{1,2},{2,3},{3,0},{4,5},{5,6},{6,7},{7,4},{8,9},{9,10},{10,1... | collective-permute-start | bytes 1769480 | tf_op jit(solution)/shard_map/ppermute | solution.py:411
  12.5 2.2 %collective-permute-done.4.refs_6_.refs_1_ = bf16[256,384]{1,0:T(8,128)(2,1)S(1)} collective-permute-done((bf16[256,384]{1,0:T(8,128)(2,1)S(1)}, bf16[256,384]{1,0:T(8,128)(2,1)S(1)}, u32[]{:S(2)}, u32[]{:S(2)}) %collective-permute-start.4) | collective-permute-done | bytes 196640 | tf_op jit(solution)/shard_map/ppermute | solution.py:362
  18.9 1.5 %collective-permute-start.7 = (bf16[256,384]{1,0:T(8,128)(2,1)S(1)}, bf16[256,384]{1,0:T(8,128)(2,1)S(1)}, u32[]{:S(2)}, u32[]{:S(2)}) collective-permute-start(bf16[256,384]{1,0:T(8,128)(2,1)S(1)} %get-tuple-element.115), channel_id=1, source_target_pairs={{0,16},{4,20},{8,24},{12,28},{16,0},{20,4},{24,8},{28,12},{1,17},{... | collective-permute-start | bytes 589832 | tf_op jit(solution)/shard_map/ppermute | solution.py:362
  21.4 1.9 %collective-permute-done.10.refs_3_ = bf16[256,384]{1,0:T(8,128)(2,1)S(1)} collective-permute-done((bf16[256,384]{1,0:T(8,128)(2,1)S(1)}, bf16[256,384]{1,0:T(8,128)(2,1)S(1)}, u32[]{:S(2)}, u32[]{:S(2)}) %collective-permute-start.10) | collective-permute-done | bytes 196640 | tf_op jit(solution)/shard_map/ppermute | solution.py:362
  23.4 1.9 %lag_spectra.1.refs_2_.refs_3_.refs_8_.refs_7_ = f32[5,544,384]{2,1,0:T(8,128)S(1)} custom-call(bf16[256,384]{1,0:T(8,128)(2,1)S(1)} %maximum_select_fusion.refs_0_, bf16[256,384]{1,0:T(8,128)(2,1)S(1)} %collective-permute-done.4.refs_6_.refs_1_, bf16[256,384]{1,0:T(8,128)(2,1)S(1)} %collective-permute-done.5.refs_7_.refs_2_, ...), custom_call_target="tpu_custom_call" | custom-call | flops 2400000000 | tf_op jit(solution)/shard_map/lag_spectra/pallas_call | solution.py:57
  25.2 3.0 %collective-permute-done.11.refs_2_.refs_1_ = bf16[384,768]{1,0:T(8,128)(2,1)S(1)} collective-permute-done((bf16[384,768]{1,0:T(8,128)(2,1)S(1)}, bf16[384,768]{1,0:T(8,128)(2,1)S(1)}, u32[]{:S(2)}, u32[]{:S(2)}) %collective-permute-start.11) | collective-permute-done | bytes 589856 | tf_op jit(solution)/shard_map/ppermute | solution.py:411
  31.6 3.6 %late_first.1 = (f32[272,768]{1,0:T(8,128)S(1)}, bf16[272,768]{1,0:T(8,128)(2,1)S(1)}, bf16[272,384]{1,0:T(8,128)(2,1)S(1)}) custom-call(bf16[256,384]{1,0:T(8,128)(2,1)S(1)} %collective-permute-done.7.refs_0_, bf16[256,384]{1,0:T(8,128)(2,1)S(1)} %collective-permute-done.8.refs_1_, f32[544,384]{1,0:T(8,128)S(1)} %get-tuple-element.69.refs_2_.refs_3_, ...), custom_call_target="tpu_custom_call" | custom-call | flops 4000000000 | tf_op jit(solution)/shard_map/late_first/pallas_call | solution.py:57
  40.0 5.8 %collective-permute-done.16.refs_0_.refs_1_ = bf16[272,384]{1,0:T(8,128)(2,1)S(1)} collective-permute-done((bf16[272,384]{1,0:T(8,128)(2,1)S(1)}, bf16[272,384]{1,0:T(8,128)(2,1)S(1)}, u32[]{:S(2)}, u32[]{:S(2)}) %collective-permute-start.16) | collective-permute-done | bytes 208928 | tf_op jit(solution)/shard_map/ppermute | solution.py:371
  45.9 1.5 %collective-permute-start.20 = (bf16[256,384]{1,0:T(8,128)(2,1)S(1)}, bf16[256,384]{1,0:T(8,128)(2,1)S(1)}, u32[]{:S(2)}, u32[]{:S(2)}) collective-permute-start(bf16[256,384]{1,0:T(8,128)(2,1)S(1)} %get-tuple-element.80.refs_0_.refs_5_), channel_id=1, source_target_pairs={{0,8},{4,12},{8,0},{12,4},{16,24},{20,28},{24,16},{28,20},{1,9},{5... | collective-permute-start | bytes 589832 | tf_op jit(solution)/shard_map/ppermute | solution.py:362
  49.5 2.4 %collective-permute-start.19 = (bf16[128,384]{1,0:T(8,128)(2,1)S(1)}, bf16[128,384]{1,0:T(8,128)(2,1)S(1)}, u32[]{:S(2)}, u32[]{:S(2)}) collective-permute-start(bf16[128,384]{1,0:T(8,128)(2,1)S(1)} %get-tuple-element.82), channel_id=1, source_target_pairs={{0,24},{4,28},{8,16},{12,20},{16,8},{20,12},{24,0},{28,4},{1,25},{... | collective-permute-start | bytes 294920 | tf_op jit(solution)/shard_map/ppermute | solution.py:362
  56.9 2.5 %late.3 = (f32[272,768]{1,0:T(8,128)S(1)}, bf16[272,768]{1,0:T(8,128)(2,1)S(1)}, bf16[272,384]{1,0:T(8,128)(2,1)S(1)}) custom-call(bf16[256,384]{1,0:T(8,128)(2,1)S(1)} %collective-permute-done.17.refs_0_, bf16[128,384]{1,0:T(8,128)(2,1)S(1)} %collective-permute-done.18.refs_1_, bf16[128,384]{1,0:T(8,128)(2,1)S(1)} %collective-permute-done.19.refs_2_, ...), custom_call_target="tpu_custom_call" | custom-call | flops 2500000000 | tf_op jit(solution)/shard_map/late/pallas_call | solution.py:57
  64.9 1.7 %collective-permute-start.27 = (bf16[128,384]{1,0:T(8,128)(2,1)S(1)}, bf16[128,384]{1,0:T(8,128)(2,1)S(1)}, u32[]{:S(2)}, u32[]{:S(2)}) collective-permute-start(bf16[128,384]{1,0:T(8,128)(2,1)S(1)} %get-tuple-element.93), channel_id=1, source_target_pairs={{0,24},{4,28},{8,16},{12,20},{16,8},{20,12},{24,0},{28,4},{1,25},{... | collective-permute-start | bytes 294920 | tf_op jit(solution)/shard_map/ppermute | solution.py:362
  69.0 1.9 %collective-permute-done.29.refs_0_ = bf16[256,384]{1,0:T(8,128)(2,1)S(1)} collective-permute-done((bf16[256,384]{1,0:T(8,128)(2,1)S(1)}, bf16[256,384]{1,0:T(8,128)(2,1)S(1)}, u32[]{:S(2)}, u32[]{:S(2)}) %collective-permute-start.29) | collective-permute-done | bytes 196640 | tf_op jit(solution)/shard_map/ppermute | solution.py:362
  71.9 1.7 %collective-permute-done.27.refs_1_ = bf16[128,384]{1,0:T(8,128)(2,1)S(1)} collective-permute-done((bf16[128,384]{1,0:T(8,128)(2,1)S(1)}, bf16[128,384]{1,0:T(8,128)(2,1)S(1)}, u32[]{:S(2)}, u32[]{:S(2)}) %collective-permute-start.27) | collective-permute-done | bytes 98336 | tf_op jit(solution)/shard_map/ppermute | solution.py:362
  73.6 1.5 %collective-permute-done.28.refs_2_ = bf16[128,384]{1,0:T(8,128)(2,1)S(1)} collective-permute-done((bf16[128,384]{1,0:T(8,128)(2,1)S(1)}, bf16[128,384]{1,0:T(8,128)(2,1)S(1)}, u32[]{:S(2)}, u32[]{:S(2)}) %collective-permute-start.28) | collective-permute-done | bytes 98336 | tf_op jit(solution)/shard_map/ppermute | solution.py:362
  75.2 2.8 %late.4 = (f32[272,768]{1,0:T(8,128)S(1)}, bf16[272,768]{1,0:T(8,128)(2,1)S(1)}, bf16[272,384]{1,0:T(8,128)(2,1)S(1)}) custom-call(bf16[256,384]{1,0:T(8,128)(2,1)S(1)} %collective-permute-done.26.refs_0_, bf16[128,384]{1,0:T(8,128)(2,1)S(1)} %collective-permute-done.27.refs_1_, bf16[128,384]{1,0:T(8,128)(2,1)S(1)} %collective-permute-done.28.refs_2_, ...), custom_call_target="tpu_custom_call" | custom-call | flops 2500000000 | tf_op jit(solution)/shard_map/late/pallas_call | solution.py:57
  79.8 5.7 %collective-permute-start.34 = (bf16[272,384]{1,0:T(8,128)(2,1)S(1)}, bf16[272,384]{1,0:T(8,128)(2,1)S(1)}, u32[]{:S(2)}, u32[]{:S(2)}) collective-permute-start(bf16[272,384]{1,0:T(8,128)(2,1)S(1)} %add_convert_fusion.3.refs_1_), channel_id=1, source_target_pairs={{0,1},{1,0},{2,3},{3,2},{4,5},{5,4},{6,7},{7,6},{8,9},{9,8},{10,11... | collective-permute-start | bytes 626696 | tf_op jit(solution)/shard_map/ppermute | solution.py:371
  85.6 5.6 %collective-permute-done.34.refs_0_.refs_1_ = bf16[272,384]{1,0:T(8,128)(2,1)S(1)} collective-permute-done((bf16[272,384]{1,0:T(8,128)(2,1)S(1)}, bf16[272,384]{1,0:T(8,128)(2,1)S(1)}, u32[]{:S(2)}, u32[]{:S(2)}) %collective-permute-start.34) | collective-permute-done | bytes 208928 | tf_op jit(solution)/shard_map/ppermute | solution.py:371
  93.5 1.7 %collective-permute-start.33 = (bf16[144,768]{1,0:T(8,128)(2,1)S(1)}, bf16[144,768]{1,0:T(8,128)(2,1)S(1)}, u32[]{:S(2)}, u32[]{:S(2)}) collective-permute-start(bf16[144,768]{1,0:T(8,128)(2,1)S(1)} %add_convert_fusion.refs_2_), channel_id=1, source_target_pairs={{0,1},{1,0},{2,3},{3,2},{4,5},{5,4},{6,7},{7,6},{8,9},{9,8},{10,11... | collective-permute-start | bytes 663560 | tf_op jit(solution)/shard_map/ppermute | solution.py:371
  96.5 1.6 %collective-permute-start.37 = (bf16[128,384]{1,0:T(8,128)(2,1)S(1)}, bf16[128,384]{1,0:T(8,128)(2,1)S(1)}, u32[]{:S(2)}, u32[]{:S(2)}) collective-permute-start(bf16[128,384]{1,0:T(8,128)(2,1)S(1)} %get-tuple-element.105), channel_id=1, source_target_pairs={{0,24},{4,28},{8,16},{12,20},{16,8},{20,12},{24,0},{28,4},{1,25},{... | collective-permute-start | bytes 294920 | tf_op jit(solution)/shard_map/ppermute | solution.py:362
  99.9 1.5 %collective-permute-done.36.refs_1_ = bf16[128,384]{1,0:T(8,128)(2,1)S(1)} collective-permute-done((bf16[128,384]{1,0:T(8,128)(2,1)S(1)}, bf16[128,384]{1,0:T(8,128)(2,1)S(1)}, u32[]{:S(2)}, u32[]{:S(2)}) %collective-permute-start.36) | collective-permute-done | bytes 98336 | tf_op jit(solution)/shard_map/ppermute | solution.py:362
  102.6 3.1 %late.5 = (f32[272,768]{1,0:T(8,128)S(1)}, bf16[272,768]{1,0:T(8,128)(2,1)}, bf16[272,384]{1,0:T(8,128)(2,1)S(1)}) custom-call(bf16[256,384]{1,0:T(8,128)(2,1)S(1)} %collective-permute-done.35.refs_0_, bf16[128,384]{1,0:T(8,128)(2,1)S(1)} %collective-permute-done.36.refs_1_, bf16[128,384]{1,0:T(8,128)(2,1)S(1)} %collective-permute-done.37.refs_2_, ...), custom_call_target="tpu_custom_call" | custom-call | flops 2500000000 | tf_op jit(solution)/shard_map/late/pallas_call | solution.py:57
  (114 shorter events, 45.3 us)
Async XLA Ops:
  6.2 9.5 %collective-permute-start = (bf16[128,1152]{1,0:T(8,128)(2,1)}, bf16[128,1152]{1,0:T(8,128)(2,1)S(1)}, u32[]{:S(2)}, u32[]{:S(2)}) collective-permute-start(bf16[128,1152]{1,0:T(8,128)(2,1)} %get-tuple-element.59), channel_id=1, source_target_pairs={{0,4},{4,0},{8,12},{12,8},{16,20},{20,16},{24,28},{28,24},{1,5},{5... | collective-permute-start | bytes 884744 | tf_op jit(solution)/shard_map/ppermute | solution.py:359
  7.3 7.4 %collective-permute-start.4 = (bf16[256,384]{1,0:T(8,128)(2,1)S(1)}, bf16[256,384]{1,0:T(8,128)(2,1)S(1)}, u32[]{:S(2)}, u32[]{:S(2)}) collective-permute-start(bf16[256,384]{1,0:T(8,128)(2,1)S(1)} %maximum_select_fusion.refs_0_), channel_id=1, source_target_pairs={{0,8},{4,12},{8,0},{12,4},{16,24},{20,28},{24,16},{28,20},{1,9},{5... | collective-permute-start | bytes 589832 | tf_op jit(solution)/shard_map/ppermute | solution.py:362
  7.9 7.8 %collective-permute-start.5 = (bf16[256,384]{1,0:T(8,128)(2,1)S(1)}, bf16[256,384]{1,0:T(8,128)(2,1)S(1)}, u32[]{:S(2)}, u32[]{:S(2)}) collective-permute-start(bf16[256,384]{1,0:T(8,128)(2,1)S(1)} %maximum_select_fusion.refs_0_), channel_id=1, source_target_pairs={{0,16},{4,20},{8,24},{12,28},{16,0},{20,4},{24,8},{28,12},{1,17},{... | collective-permute-start | bytes 589832 | tf_op jit(solution)/shard_map/ppermute | solution.py:362
  9.3 7.2 %collective-permute-start.6 = (bf16[128,768]{1,0:T(8,128)(2,1)S(1)}, bf16[128,768]{1,0:T(8,128)(2,1)S(1)}, u32[]{:S(2)}, u32[]{:S(2)}) collective-permute-start(bf16[128,768]{1,0:T(8,128)(2,1)S(1)} %bitcast.29), channel_id=1, source_target_pairs={{0,4},{4,0},{8,12},{12,8},{16,20},{20,16},{24,28},{28,24},{1,5},{5... | collective-permute-start | bytes 589832 | tf_op jit(solution)/shard_map/ppermute | solution.py:359
  10.9 17.3 %collective-permute-start.11 = (bf16[384,768]{1,0:T(8,128)(2,1)S(1)}, bf16[384,768]{1,0:T(8,128)(2,1)S(1)}, u32[]{:S(2)}, u32[]{:S(2)}) collective-permute-start(bf16[384,768]{1,0:T(8,128)(2,1)S(1)} %dynamic-slice_bitcast_fusion), channel_id=1, source_target_pairs={{0,1},{1,2},{2,3},{3,0},{4,5},{5,6},{6,7},{7,4},{8,9},{9,10},{10,1... | collective-permute-start | bytes 1769480 | tf_op jit(solution)/shard_map/ppermute | solution.py:411
  14.7 8.7 %collective-permute-start.10 = (bf16[256,384]{1,0:T(8,128)(2,1)S(1)}, bf16[256,384]{1,0:T(8,128)(2,1)S(1)}, u32[]{:S(2)}, u32[]{:S(2)}) collective-permute-start(bf16[256,384]{1,0:T(8,128)(2,1)S(1)} %maximum_select_fusion.refs_0_), channel_id=1, source_target_pairs={{0,24},{4,28},{8,16},{12,20},{16,8},{20,12},{24,0},{28,4},{1,25},{... | collective-permute-start | bytes 589832 | tf_op jit(solution)/shard_map/ppermute | solution.py:362
  17.9 11.7 %collective-permute-start.9 = (bf16[256,384]{1,0:T(8,128)(2,1)S(1)}, bf16[256,384]{1,0:T(8,128)(2,1)S(1)}, u32[]{:S(2)}, u32[]{:S(2)}) collective-permute-start(bf16[256,384]{1,0:T(8,128)(2,1)S(1)} %get-tuple-element.113), channel_id=1, source_target_pairs={{0,8},{4,12},{8,0},{12,4},{16,24},{20,28},{24,16},{28,20},{1,9},{5... | collective-permute-start | bytes 589832 | tf_op jit(solution)/shard_map/ppermute | solution.py:362
  18.9 11.6 %collective-permute-start.7 = (bf16[256,384]{1,0:T(8,128)(2,1)S(1)}, bf16[256,384]{1,0:T(8,128)(2,1)S(1)}, u32[]{:S(2)}, u32[]{:S(2)}) collective-permute-start(bf16[256,384]{1,0:T(8,128)(2,1)S(1)} %get-tuple-element.115), channel_id=1, source_target_pairs={{0,16},{4,20},{8,24},{12,28},{16,0},{20,4},{24,8},{28,12},{1,17},{... | collective-permute-start | bytes 589832 | tf_op jit(solution)/shard_map/ppermute | solution.py:362
  20.4 10.1 %collective-permute-start.8 = (bf16[256,384]{1,0:T(8,128)(2,1)S(1)}, bf16[256,384]{1,0:T(8,128)(2,1)S(1)}, u32[]{:S(2)}, u32[]{:S(2)}) collective-permute-start(bf16[256,384]{1,0:T(8,128)(2,1)S(1)} %get-tuple-element.114), channel_id=1, source_target_pairs={{0,24},{4,28},{8,16},{12,20},{16,8},{20,12},{24,0},{28,4},{1,25},{... | collective-permute-start | bytes 589832 | tf_op jit(solution)/shard_map/ppermute | solution.py:362
  28.2 7.0 %collective-permute-start.12 = (bf16[384,768]{1,0:T(8,128)(2,1)S(1)}, bf16[384,768]{1,0:T(8,128)(2,1)S(1)}, u32[]{:S(2)}, u32[]{:S(2)}) collective-permute-start(bf16[384,768]{1,0:T(8,128)(2,1)S(1)} %collective-permute-done.11.refs_2_.refs_1_), channel_id=1, source_target_pairs={{0,4},{4,0},{8,12},{12,8},{16,20},{20,16},{24,28},{28,24},{1,5},{5... | collective-permute-start | bytes 1769480 | tf_op jit(solution)/shard_map/ppermute | solution.py:359
  37.9 8.0 %collective-permute-start.16 = (bf16[272,384]{1,0:T(8,128)(2,1)S(1)}, bf16[272,384]{1,0:T(8,128)(2,1)S(1)}, u32[]{:S(2)}, u32[]{:S(2)}) collective-permute-start(bf16[272,384]{1,0:T(8,128)(2,1)S(1)} %add_convert_fusion.5.refs_1_), channel_id=1, source_target_pairs={{0,1},{1,0},{2,3},{3,2},{4,5},{5,4},{6,7},{7,6},{8,9},{9,8},{10,11... | collective-permute-start | bytes 626696 | tf_op jit(solution)/shard_map/ppermute | solution.py:371
  39.0 12.8 %collective-permute-start.15 = (bf16[144,768]{1,0:T(8,128)(2,1)S(1)}, bf16[144,768]{1,0:T(8,128)(2,1)S(1)}, u32[]{:S(2)}, u32[]{:S(2)}) collective-permute-start(bf16[144,768]{1,0:T(8,128)(2,1)S(1)} %add_convert_fusion.2.refs_2_), channel_id=1, source_target_pairs={{0,1},{1,0},{2,3},{3,2},{4,5},{5,4},{6,7},{7,6},{8,9},{9,8},{10,11... | collective-permute-start | bytes 663560 | tf_op jit(solution)/shard_map/ppermute | solution.py:371
  45.9 7.7 %collective-permute-start.20 = (bf16[256,384]{1,0:T(8,128)(2,1)S(1)}, bf16[256,384]{1,0:T(8,128)(2,1)S(1)}, u32[]{:S(2)}, u32[]{:S(2)}) collective-permute-start(bf16[256,384]{1,0:T(8,128)(2,1)S(1)} %get-tuple-element.80.refs_0_.refs_5_), channel_id=1, source_target_pairs={{0,8},{4,12},{8,0},{12,4},{16,24},{20,28},{24,16},{28,20},{1,9},{5... | collective-permute-start | bytes 589832 | tf_op jit(solution)/shard_map/ppermute | solution.py:362
  47.4 9.5 %collective-permute-start.17 = (bf16[256,384]{1,0:T(8,128)(2,1)S(1)}, bf16[256,384]{1,0:T(8,128)(2,1)S(1)}, u32[]{:S(2)}, u32[]{:S(2)}) collective-permute-start(bf16[256,384]{1,0:T(8,128)(2,1)S(1)} %get-tuple-element.80.refs_0_.refs_5_), channel_id=1, source_target_pairs={{0,16},{4,20},{8,24},{12,28},{16,0},{20,4},{24,8},{28,12},{1,17},{... | collective-permute-start | bytes 589832 | tf_op jit(solution)/shard_map/ppermute | solution.py:362
  48.9 6.8 %collective-permute-start.18 = (bf16[128,384]{1,0:T(8,128)(2,1)S(1)}, bf16[128,384]{1,0:T(8,128)(2,1)S(1)}, u32[]{:S(2)}, u32[]{:S(2)}) collective-permute-start(bf16[128,384]{1,0:T(8,128)(2,1)S(1)} %get-tuple-element.81), channel_id=1, source_target_pairs={{0,24},{4,28},{8,16},{12,20},{16,8},{20,12},{24,0},{28,4},{1,25},{... | collective-permute-start | bytes 294920 | tf_op jit(solution)/shard_map/ppermute | solution.py:362
  49.5 7.3 %collective-permute-start.19 = (bf16[128,384]{1,0:T(8,128)(2,1)S(1)}, bf16[128,384]{1,0:T(8,128)(2,1)S(1)}, u32[]{:S(2)}, u32[]{:S(2)}) collective-permute-start(bf16[128,384]{1,0:T(8,128)(2,1)S(1)} %get-tuple-element.82), channel_id=1, source_target_pairs={{0,24},{4,28},{8,16},{12,20},{16,8},{20,12},{24,0},{28,4},{1,25},{... | collective-permute-start | bytes 294920 | tf_op jit(solution)/shard_map/ppermute | solution.py:362
  63.1 7.8 %collective-permute-start.29 = (bf16[256,384]{1,0:T(8,128)(2,1)S(1)}, bf16[256,384]{1,0:T(8,128)(2,1)S(1)}, u32[]{:S(2)}, u32[]{:S(2)}) collective-permute-start(bf16[256,384]{1,0:T(8,128)(2,1)S(1)} %get-tuple-element.92.refs_0_.refs_5_), channel_id=1, source_target_pairs={{0,8},{4,12},{8,0},{12,4},{16,24},{20,28},{24,16},{28,20},{1,9},{5... | collective-permute-start | bytes 589832 | tf_op jit(solution)/shard_map/ppermute | solution.py:362
  64.1 11.1 %collective-permute-start.26 = (bf16[256,384]{1,0:T(8,128)(2,1)S(1)}, bf16[256,384]{1,0:T(8,128)(2,1)S(1)}, u32[]{:S(2)}, u32[]{:S(2)}) collective-permute-start(bf16[256,384]{1,0:T(8,128)(2,1)S(1)} %get-tuple-element.92.refs_0_.refs_5_), channel_id=1, source_target_pairs={{0,16},{4,20},{8,24},{12,28},{16,0},{20,4},{24,8},{28,12},{1,17},{... | collective-permute-start | bytes 589832 | tf_op jit(solution)/shard_map/ppermute | solution.py:362
  64.9 8.7 %collective-permute-start.27 = (bf16[128,384]{1,0:T(8,128)(2,1)S(1)}, bf16[128,384]{1,0:T(8,128)(2,1)S(1)}, u32[]{:S(2)}, u32[]{:S(2)}) collective-permute-start(bf16[128,384]{1,0:T(8,128)(2,1)S(1)} %get-tuple-element.93), channel_id=1, source_target_pairs={{0,24},{4,28},{8,16},{12,20},{16,8},{20,12},{24,0},{28,4},{1,25},{... | collective-permute-start | bytes 294920 | tf_op jit(solution)/shard_map/ppermute | solution.py:362
  66.6 8.5 %collective-permute-start.28 = (bf16[128,384]{1,0:T(8,128)(2,1)S(1)}, bf16[128,384]{1,0:T(8,128)(2,1)S(1)}, u32[]{:S(2)}, u32[]{:S(2)}) collective-permute-start(bf16[128,384]{1,0:T(8,128)(2,1)S(1)} %get-tuple-element.94), channel_id=1, source_target_pairs={{0,24},{4,28},{8,16},{12,20},{16,8},{20,12},{24,0},{28,4},{1,25},{... | collective-permute-start | bytes 294920 | tf_op jit(solution)/shard_map/ppermute | solution.py:362
  79.8 11.4 %collective-permute-start.34 = (bf16[272,384]{1,0:T(8,128)(2,1)S(1)}, bf16[272,384]{1,0:T(8,128)(2,1)S(1)}, u32[]{:S(2)}, u32[]{:S(2)}) collective-permute-start(bf16[272,384]{1,0:T(8,128)(2,1)S(1)} %add_convert_fusion.3.refs_1_), channel_id=1, source_target_pairs={{0,1},{1,0},{2,3},{3,2},{4,5},{5,4},{6,7},{7,6},{8,9},{9,8},{10,11... | collective-permute-start | bytes 626696 | tf_op jit(solution)/shard_map/ppermute | solution.py:371
  91.2 8.0 %collective-permute-start.38 = (bf16[256,384]{1,0:T(8,128)(2,1)S(1)}, bf16[256,384]{1,0:T(8,128)(2,1)S(1)}, u32[]{:S(2)}, u32[]{:S(2)}) collective-permute-start(bf16[256,384]{1,0:T(8,128)(2,1)S(1)} %get-tuple-element.103.refs_0_.refs_5_), channel_id=1, source_target_pairs={{0,8},{4,12},{8,0},{12,4},{16,24},{20,28},{24,16},{28,20},{1,9},{5... | collective-permute-start | bytes 589832 | tf_op jit(solution)/shard_map/ppermute | solution.py:362
  92.1 10.5 %collective-permute-start.35 = (bf16[256,384]{1,0:T(8,128)(2,1)S(1)}, bf16[256,384]{1,0:T(8,128)(2,1)S(1)}, u32[]{:S(2)}, u32[]{:S(2)}) collective-permute-start(bf16[256,384]{1,0:T(8,128)(2,1)S(1)} %get-tuple-element.103.refs_0_.refs_5_), channel_id=1, source_target_pairs={{0,16},{4,20},{8,24},{12,28},{16,0},{20,4},{24,8},{28,12},{1,17},{... | collective-permute-start | bytes 589832 | tf_op jit(solution)/shard_map/ppermute | solution.py:362
  93.5 12.4 %collective-permute-start.33 = (bf16[144,768]{1,0:T(8,128)(2,1)S(1)}, bf16[144,768]{1,0:T(8,128)(2,1)S(1)}, u32[]{:S(2)}, u32[]{:S(2)}) collective-permute-start(bf16[144,768]{1,0:T(8,128)(2,1)S(1)} %add_convert_fusion.refs_2_), channel_id=1, source_target_pairs={{0,1},{1,0},{2,3},{3,2},{4,5},{5,4},{6,7},{7,6},{8,9},{9,8},{10,11... | collective-permute-start | bytes 663560 | tf_op jit(solution)/shard_map/ppermute | solution.py:371
  (25 other events, 123.3 us)

commit v5 on v4

--- a/solution.py
+++ b/solution.py
@@ -226,7 +226,7 @@
     at = lanes(0, width, place[1])
     mixed[0:ext] = (d_out[...].astype(f32) * conv[...].astype(f32)).astype(bf16).astype(f32)
     mixed[rows:ext] = mixed[rows:ext] * inside(place, count)
-    proj_query[...] = short_adjoint(taps, at, mixed, ext)
+    proj_query[:, 0:chans] = short_adjoint(taps, at, mixed, ext)
 
 
 def gated_part(
@@ -239,13 +239,12 @@
     mixed[0:rows] = bias_here * block[...].astype(f32)
     mixed[rows:ext] = bias_here * rim[...].astype(f32)
     d_prod = (dot(inverse[...], total[...]) + mixed[0:ext]).astype(bf16).astype(f32)
-    sums = part_share[...]
     for part, other in ((1, values), (2, keys)):
         at = lanes(part, width, core)
         mixed[0:ext] = (d_prod * other[...]).astype(bf16).astype(f32)
         mixed[rows:ext] = mixed[rows:ext] * inside(place, count)
-        proj[...] = short_adjoint(taps, at, mixed, ext)
-        sums = sums + dot_last(proj[...], w_in[:, at])
+        proj[:, (part - 1) * chans : part * chans] = short_adjoint(taps, at, mixed, ext)
+    sums = part_share[...] + dot_last(proj[...], w_in[:, chans:])
     share[...] = sums
     short_share[...] = sums.astype(bf16)
 
@@ -255,7 +254,7 @@
     spec[...] = dot(table[:, 0:rows], block[...])
     accumulate(lag_ref, [(slot_of(place, 0, count, True), spec)], True, None, total)
     query_part(place, count, d_out, conv, taps, mixed, proj)
-    share[...] = dot_last(proj[...], w_in[:, lanes(0, w_in.shape[0], place[1])])
+    share[...] = dot_last(proj[:, 0 : conv.shape[1]], w_in[:, 0 : conv.shape[1]])
 
 
 def middle(place, count, ms, *refs):
@@ -289,8 +288,8 @@
 
 def late(place, count, n_got, final, *refs):
     got, refs = refs[:n_got], refs[n_got:]
-    start, part_share, block, rim, lag_ref, table, inverse, keys, values, bias, taps, w_in, below_core, _ = refs[:14]
-    share, short_share, pass_on, spec, total, mixed, proj, side = refs[14:]
+    start, part_share, block, rim, lag_ref, table, inverse, keys, values, bias, taps, w_in, below_core = refs[:13]
+    share, short_share, pass_on, spec, total, mixed, proj, side = refs[13:]
     _, pairs = late_pairs(place, count, got, spec, table, side)
     accumulate(lag_ref, pairs, True, start, total)
     gated_part(
@@ -303,7 +302,10 @@
         pass_half(place, short_share, below_core, pass_on)
 
 
-def early_first(place, count, block, product, lag_ref, table, total, total_conv, spec):
+def early_first(place, count, block, product, lag_ref, table, w_in, total, total_conv, weight, spec):
+    chans = block.shape[1]
+    for part in range(3):
+        weight[:, part * chans : (part + 1) * chans] = w_in[:, lanes(part, 2 * chans, place[1])]
     rows = block.shape[0]
     spec[...] = dot(table[:, 0:rows], block[...])
     accumulate(lag_ref, [(slot_of(place, 0, count, True), spec)], True, None, total)
@@ -331,7 +333,7 @@
     whole = dot(inverse[...], total[...]) + bias[0:1, lanes(0, width, place[1])] * product[...].astype(f32)
     conv[...] = whole.astype(bf16)
     query_part(place, count, d_out, conv, taps, mixed, proj)
-    share[...] = dot_last(proj[...], w_in[:, lanes(0, width, place[1])])
+    share[...] = dot_last(proj[:, 0 : conv.shape[1]], w_in[:, 0 : conv.shape[1]])
     accumulate(lag_ref, pairs, True, start, total)
     gated_part(
         place, count, total, inverse, block, rim, keys, values, bias, taps, mixed, proj, w_in, share, share, short_share
@@ -403,7 +405,7 @@
         lambda place, *refs: lag_spectra(place, chips, *refs),
         jax.ShapeDtypeStruct((chips + 1, 2 * ext, chans), f32),
         [pltpu.VMEM((chips * rows + ext + PAD, chans), bf16)],
-        "lag_spectra", 2.4,
+        "lag_spectra", 10.0,
         *pieces, lag_table,
     )
 
@@ -424,7 +426,7 @@
     late_specs = pltpu.VMEM((2 * ext, late_count * chans), f32)
     side = pltpu.VMEM((rows, late_count * chans), bf16)
     gates = [shape(rows, bf16), shape(own_rows, bf16), shape(own_rows, bf16), shape(PAD, bf16)]
-    proj = pltpu.VMEM((ext, chans), bf16)
+    proj = pltpu.VMEM((ext, 2 * chans), bf16)
     late_outs = [shape(ext, f32, width), shape(ext, bf16, width)]
     ends = [shape(own_rows + PAD, f32, width), shape(own_rows + PAD, bf16, width)]
     result = jnp.zeros((own_rows, width), bf16)
@@ -454,19 +456,19 @@
         if not first:
             grad_core = swap_core(grad)
         if first:
-            start, start_conv = run(
+            start, start_conv, weight_own = run(
                 lambda place, *refs: early_first(place, chips, *refs),
-                [total_wide, total_wide], [spec], "early_first", 1.8, block, product, spectra, table,
+                [total_wide, total_wide, shape(width, bf16, 3 * chans)], [spec], "early_first", 10.0, block, product, spectra, table, weight_in,
             )
             start, start_conv = run(
                 lambda place, *refs: middle_first(place, chips, ms, *refs),
-                [total_wide, total_wide], [specs], "middle_first", 1.0, *soon, start, start_conv, spectra, table,
+                [total_wide, total_wide], [specs], "middle_first", 10.0, *soon, start, start_conv, spectra, table,
             )
             share, short_share, conv = run(
                 lambda place, *refs: late_first(place, chips, len(last), *refs),
                 late_outs + [shape(ext, bf16)], [late_specs, total_scratch, mixed, proj, side], "late_first", 4.0,
                 *last, start, start_conv, d_out, product, block, rim, spectra, table, inverse, keys, values, bias,
-                taps, weight_in,
+                taps, weight_own,
             )
             carried = run(carry_grad, shape(ext, f32), [], "carry_grad", 1.0, grad, grad_core, below, start)
             pass_on = run(pass_half, shape(ext, bf16), [], "pass_half", 0.5, short_share, below_core)
@@ -474,21 +476,20 @@
             start, part_share = run(
                 lambda place, *refs: early(place, chips, *refs),
                 [total_wide, shape(ext, f32, width)], [spec, mixed, proj], "early", 1.6,
-                block, d_out, conv, spectra, table, taps, weight_in,
+                block, d_out, conv, spectra, table, taps, weight_own,
             )
             start = run(
                 lambda place, *refs: middle(place, chips, ms, *refs),
                 total_wide, [specs], "middle", 0.8, *soon, start, spectra, table,
             )
-            carried = start
-            if not final:
-                carried = run(carry_grad, shape(ext, f32), [], "carry_grad", 1.0, grad, grad_core, below, start)
             share, short_share, pass_on = run(
                 lambda place, *refs, final=final: late(place, chips, len(last), final, *refs),
                 late_outs + [shape(ext, bf16)], [late_specs, total_scratch, mixed, proj, side], "late", 2.5,
-                *last, start, part_share, block, rim, spectra, table, inverse, keys, values, bias, taps, weight_in,
-                below_core, carried,
-            )
+                *last, start, part_share, block, rim, spectra, table, inverse, keys, values, bias, taps, weight_own,
+                below_core,
+            )
+            if not final:
+                carried = run(carry_grad, shape(ext, f32), [], "carry_grad", 0.5, grad, grad_core, below, pass_on)
         half = pass_on
         if not final:
             keep = run(keep_half, shape(ext, f32), [], "keep_half", 0.6, short_share, below, carried)

time: 108 us -> 107 us (level)
  local copies, waits for them, and re-layouts: 1.2 us -> 0.08 us
    ppermute x6, starting transfers between devices: 9.13 us -> 11.7 us  [swap_section(): return lax.ppermute(value, ('seq', 'section'), pairs)]
    ppermute x18, waiting for transfers between devices: 15 us -> 17.3 us  [swap_chip(): lax.ppermute(value, 'seq', [(i, (i // 2 ^ m) * 2 + i % 2) for i in range(...]
    ppermute x14, waiting for transfers between devices: 6.72 us -> 5.11 us  [swap_core(): return lax.ppermute(value, 'seq', [(i, i ^ 1) for i in range(seq_count)])]
    ppermute x1, waiting for transfers between devices: 2.96 us -> 1.46 us  [shards(): lax.ppermute(weight_half, 'section', [(s, (s + 1) % section_count) for s...]
    ppermute x18, starting transfers between devices: 22.5 us -> 21.4 us  [swap_chip(): lax.ppermute(value, 'seq', [(i, (i // 2 ^ m) * 2 + i % 2) for i in range(...]
    unnamed x18, local copies, waits for them, and re-layouts: 1.16 us -> 0.04 us
  transfers between devices with their start and end apart: 40 -> 40, of which waited for: 22 -> 23; matrix products, arithmetic and copies ran while one was open for 1% -> 1% of each run, Pallas kernels for 19% -> 24%
where the time goes in v5:
time: 107 us
  starting transfers between devices  40.2 us (38%)
  waiting for transfers between devices  35.4 us (33%)
  Pallas kernels  28 us (26%)
  other arithmetic  2.31 us (2%)
    pallas_call x30, Pallas kernels, call(): pl.pallas_call(placed, out_shape=outs, in_specs=[vmem] * len(operands), o...  28 us
    ppermute x18, starting transfers between devices, swap_chip(): lax.ppermute(value, 'seq', [(i, (i // 2 ^ m) * 2 + i % 2) for i in range(...  21.4 us
    ppermute x18, waiting for transfers between devices, swap_chip(): lax.ppermute(value, 'seq', [(i, (i // 2 ^ m) * 2 + i % 2) for i in range(...  17.3 us
    ppermute x6, starting transfers between devices, swap_section(): return lax.ppermute(value, ('seq', 'section'), pairs)  11.7 us
    ppermute x6, waiting for transfers between devices, swap_section(): return lax.ppermute(value, ('seq', 'section'), pairs)  11.6 us
    ppermute x14, waiting for transfers between devices, swap_core(): return lax.ppermute(value, 'seq', [(i, i ^ 1) for i in range(seq_count)])  5.11 us
    ppermute x1, starting transfers between devices, shards(): lax.ppermute(rim_send, 'seq', rim_pairs + [(b, a) for a, b in rim_pairs])  3.56 us
  transfers between devices with their start and end apart: 40, of which 23 were waited for; matrix products, arithmetic and copies ran while one was open for 1% of the time, Pallas kernels for 24%

profile of v5, /device:TPU:0, one launch (start us, length us, event | category | flops | bytes accessed | tf_op | source)
XLA Modules:
  0.0 106.5 jit_solution(16893126915620610225)
XLA Ops:
  0.0 2.2 %split_inputs.1 = (bf16[128,384]{1,0:T(8,128)(2,1)}, bf16[128,384]{1,0:T(8,128)(2,1)}, bf16[128,1152]{1,0:T(8,128)(2,1)}, bf16[16,3072]{1,0:T(8,128)(2,1)}) custom-call(f32[128,768]{1,0:T(8,128)} %bitcast.25, bf16[128,2304]{1,0:T(8,128)(2,1)} %bitcast.20, bf16[128,768]{1,0:T(8,128)(2,1)} %bitcast.22), custom_call_target="tpu_custom_call" | custom-call | flops 1000000000 | tf_op jit(solution)/shard_map/split_inputs/pallas_call | solution.py:57
  2.7 3.6 %collective-permute-start.1 = (bf16[16,3072]{1,0:T(8,128)(2,1)}, bf16[16,3072]{1,0:T(8,128)(2,1)S(1)}, u32[]{:S(2)}, u32[]{:S(2)}) collective-permute-start(bf16[16,3072]{1,0:T(8,128)(2,1)} %get-tuple-element.61), channel_id=1, source_target_pairs={{4,8},{12,16},{20,24},{28,0},{8,4},{16,12},{24,20},{0,28},{5,9},{1... | collective-permute-start | bytes 294920 | tf_op jit(solution)/shard_map/ppermute | solution.py:389
  10.9 1.6 %collective-permute-start.11 = (bf16[384,768]{1,0:T(8,128)(2,1)S(1)}, bf16[384,768]{1,0:T(8,128)(2,1)S(1)}, u32[]{:S(2)}, u32[]{:S(2)}) collective-permute-start(bf16[384,768]{1,0:T(8,128)(2,1)S(1)} %dynamic-slice_bitcast_fusion), channel_id=1, source_target_pairs={{0,1},{1,2},{2,3},{3,0},{4,5},{5,6},{6,7},{7,4},{8,9},{9,10},{10,1... | collective-permute-start | bytes 1769480 | tf_op jit(solution)/shard_map/ppermute | solution.py:413
  12.5 2.2 %collective-permute-done.4.refs_6_.refs_1_ = bf16[256,384]{1,0:T(8,128)(2,1)S(1)} collective-permute-done((bf16[256,384]{1,0:T(8,128)(2,1)S(1)}, bf16[256,384]{1,0:T(8,128)(2,1)S(1)}, u32[]{:S(2)}, u32[]{:S(2)}) %collective-permute-start.4) | collective-permute-done | bytes 196640 | tf_op jit(solution)/shard_map/ppermute | solution.py:364
  18.9 1.5 %collective-permute-start.7 = (bf16[256,384]{1,0:T(8,128)(2,1)S(1)}, bf16[256,384]{1,0:T(8,128)(2,1)S(1)}, u32[]{:S(2)}, u32[]{:S(2)}) collective-permute-start(bf16[256,384]{1,0:T(8,128)(2,1)S(1)} %get-tuple-element.117), channel_id=1, source_target_pairs={{0,16},{4,20},{8,24},{12,28},{16,0},{20,4},{24,8},{28,12},{1,17},{... | collective-permute-start | bytes 589832 | tf_op jit(solution)/shard_map/ppermute | solution.py:364
  21.4 1.9 %collective-permute-done.10.refs_3_ = bf16[256,384]{1,0:T(8,128)(2,1)S(1)} collective-permute-done((bf16[256,384]{1,0:T(8,128)(2,1)S(1)}, bf16[256,384]{1,0:T(8,128)(2,1)S(1)}, u32[]{:S(2)}, u32[]{:S(2)}) %collective-permute-start.10) | collective-permute-done | bytes 196640 | tf_op jit(solution)/shard_map/ppermute | solution.py:364
  23.4 1.9 %lag_spectra.1.refs_2_.refs_3_.refs_8_.refs_7_ = f32[5,544,384]{2,1,0:T(8,128)S(1)} custom-call(bf16[256,384]{1,0:T(8,128)(2,1)S(1)} %maximum_select_fusion.refs_0_, bf16[256,384]{1,0:T(8,128)(2,1)S(1)} %collective-permute-done.4.refs_6_.refs_1_, bf16[256,384]{1,0:T(8,128)(2,1)S(1)} %collective-permute-done.5.refs_7_.refs_2_, ...), custom_call_target="tpu_custom_call" | custom-call | flops 10000000000 | tf_op jit(solution)/shard_map/lag_spectra/pallas_call | solution.py:57
  25.3 1.5 %early_first.1 = (f32[544,384]{1,0:T(8,128)S(1)}, f32[544,384]{1,0:T(8,128)S(1)}, bf16[768,1152]{1,0:T(8,128)(2,1)S(1)}) custom-call(bf16[256,384]{1,0:T(8,128)(2,1)S(1)} %get-tuple-element.67.refs_0_.refs_6_, bf16[272,384]{1,0:T(8,128)(2,1)S(1)} %get-tuple-element.65.refs_1_.refs_5_, f32[5,544,384]{2,1,0:T(8,128)S(1)} %lag_spectra.1.refs_2_.refs_3_.refs_8_.refs_7_, ...), custom_call_target="tpu_custom_call" | custom-call | flops 10000000000 | tf_op jit(solution)/shard_map/early_first/pallas_call | solution.py:57
  26.7 1.5 %collective-permute-done.11.refs_2_.refs_1_ = bf16[384,768]{1,0:T(8,128)(2,1)S(1)} collective-permute-done((bf16[384,768]{1,0:T(8,128)(2,1)S(1)}, bf16[384,768]{1,0:T(8,128)(2,1)S(1)}, u32[]{:S(2)}, u32[]{:S(2)}) %collective-permute-start.11) | collective-permute-done | bytes 589856 | tf_op jit(solution)/shard_map/ppermute | solution.py:413
  30.5 3.4 %late_first.1 = (f32[272,768]{1,0:T(8,128)S(1)}, bf16[272,768]{1,0:T(8,128)(2,1)S(1)}, bf16[272,384]{1,0:T(8,128)(2,1)S(1)}) custom-call(bf16[256,384]{1,0:T(8,128)(2,1)S(1)} %collective-permute-done.7.refs_0_, bf16[256,384]{1,0:T(8,128)(2,1)S(1)} %collective-permute-done.8.refs_1_, f32[544,384]{1,0:T(8,128)S(1)} %get-tuple-element.70.refs_2_.refs_3_, ...), custom_call_target="tpu_custom_call" | custom-call | flops 4000000000 | tf_op jit(solution)/shard_map/late_first/pallas_call | solution.py:57
  36.2 1.6 %collective-permute-start.16 = (bf16[272,384]{1,0:T(8,128)(2,1)S(1)}, bf16[272,384]{1,0:T(8,128)(2,1)S(1)}, u32[]{:S(2)}, u32[]{:S(2)}) collective-permute-start(bf16[272,384]{1,0:T(8,128)(2,1)S(1)} %add_convert_fusion.5.refs_1_), channel_id=1, source_target_pairs={{0,1},{1,0},{2,3},{3,2},{4,5},{5,4},{6,7},{7,6},{8,9},{9,8},{10,11... | collective-permute-start | bytes 626696 | tf_op jit(solution)/shard_map/ppermute | solution.py:373
  37.9 5.8 %collective-permute-done.16.refs_0_.refs_1_ = bf16[272,384]{1,0:T(8,128)(2,1)S(1)} collective-permute-done((bf16[272,384]{1,0:T(8,128)(2,1)S(1)}, bf16[272,384]{1,0:T(8,128)(2,1)S(1)}, u32[]{:S(2)}, u32[]{:S(2)}) %collective-permute-start.16) | collective-permute-done | bytes 208928 | tf_op jit(solution)/shard_map/ppermute | solution.py:373
  46.7 2.1 %collective-permute-start.18 = (bf16[128,384]{1,0:T(8,128)(2,1)S(1)}, bf16[128,384]{1,0:T(8,128)(2,1)S(1)}, u32[]{:S(2)}, u32[]{:S(2)}) collective-permute-start(bf16[128,384]{1,0:T(8,128)(2,1)S(1)} %get-tuple-element.83), channel_id=1, source_target_pairs={{0,24},{4,28},{8,16},{12,20},{16,8},{20,12},{24,0},{28,4},{1,25},{... | collective-permute-start | bytes 294920 | tf_op jit(solution)/shard_map/ppermute | solution.py:364
  52.1 1.6 %collective-permute-done.18.refs_1_ = bf16[128,384]{1,0:T(8,128)(2,1)S(1)} collective-permute-done((bf16[128,384]{1,0:T(8,128)(2,1)S(1)}, bf16[128,384]{1,0:T(8,128)(2,1)S(1)}, u32[]{:S(2)}, u32[]{:S(2)}) %collective-permute-start.18) | collective-permute-done | bytes 98336 | tf_op jit(solution)/shard_map/ppermute | solution.py:364
  54.7 2.4 %late.3 = (f32[272,768]{1,0:T(8,128)S(1)}, bf16[272,768]{1,0:T(8,128)(2,1)S(1)}, bf16[272,384]{1,0:T(8,128)(2,1)S(1)}) custom-call(bf16[256,384]{1,0:T(8,128)(2,1)S(1)} %collective-permute-done.17.refs_0_, bf16[128,384]{1,0:T(8,128)(2,1)S(1)} %collective-permute-done.18.refs_1_, bf16[128,384]{1,0:T(8,128)(2,1)S(1)} %collective-permute-done.19.refs_2_, ...), custom_call_target="tpu_custom_call" | custom-call | flops 2500000000 | tf_op jit(solution)/shard_map/late/pallas_call | solution.py:57
  64.2 1.7 %collective-permute-start.28 = (bf16[128,384]{1,0:T(8,128)(2,1)S(1)}, bf16[128,384]{1,0:T(8,128)(2,1)S(1)}, u32[]{:S(2)}, u32[]{:S(2)}) collective-permute-start(bf16[128,384]{1,0:T(8,128)(2,1)S(1)} %get-tuple-element.96), channel_id=1, source_target_pairs={{0,24},{4,28},{8,16},{12,20},{16,8},{20,12},{24,0},{28,4},{1,25},{... | collective-permute-start | bytes 294920 | tf_op jit(solution)/shard_map/ppermute | solution.py:364
  69.1 2.1 %collective-permute-done.27.refs_1_ = bf16[128,384]{1,0:T(8,128)(2,1)S(1)} collective-permute-done((bf16[128,384]{1,0:T(8,128)(2,1)S(1)}, bf16[128,384]{1,0:T(8,128)(2,1)S(1)}, u32[]{:S(2)}, u32[]{:S(2)}) %collective-permute-start.27) | collective-permute-done | bytes 98336 | tf_op jit(solution)/shard_map/ppermute | solution.py:364
  73.0 2.6 %late.4 = (f32[272,768]{1,0:T(8,128)S(1)}, bf16[272,768]{1,0:T(8,128)(2,1)S(1)}, bf16[272,384]{1,0:T(8,128)(2,1)S(1)}) custom-call(bf16[256,384]{1,0:T(8,128)(2,1)S(1)} %collective-permute-done.26.refs_0_, bf16[128,384]{1,0:T(8,128)(2,1)S(1)} %collective-permute-done.27.refs_1_, bf16[128,384]{1,0:T(8,128)(2,1)S(1)} %collective-permute-done.28.refs_2_, ...), custom_call_target="tpu_custom_call" | custom-call | flops 2500000000 | tf_op jit(solution)/shard_map/late/pallas_call | solution.py:57
  77.4 6.8 %collective-permute-start.34 = (bf16[272,384]{1,0:T(8,128)(2,1)S(1)}, bf16[272,384]{1,0:T(8,128)(2,1)S(1)}, u32[]{:S(2)}, u32[]{:S(2)}) collective-permute-start(bf16[272,384]{1,0:T(8,128)(2,1)S(1)} %add_convert_fusion.3.refs_1_), channel_id=1, source_target_pairs={{0,1},{1,0},{2,3},{3,2},{4,5},{5,4},{6,7},{7,6},{8,9},{9,8},{10,11... | collective-permute-start | bytes 626696 | tf_op jit(solution)/shard_map/ppermute | solution.py:373
  84.3 5.6 %collective-permute-done.34.refs_0_.refs_1_ = bf16[272,384]{1,0:T(8,128)(2,1)S(1)} collective-permute-done((bf16[272,384]{1,0:T(8,128)(2,1)S(1)}, bf16[272,384]{1,0:T(8,128)(2,1)S(1)}, u32[]{:S(2)}, u32[]{:S(2)}) %collective-permute-start.34) | collective-permute-done | bytes 208928 | tf_op jit(solution)/shard_map/ppermute | solution.py:373
  91.7 1.7 %collective-permute-start.33 = (bf16[144,768]{1,0:T(8,128)(2,1)S(1)}, bf16[144,768]{1,0:T(8,128)(2,1)S(1)}, u32[]{:S(2)}, u32[]{:S(2)}) collective-permute-start(bf16[144,768]{1,0:T(8,128)(2,1)S(1)} %add_convert_fusion.refs_2_), channel_id=1, source_target_pairs={{0,1},{1,0},{2,3},{3,2},{4,5},{5,4},{6,7},{7,6},{8,9},{9,8},{10,11... | collective-permute-start | bytes 663560 | tf_op jit(solution)/shard_map/ppermute | solution.py:373
  93.5 1.7 %collective-permute-start.36 = (bf16[128,384]{1,0:T(8,128)(2,1)S(1)}, bf16[128,384]{1,0:T(8,128)(2,1)S(1)}, u32[]{:S(2)}, u32[]{:S(2)}) collective-permute-start(bf16[128,384]{1,0:T(8,128)(2,1)S(1)} %get-tuple-element.106), channel_id=1, source_target_pairs={{0,24},{4,28},{8,16},{12,20},{16,8},{20,12},{24,0},{28,4},{1,25},{... | collective-permute-start | bytes 294920 | tf_op jit(solution)/shard_map/ppermute | solution.py:364
  98.3 1.8 %collective-permute-done.36.refs_1_ = bf16[128,384]{1,0:T(8,128)(2,1)S(1)} collective-permute-done((bf16[128,384]{1,0:T(8,128)(2,1)S(1)}, bf16[128,384]{1,0:T(8,128)(2,1)S(1)}, u32[]{:S(2)}, u32[]{:S(2)}) %collective-permute-start.36) | collective-permute-done | bytes 98336 | tf_op jit(solution)/shard_map/ppermute | solution.py:364
  101.2 2.9 %late.5 = (f32[272,768]{1,0:T(8,128)S(1)}, bf16[272,768]{1,0:T(8,128)(2,1)}, bf16[272,384]{1,0:T(8,128)(2,1)S(1)}) custom-call(bf16[256,384]{1,0:T(8,128)(2,1)S(1)} %collective-permute-done.35.refs_0_, bf16[128,384]{1,0:T(8,128)(2,1)S(1)} %collective-permute-done.36.refs_1_, bf16[128,384]{1,0:T(8,128)(2,1)S(1)} %collective-permute-done.37.refs_2_, ...), custom_call_target="tpu_custom_call" | custom-call | flops 2500000000 | tf_op jit(solution)/shard_map/late/pallas_call | solution.py:57
  (114 shorter events, 44.6 us)
Async XLA Ops:
  6.2 9.5 %collective-permute-start = (bf16[128,1152]{1,0:T(8,128)(2,1)}, bf16[128,1152]{1,0:T(8,128)(2,1)S(1)}, u32[]{:S(2)}, u32[]{:S(2)}) collective-permute-start(bf16[128,1152]{1,0:T(8,128)(2,1)} %get-tuple-element.60), channel_id=1, source_target_pairs={{0,4},{4,0},{8,12},{12,8},{16,20},{20,16},{24,28},{28,24},{1,5},{5... | collective-permute-start | bytes 884744 | tf_op jit(solution)/shard_map/ppermute | solution.py:361
  7.3 7.4 %collective-permute-start.4 = (bf16[256,384]{1,0:T(8,128)(2,1)S(1)}, bf16[256,384]{1,0:T(8,128)(2,1)S(1)}, u32[]{:S(2)}, u32[]{:S(2)}) collective-permute-start(bf16[256,384]{1,0:T(8,128)(2,1)S(1)} %maximum_select_fusion.refs_0_), channel_id=1, source_target_pairs={{0,8},{4,12},{8,0},{12,4},{16,24},{20,28},{24,16},{28,20},{1,9},{5... | collective-permute-start | bytes 589832 | tf_op jit(solution)/shard_map/ppermute | solution.py:364
  7.9 7.8 %collective-permute-start.5 = (bf16[256,384]{1,0:T(8,128)(2,1)S(1)}, bf16[256,384]{1,0:T(8,128)(2,1)S(1)}, u32[]{:S(2)}, u32[]{:S(2)}) collective-permute-start(bf16[256,384]{1,0:T(8,128)(2,1)S(1)} %maximum_select_fusion.refs_0_), channel_id=1, source_target_pairs={{0,16},{4,20},{8,24},{12,28},{16,0},{20,4},{24,8},{28,12},{1,17},{... | collective-permute-start | bytes 589832 | tf_op jit(solution)/shard_map/ppermute | solution.py:364
  9.3 7.2 %collective-permute-start.6 = (bf16[128,768]{1,0:T(8,128)(2,1)S(1)}, bf16[128,768]{1,0:T(8,128)(2,1)S(1)}, u32[]{:S(2)}, u32[]{:S(2)}) collective-permute-start(bf16[128,768]{1,0:T(8,128)(2,1)S(1)} %bitcast.23), channel_id=1, source_target_pairs={{0,4},{4,0},{8,12},{12,8},{16,20},{20,16},{24,28},{28,24},{1,5},{5... | collective-permute-start | bytes 589832 | tf_op jit(solution)/shard_map/ppermute | solution.py:361
  10.9 17.3 %collective-permute-start.11 = (bf16[384,768]{1,0:T(8,128)(2,1)S(1)}, bf16[384,768]{1,0:T(8,128)(2,1)S(1)}, u32[]{:S(2)}, u32[]{:S(2)}) collective-permute-start(bf16[384,768]{1,0:T(8,128)(2,1)S(1)} %dynamic-slice_bitcast_fusion), channel_id=1, source_target_pairs={{0,1},{1,2},{2,3},{3,0},{4,5},{5,6},{6,7},{7,4},{8,9},{9,10},{10,1... | collective-permute-start | bytes 1769480 | tf_op jit(solution)/shard_map/ppermute | solution.py:413
  14.7 8.7 %collective-permute-start.10 = (bf16[256,384]{1,0:T(8,128)(2,1)S(1)}, bf16[256,384]{1,0:T(8,128)(2,1)S(1)}, u32[]{:S(2)}, u32[]{:S(2)}) collective-permute-start(bf16[256,384]{1,0:T(8,128)(2,1)S(1)} %maximum_select_fusion.refs_0_), channel_id=1, source_target_pairs={{0,24},{4,28},{8,16},{12,20},{16,8},{20,12},{24,0},{28,4},{1,25},{... | collective-permute-start | bytes 589832 | tf_op jit(solution)/shard_map/ppermute | solution.py:364
  17.9 10.3 %collective-permute-start.9 = (bf16[256,384]{1,0:T(8,128)(2,1)S(1)}, bf16[256,384]{1,0:T(8,128)(2,1)S(1)}, u32[]{:S(2)}, u32[]{:S(2)}) collective-permute-start(bf16[256,384]{1,0:T(8,128)(2,1)S(1)} %get-tuple-element.115), channel_id=1, source_target_pairs={{0,8},{4,12},{8,0},{12,4},{16,24},{20,28},{24,16},{28,20},{1,9},{5... | collective-permute-start | bytes 589832 | tf_op jit(solution)/shard_map/ppermute | solution.py:364
  18.9 10.2 %collective-permute-start.7 = (bf16[256,384]{1,0:T(8,128)(2,1)S(1)}, bf16[256,384]{1,0:T(8,128)(2,1)S(1)}, u32[]{:S(2)}, u32[]{:S(2)}) collective-permute-start(bf16[256,384]{1,0:T(8,128)(2,1)S(1)} %get-tuple-element.117), channel_id=1, source_target_pairs={{0,16},{4,20},{8,24},{12,28},{16,0},{20,4},{24,8},{28,12},{1,17},{... | collective-permute-start | bytes 589832 | tf_op jit(solution)/shard_map/ppermute | solution.py:364
  20.4 10.1 %collective-permute-start.8 = (bf16[256,384]{1,0:T(8,128)(2,1)S(1)}, bf16[256,384]{1,0:T(8,128)(2,1)S(1)}, u32[]{:S(2)}, u32[]{:S(2)}) collective-permute-start(bf16[256,384]{1,0:T(8,128)(2,1)S(1)} %get-tuple-element.116), channel_id=1, source_target_pairs={{0,24},{4,28},{8,16},{12,20},{16,8},{20,12},{24,0},{28,4},{1,25},{... | collective-permute-start | bytes 589832 | tf_op jit(solution)/shard_map/ppermute | solution.py:364
  36.2 7.4 %collective-permute-start.16 = (bf16[272,384]{1,0:T(8,128)(2,1)S(1)}, bf16[272,384]{1,0:T(8,128)(2,1)S(1)}, u32[]{:S(2)}, u32[]{:S(2)}) collective-permute-start(bf16[272,384]{1,0:T(8,128)(2,1)S(1)} %add_convert_fusion.5.refs_1_), channel_id=1, source_target_pairs={{0,1},{1,0},{2,3},{3,2},{4,5},{5,4},{6,7},{7,6},{8,9},{9,8},{10,11... | collective-permute-start | bytes 626696 | tf_op jit(solution)/shard_map/ppermute | solution.py:373
  43.7 7.8 %collective-permute-start.20 = (bf16[256,384]{1,0:T(8,128)(2,1)S(1)}, bf16[256,384]{1,0:T(8,128)(2,1)S(1)}, u32[]{:S(2)}, u32[]{:S(2)}) collective-permute-start(bf16[256,384]{1,0:T(8,128)(2,1)S(1)} %get-tuple-element.82.refs_0_.refs_5_), channel_id=1, source_target_pairs={{0,8},{4,12},{8,0},{12,4},{16,24},{20,28},{24,16},{28,20},{1,9},{5... | collective-permute-start | bytes 589832 | tf_op jit(solution)/shard_map/ppermute | solution.py:364
  44.4 10.3 %collective-permute-start.17 = (bf16[256,384]{1,0:T(8,128)(2,1)S(1)}, bf16[256,384]{1,0:T(8,128)(2,1)S(1)}, u32[]{:S(2)}, u32[]{:S(2)}) collective-permute-start(bf16[256,384]{1,0:T(8,128)(2,1)S(1)} %get-tuple-element.82.refs_0_.refs_5_), channel_id=1, source_target_pairs={{0,16},{4,20},{8,24},{12,28},{16,0},{20,4},{24,8},{28,12},{1,17},{... | collective-permute-start | bytes 589832 | tf_op jit(solution)/shard_map/ppermute | solution.py:364
  46.7 6.9 %collective-permute-start.18 = (bf16[128,384]{1,0:T(8,128)(2,1)S(1)}, bf16[128,384]{1,0:T(8,128)(2,1)S(1)}, u32[]{:S(2)}, u32[]{:S(2)}) collective-permute-start(bf16[128,384]{1,0:T(8,128)(2,1)S(1)} %get-tuple-element.83), channel_id=1, source_target_pairs={{0,24},{4,28},{8,16},{12,20},{16,8},{20,12},{24,0},{28,4},{1,25},{... | collective-permute-start | bytes 294920 | tf_op jit(solution)/shard_map/ppermute | solution.py:364
  60.6 7.8 %collective-permute-start.29 = (bf16[256,384]{1,0:T(8,128)(2,1)S(1)}, bf16[256,384]{1,0:T(8,128)(2,1)S(1)}, u32[]{:S(2)}, u32[]{:S(2)}) collective-permute-start(bf16[256,384]{1,0:T(8,128)(2,1)S(1)} %get-tuple-element.94.refs_0_.refs_5_), channel_id=1, source_target_pairs={{0,8},{4,12},{8,0},{12,4},{16,24},{20,28},{24,16},{28,20},{1,9},{5... | collective-permute-start | bytes 589832 | tf_op jit(solution)/shard_map/ppermute | solution.py:364
  62.0 10.9 %collective-permute-start.26 = (bf16[256,384]{1,0:T(8,128)(2,1)S(1)}, bf16[256,384]{1,0:T(8,128)(2,1)S(1)}, u32[]{:S(2)}, u32[]{:S(2)}) collective-permute-start(bf16[256,384]{1,0:T(8,128)(2,1)S(1)} %get-tuple-element.94.refs_0_.refs_5_), channel_id=1, source_target_pairs={{0,16},{4,20},{8,24},{12,28},{16,0},{20,4},{24,8},{28,12},{1,17},{... | collective-permute-start | bytes 589832 | tf_op jit(solution)/shard_map/ppermute | solution.py:364
  63.0 8.2 %collective-permute-start.27 = (bf16[128,384]{1,0:T(8,128)(2,1)S(1)}, bf16[128,384]{1,0:T(8,128)(2,1)S(1)}, u32[]{:S(2)}, u32[]{:S(2)}) collective-permute-start(bf16[128,384]{1,0:T(8,128)(2,1)S(1)} %get-tuple-element.95), channel_id=1, source_target_pairs={{0,24},{4,28},{8,16},{12,20},{16,8},{20,12},{24,0},{28,4},{1,25},{... | collective-permute-start | bytes 294920 | tf_op jit(solution)/shard_map/ppermute | solution.py:364
  64.2 8.4 %collective-permute-start.28 = (bf16[128,384]{1,0:T(8,128)(2,1)S(1)}, bf16[128,384]{1,0:T(8,128)(2,1)S(1)}, u32[]{:S(2)}, u32[]{:S(2)}) collective-permute-start(bf16[128,384]{1,0:T(8,128)(2,1)S(1)} %get-tuple-element.96), channel_id=1, source_target_pairs={{0,24},{4,28},{8,16},{12,20},{16,8},{20,12},{24,0},{28,4},{1,25},{... | collective-permute-start | bytes 294920 | tf_op jit(solution)/shard_map/ppermute | solution.py:364
  69.0 6.7 %collective-permute-start.30 = (bf16[144,768]{1,0:T(8,128)(2,1)S(1)}, bf16[144,768]{1,0:T(8,128)(2,1)S(1)}, u32[]{:S(2)}, u32[]{:S(2)}) collective-permute-start(bf16[144,768]{1,0:T(8,128)(2,1)S(1)} %collective-permute-done.24.refs_0_), channel_id=1, source_target_pairs={{0,4},{4,0},{8,12},{12,8},{16,20},{20,16},{24,28},{28,24},{1,5},{5... | collective-permute-start | bytes 663560 | tf_op jit(solution)/shard_map/ppermute | solution.py:361
  77.2 7.0 %collective-permute-start.32 = (bf16[144,768]{1,0:T(8,128)(2,1)S(1)}, bf16[144,768]{1,0:T(8,128)(2,1)S(1)}, u32[]{:S(2)}, u32[]{:S(2)}) collective-permute-start(bf16[144,768]{1,0:T(8,128)(2,1)S(1)} %get-tuple-element.104), channel_id=1, source_target_pairs={{0,4},{4,0},{8,12},{12,8},{16,20},{20,16},{24,28},{28,24},{1,5},{5... | collective-permute-start | bytes 663560 | tf_op jit(solution)/shard_map/ppermute | solution.py:361
  77.4 12.4 %collective-permute-start.34 = (bf16[272,384]{1,0:T(8,128)(2,1)S(1)}, bf16[272,384]{1,0:T(8,128)(2,1)S(1)}, u32[]{:S(2)}, u32[]{:S(2)}) collective-permute-start(bf16[272,384]{1,0:T(8,128)(2,1)S(1)} %add_convert_fusion.3.refs_1_), channel_id=1, source_target_pairs={{0,1},{1,0},{2,3},{3,2},{4,5},{5,4},{6,7},{7,6},{8,9},{9,8},{10,11... | collective-permute-start | bytes 626696 | tf_op jit(solution)/shard_map/ppermute | solution.py:373
  89.9 7.9 %collective-permute-start.38 = (bf16[256,384]{1,0:T(8,128)(2,1)S(1)}, bf16[256,384]{1,0:T(8,128)(2,1)S(1)}, u32[]{:S(2)}, u32[]{:S(2)}) collective-permute-start(bf16[256,384]{1,0:T(8,128)(2,1)S(1)} %get-tuple-element.105.refs_0_.refs_5_), channel_id=1, source_target_pairs={{0,8},{4,12},{8,0},{12,4},{16,24},{20,28},{24,16},{28,20},{1,9},{5... | collective-permute-start | bytes 589832 | tf_op jit(solution)/shard_map/ppermute | solution.py:364
  90.6 10.5 %collective-permute-start.35 = (bf16[256,384]{1,0:T(8,128)(2,1)S(1)}, bf16[256,384]{1,0:T(8,128)(2,1)S(1)}, u32[]{:S(2)}, u32[]{:S(2)}) collective-permute-start(bf16[256,384]{1,0:T(8,128)(2,1)S(1)} %get-tuple-element.105.refs_0_.refs_5_), channel_id=1, source_target_pairs={{0,16},{4,20},{8,24},{12,28},{16,0},{20,4},{24,8},{28,12},{1,17},{... | collective-permute-start | bytes 589832 | tf_op jit(solution)/shard_map/ppermute | solution.py:364
  91.7 12.5 %collective-permute-start.33 = (bf16[144,768]{1,0:T(8,128)(2,1)S(1)}, bf16[144,768]{1,0:T(8,128)(2,1)S(1)}, u32[]{:S(2)}, u32[]{:S(2)}) collective-permute-start(bf16[144,768]{1,0:T(8,128)(2,1)S(1)} %add_convert_fusion.refs_2_), channel_id=1, source_target_pairs={{0,1},{1,0},{2,3},{3,2},{4,5},{5,4},{6,7},{7,6},{8,9},{9,8},{10,11... | collective-permute-start | bytes 663560 | tf_op jit(solution)/shard_map/ppermute | solution.py:373
  93.5 6.6 %collective-permute-start.36 = (bf16[128,384]{1,0:T(8,128)(2,1)S(1)}, bf16[128,384]{1,0:T(8,128)(2,1)S(1)}, u32[]{:S(2)}, u32[]{:S(2)}) collective-permute-start(bf16[128,384]{1,0:T(8,128)(2,1)S(1)} %get-tuple-element.106), channel_id=1, source_target_pairs={{0,24},{4,28},{8,16},{12,20},{16,8},{20,12},{24,0},{28,4},{1,25},{... | collective-permute-start | bytes 294920 | tf_op jit(solution)/shard_map/ppermute | solution.py:364
  (25 other events, 130.2 us)

commit v6 on v5

--- a/solution.py
+++ b/solution.py
@@ -79,7 +79,7 @@
     rim[:, 3 * width :] = grad[edge]
 
 
-def mix_stored(place, stored, stored_core, rim_own, rim_core, grad, taps, _, __, query, keys, values, product, grad_ext, padded):
+def mix_stored(place, stored, stored_core, rim_own, rim_core, grad, taps, _, __, ___, query, keys, values, product, grad_ext, padded):
     core = place[1]
     own, width = grad.shape
     rows = 2 * own
@@ -120,7 +120,7 @@
     out[count] = jnp.zeros(out.shape[1:], f32)
 
 
-def gate_grad(place, g_own, g_core, w_out, query, block, upper, lower, rim, d_out):
+def gate_grad(place, g_own, g_core, w_out, query, block, rim, d_out):
     core = place[1]
     rows, chans = block.shape
     own = rows // 2
@@ -129,10 +129,7 @@
     d_out[side_rows(core, own)] = wide[:own]
     d_out[rows:] = wide[own:]
     d_out[side_rows(1 - core, own)] = dot_last(g_core[0:own], weight)
-    upper[...] = (d_out[0:own] * query[0:own]).astype(bf16)
-    lower[...] = (d_out[own:rows] * query[own:rows]).astype(bf16)
-    block[0:own] = upper[...]
-    block[own:rows] = lower[...]
+    block[...] = (d_out[0:rows] * query[0:rows]).astype(bf16)
     rim[...] = (d_out[rows:] * query[rows:]).astype(bf16)
 
 
@@ -289,16 +286,17 @@
 def late(place, count, n_got, final, *refs):
     got, refs = refs[:n_got], refs[n_got:]
     start, part_share, block, rim, lag_ref, table, inverse, keys, values, bias, taps, w_in, below_core = refs[:13]
-    share, short_share, pass_on, spec, total, mixed, proj, side = refs[13:]
+    if final:
+        share, spec, total, mixed, proj, side, short_share = refs[13:]
+    else:
+        share, short_share, pass_on, spec, total, mixed, proj, side = refs[13:]
     _, pairs = late_pairs(place, count, got, spec, table, side)
     accumulate(lag_ref, pairs, True, start, total)
     gated_part(
         place, count, total, inverse, block, rim, keys, values, bias, taps, mixed, proj, w_in, part_share, share,
         short_share,
     )
-    if final:
-        pass_on[...] = jnp.zeros(pass_on.shape, bf16)
-    else:
+    if not final:
         pass_half(place, short_share, below_core, pass_on)
 
 
@@ -399,7 +397,7 @@
         [shape(ext, f32), shape(ext, f32), shape(ext, f32), shape(ext, bf16), shape(own_rows + PAD, bf16, width)],
         [pltpu.VMEM((rows + 2 * PAD, chans), f32)],
         "mix_stored", 1.3,
-        stored, stored_core, rim_own, rim_core, grad, taps, pieces[1], pieces[2],
+        stored, stored_core, rim_own, rim_core, grad, taps, pieces[1], pieces[2], weight_out,
     )
     spectra = run(
         lambda place, *refs: lag_spectra(place, chips, *refs),
@@ -435,8 +433,8 @@
         first, final = turn == 0, turn == section_count - 1
         upper = section_count - 1 - turn
         if first:
-            block, upper_half, lower_half, rim, d_out = run(
-                gate_grad, gates + [shape(ext, f32)], [], "gate_grad", 1.0, grad, grad_core, weight_out, query
+            block, rim, d_out = run(
+                gate_grad, [gates[0], gates[-1], shape(ext, f32)], [], "gate_grad", 1.0, grad, grad_core, weight_out, query
             )
         else:
             block, upper_half, lower_half, rim = run(gate_only, gates, [], "gate_only", 0.3, d_out, query, ready)
@@ -482,15 +480,19 @@
                 lambda place, *refs: middle(place, chips, ms, *refs),
                 total_wide, [specs], "middle", 0.8, *soon, start, spectra, table,
             )
-            share, short_share, pass_on = run(
+            scratch = [late_specs, total_scratch, mixed, proj, side]
+            answer = run(
                 lambda place, *refs, final=final: late(place, chips, len(last), final, *refs),
-                late_outs + [shape(ext, bf16)], [late_specs, total_scratch, mixed, proj, side], "late", 2.5,
+                late_outs[:1] if final else late_outs + [shape(ext, bf16)],
+                scratch + [pltpu.VMEM((ext, width), bf16)] if final else scratch, "late", 2.5,
                 *last, start, part_share, block, rim, spectra, table, inverse, keys, values, bias, taps, weight_own,
                 below_core,
             )
+            share = answer[0]
             if not final:
+                short_share, pass_on = answer[1:]
                 carried = run(carry_grad, shape(ext, f32), [], "carry_grad", 0.5, grad, grad_core, below, pass_on)
-        half = pass_on
+        half = share if final else pass_on
         if not final:
             keep = run(keep_half, shape(ext, f32), [], "keep_half", 0.6, short_share, below, carried)
             half = (keep + swap_core(pass_on).astype(f32)).astype(bf16)

time: 107 us -> 106 us (level)
  Pallas kernels: 28 us -> 26.6 us
    pallas_call x30, Pallas kernels: 28 us -> 26.6 us  [call(): pl.pallas_call(placed, out_shape=outs, in_specs=[vmem] * len(operands), o...]
  transfers between devices with their start and end apart: 40 -> 40, of which waited for: 23 -> 25; matrix products, arithmetic and copies ran while one was open for 1% -> 1% of each run, Pallas kernels for 24% -> 22%
where the time goes in v6:
time: 106 us
  starting transfers between devices  40 us (38%)
  waiting for transfers between devices  36.4 us (34%)
  Pallas kernels  26.6 us (25%)
  other arithmetic  2.34 us (2%)
    pallas_call x30, Pallas kernels, call(): pl.pallas_call(placed, out_shape=outs, in_specs=[vmem] * len(operands), o...  26.6 us
    ppermute x18, starting transfers between devices, swap_chip(): lax.ppermute(value, 'seq', [(i, (i // 2 ^ m) * 2 + i % 2) for i in range(...  21.1 us
    ppermute x18, waiting for transfers between devices, swap_chip(): lax.ppermute(value, 'seq', [(i, (i // 2 ^ m) * 2 + i % 2) for i in range(...  18.2 us
    ppermute x6, starting transfers between devices, swap_section(): return lax.ppermute(value, ('seq', 'section'), pairs)  11.8 us
    ppermute x6, waiting for transfers between devices, swap_section(): return lax.ppermute(value, ('seq', 'section'), pairs)  11.6 us
    ppermute x14, waiting for transfers between devices, swap_core(): return lax.ppermute(value, 'seq', [(i, i ^ 1) for i in range(seq_count)])  5.11 us
    ppermute x1, starting transfers between devices, shards(): lax.ppermute(rim_send, 'seq', rim_pairs + [(b, a) for a, b in rim_pairs])  3.56 us
  transfers between devices with their start and end apart: 40, of which 25 were waited for; matrix products, arithmetic and copies ran while one was open for 1% of the time, Pallas kernels for 22%

profile of v6, /device:TPU:0, one launch (start us, length us, event | category | flops | bytes accessed | tf_op | source)
XLA Modules:
  0.0 105.7 jit_solution(3179880688880158164)
XLA Ops:
  0.0 2.2 %split_inputs.1 = (bf16[128,384]{1,0:T(8,128)(2,1)}, bf16[128,384]{1,0:T(8,128)(2,1)}, bf16[128,1152]{1,0:T(8,128)(2,1)}, bf16[16,3072]{1,0:T(8,128)(2,1)}) custom-call(f32[128,768]{1,0:T(8,128)} %bitcast.26, bf16[128,2304]{1,0:T(8,128)(2,1)} %bitcast.21, bf16[128,768]{1,0:T(8,128)(2,1)} %bitcast.23), custom_call_target="tpu_custom_call" | custom-call | flops 1000000000 | tf_op jit(solution)/shard_map/split_inputs/pallas_call | solution.py:57
  2.7 3.6 %collective-permute-start.1 = (bf16[16,3072]{1,0:T(8,128)(2,1)}, bf16[16,3072]{1,0:T(8,128)(2,1)S(1)}, u32[]{:S(2)}, u32[]{:S(2)}) collective-permute-start(bf16[16,3072]{1,0:T(8,128)(2,1)} %get-tuple-element.59), channel_id=1, source_target_pairs={{4,8},{12,16},{20,24},{28,0},{8,4},{16,12},{24,20},{0,28},{5,9},{1... | collective-permute-start | bytes 294920 | tf_op jit(solution)/shard_map/ppermute | solution.py:387
  10.9 1.6 %collective-permute-start.11 = (bf16[384,768]{1,0:T(8,128)(2,1)S(1)}, bf16[384,768]{1,0:T(8,128)(2,1)S(1)}, u32[]{:S(2)}, u32[]{:S(2)}) collective-permute-start(bf16[384,768]{1,0:T(8,128)(2,1)S(1)} %dynamic-slice_bitcast_fusion), channel_id=1, source_target_pairs={{0,1},{1,2},{2,3},{3,0},{4,5},{5,6},{6,7},{7,4},{8,9},{9,10},{10,1... | collective-permute-start | bytes 1769480 | tf_op jit(solution)/shard_map/ppermute | solution.py:411
  12.5 2.2 %collective-permute-done.4.refs_6_.refs_1_ = bf16[256,384]{1,0:T(8,128)(2,1)S(1)} collective-permute-done((bf16[256,384]{1,0:T(8,128)(2,1)S(1)}, bf16[256,384]{1,0:T(8,128)(2,1)S(1)}, u32[]{:S(2)}, u32[]{:S(2)}) %collective-permute-start.4) | collective-permute-done | bytes 196640 | tf_op jit(solution)/shard_map/ppermute | solution.py:362
  18.2 1.5 %collective-permute-start.7 = (bf16[256,384]{1,0:T(8,128)(2,1)S(1)}, bf16[256,384]{1,0:T(8,128)(2,1)S(1)}, u32[]{:S(2)}, u32[]{:S(2)}) collective-permute-start(bf16[256,384]{1,0:T(8,128)(2,1)S(1)} %get-tuple-element.113), channel_id=1, source_target_pairs={{0,16},{4,20},{8,24},{12,28},{16,0},{20,4},{24,8},{28,12},{1,17},{... | collective-permute-start | bytes 589832 | tf_op jit(solution)/shard_map/ppermute | solution.py:362
  20.7 2.6 %collective-permute-done.10.refs_3_ = bf16[256,384]{1,0:T(8,128)(2,1)S(1)} collective-permute-done((bf16[256,384]{1,0:T(8,128)(2,1)S(1)}, bf16[256,384]{1,0:T(8,128)(2,1)S(1)}, u32[]{:S(2)}, u32[]{:S(2)}) %collective-permute-start.10) | collective-permute-done | bytes 196640 | tf_op jit(solution)/shard_map/ppermute | solution.py:362
  23.4 1.9 %lag_spectra.1.refs_2_.refs_3_.refs_8_.refs_7_ = f32[5,544,384]{2,1,0:T(8,128)S(1)} custom-call(bf16[256,384]{1,0:T(8,128)(2,1)S(1)} %maximum_select_fusion.refs_0_, bf16[256,384]{1,0:T(8,128)(2,1)S(1)} %collective-permute-done.4.refs_6_.refs_1_, bf16[256,384]{1,0:T(8,128)(2,1)S(1)} %collective-permute-done.5.refs_7_.refs_2_, ...), custom_call_target="tpu_custom_call" | custom-call | flops 10000000000 | tf_op jit(solution)/shard_map/lag_spectra/pallas_call | solution.py:57
  26.7 1.5 %collective-permute-done.11.refs_2_.refs_1_ = bf16[384,768]{1,0:T(8,128)(2,1)S(1)} collective-permute-done((bf16[384,768]{1,0:T(8,128)(2,1)S(1)}, bf16[384,768]{1,0:T(8,128)(2,1)S(1)}, u32[]{:S(2)}, u32[]{:S(2)}) %collective-permute-start.11) | collective-permute-done | bytes 589856 | tf_op jit(solution)/shard_map/ppermute | solution.py:411
  30.5 3.4 %late_first.1 = (f32[272,768]{1,0:T(8,128)S(1)}, bf16[272,768]{1,0:T(8,128)(2,1)S(1)}, bf16[272,384]{1,0:T(8,128)(2,1)S(1)}) custom-call(bf16[256,384]{1,0:T(8,128)(2,1)S(1)} %collective-permute-done.7.refs_0_, bf16[256,384]{1,0:T(8,128)(2,1)S(1)} %collective-permute-done.8.refs_1_, f32[544,384]{1,0:T(8,128)S(1)} %get-tuple-element.68.refs_2_.refs_3_, ...), custom_call_target="tpu_custom_call" | custom-call | flops 4000000000 | tf_op jit(solution)/shard_map/late_first/pallas_call | solution.py:57
  36.2 1.6 %collective-permute-start.16 = (bf16[272,384]{1,0:T(8,128)(2,1)S(1)}, bf16[272,384]{1,0:T(8,128)(2,1)S(1)}, u32[]{:S(2)}, u32[]{:S(2)}) collective-permute-start(bf16[272,384]{1,0:T(8,128)(2,1)S(1)} %add_convert_fusion.5.refs_1_), channel_id=1, source_target_pairs={{0,1},{1,0},{2,3},{3,2},{4,5},{5,4},{6,7},{7,6},{8,9},{9,8},{10,11... | collective-permute-start | bytes 626696 | tf_op jit(solution)/shard_map/ppermute | solution.py:371
  37.9 5.8 %collective-permute-done.16.refs_0_.refs_1_ = bf16[272,384]{1,0:T(8,128)(2,1)S(1)} collective-permute-done((bf16[272,384]{1,0:T(8,128)(2,1)S(1)}, bf16[272,384]{1,0:T(8,128)(2,1)S(1)}, u32[]{:S(2)}, u32[]{:S(2)}) %collective-permute-start.16) | collective-permute-done | bytes 208928 | tf_op jit(solution)/shard_map/ppermute | solution.py:371
  46.8 2.0 %collective-permute-start.18 = (bf16[128,384]{1,0:T(8,128)(2,1)S(1)}, bf16[128,384]{1,0:T(8,128)(2,1)S(1)}, u32[]{:S(2)}, u32[]{:S(2)}) collective-permute-start(bf16[128,384]{1,0:T(8,128)(2,1)S(1)} %get-tuple-element.81), channel_id=1, source_target_pairs={{0,24},{4,28},{8,16},{12,20},{16,8},{20,12},{24,0},{28,4},{1,25},{... | collective-permute-start | bytes 294920 | tf_op jit(solution)/shard_map/ppermute | solution.py:362
  54.7 2.4 %late.3 = (f32[272,768]{1,0:T(8,128)S(1)}, bf16[272,768]{1,0:T(8,128)(2,1)S(1)}, bf16[272,384]{1,0:T(8,128)(2,1)S(1)}) custom-call(bf16[256,384]{1,0:T(8,128)(2,1)S(1)} %collective-permute-done.17.refs_0_, bf16[128,384]{1,0:T(8,128)(2,1)S(1)} %collective-permute-done.18.refs_1_, bf16[128,384]{1,0:T(8,128)(2,1)S(1)} %collective-permute-done.19.refs_2_, ...), custom_call_target="tpu_custom_call" | custom-call | flops 2500000000 | tf_op jit(solution)/shard_map/late/pallas_call | solution.py:57
  60.6 1.5 %collective-permute-start.29 = (bf16[256,384]{1,0:T(8,128)(2,1)S(1)}, bf16[256,384]{1,0:T(8,128)(2,1)S(1)}, u32[]{:S(2)}, u32[]{:S(2)}) collective-permute-start(bf16[256,384]{1,0:T(8,128)(2,1)S(1)} %get-tuple-element.92.refs_0_.refs_5_), channel_id=1, source_target_pairs={{0,8},{4,12},{8,0},{12,4},{16,24},{20,28},{24,16},{28,20},{1,9},{5... | collective-permute-start | bytes 589832 | tf_op jit(solution)/shard_map/ppermute | solution.py:362
  62.7 1.5 %collective-permute-start.27 = (bf16[128,384]{1,0:T(8,128)(2,1)S(1)}, bf16[128,384]{1,0:T(8,128)(2,1)S(1)}, u32[]{:S(2)}, u32[]{:S(2)}) collective-permute-start(bf16[128,384]{1,0:T(8,128)(2,1)S(1)} %get-tuple-element.93), channel_id=1, source_target_pairs={{0,24},{4,28},{8,16},{12,20},{16,8},{20,12},{24,0},{28,4},{1,25},{... | collective-permute-start | bytes 294920 | tf_op jit(solution)/shard_map/ppermute | solution.py:362
  66.7 1.7 %collective-permute-done.29.refs_0_ = bf16[256,384]{1,0:T(8,128)(2,1)S(1)} collective-permute-done((bf16[256,384]{1,0:T(8,128)(2,1)S(1)}, bf16[256,384]{1,0:T(8,128)(2,1)S(1)}, u32[]{:S(2)}, u32[]{:S(2)}) %collective-permute-start.29) | collective-permute-done | bytes 196640 | tf_op jit(solution)/shard_map/ppermute | solution.py:362
  69.1 2.1 %collective-permute-done.27.refs_1_ = bf16[128,384]{1,0:T(8,128)(2,1)S(1)} collective-permute-done((bf16[128,384]{1,0:T(8,128)(2,1)S(1)}, bf16[128,384]{1,0:T(8,128)(2,1)S(1)}, u32[]{:S(2)}, u32[]{:S(2)}) %collective-permute-start.27) | collective-permute-done | bytes 98336 | tf_op jit(solution)/shard_map/ppermute | solution.py:362
  73.0 2.6 %late.4 = (f32[272,768]{1,0:T(8,128)S(1)}, bf16[272,768]{1,0:T(8,128)(2,1)S(1)}, bf16[272,384]{1,0:T(8,128)(2,1)S(1)}) custom-call(bf16[256,384]{1,0:T(8,128)(2,1)S(1)} %collective-permute-done.26.refs_0_, bf16[128,384]{1,0:T(8,128)(2,1)S(1)} %collective-permute-done.27.refs_1_, bf16[128,384]{1,0:T(8,128)(2,1)S(1)} %collective-permute-done.28.refs_2_, ...), custom_call_target="tpu_custom_call" | custom-call | flops 2500000000 | tf_op jit(solution)/shard_map/late/pallas_call | solution.py:57
  77.4 6.8 %collective-permute-start.34 = (bf16[272,384]{1,0:T(8,128)(2,1)S(1)}, bf16[272,384]{1,0:T(8,128)(2,1)S(1)}, u32[]{:S(2)}, u32[]{:S(2)}) collective-permute-start(bf16[272,384]{1,0:T(8,128)(2,1)S(1)} %add_convert_fusion.3.refs_1_), channel_id=1, source_target_pairs={{0,1},{1,0},{2,3},{3,2},{4,5},{5,4},{6,7},{7,6},{8,9},{9,8},{10,11... | collective-permute-start | bytes 626696 | tf_op jit(solution)/shard_map/ppermute | solution.py:371
  84.3 5.6 %collective-permute-done.34.refs_0_.refs_1_ = bf16[272,384]{1,0:T(8,128)(2,1)S(1)} collective-permute-done((bf16[272,384]{1,0:T(8,128)(2,1)S(1)}, bf16[272,384]{1,0:T(8,128)(2,1)S(1)}, u32[]{:S(2)}, u32[]{:S(2)}) %collective-permute-start.34) | collective-permute-done | bytes 208928 | tf_op jit(solution)/shard_map/ppermute | solution.py:371
  91.8 1.7 %collective-permute-start.33 = (bf16[144,768]{1,0:T(8,128)(2,1)S(1)}, bf16[144,768]{1,0:T(8,128)(2,1)S(1)}, u32[]{:S(2)}, u32[]{:S(2)}) collective-permute-start(bf16[144,768]{1,0:T(8,128)(2,1)S(1)} %add_convert_fusion.refs_2_), channel_id=1, source_target_pairs={{0,1},{1,0},{2,3},{3,2},{4,5},{5,4},{6,7},{7,6},{8,9},{9,8},{10,11... | collective-permute-start | bytes 663560 | tf_op jit(solution)/shard_map/ppermute | solution.py:371
  93.5 1.7 %collective-permute-start.36 = (bf16[128,384]{1,0:T(8,128)(2,1)S(1)}, bf16[128,384]{1,0:T(8,128)(2,1)S(1)}, u32[]{:S(2)}, u32[]{:S(2)}) collective-permute-start(bf16[128,384]{1,0:T(8,128)(2,1)S(1)} %get-tuple-element.104), channel_id=1, source_target_pairs={{0,24},{4,28},{8,16},{12,20},{16,8},{20,12},{24,0},{28,4},{1,25},{... | collective-permute-start | bytes 294920 | tf_op jit(solution)/shard_map/ppermute | solution.py:362
  98.4 1.5 %collective-permute-done.36.refs_1_ = bf16[128,384]{1,0:T(8,128)(2,1)S(1)} collective-permute-done((bf16[128,384]{1,0:T(8,128)(2,1)S(1)}, bf16[128,384]{1,0:T(8,128)(2,1)S(1)}, u32[]{:S(2)}, u32[]{:S(2)}) %collective-permute-start.36) | collective-permute-done | bytes 98336 | tf_op jit(solution)/shard_map/ppermute | solution.py:362
  101.2 2.1 %late.5.refs_0_.refs_1_ = f32[272,768]{1,0:T(8,128)S(1)} custom-call(bf16[256,384]{1,0:T(8,128)(2,1)S(1)} %collective-permute-done.35.refs_0_, bf16[128,384]{1,0:T(8,128)(2,1)S(1)} %collective-permute-done.36.refs_1_, bf16[128,384]{1,0:T(8,128)(2,1)S(1)} %collective-permute-done.37.refs_2_, f32[544,384]{1,0:T(8,128)S(1)} %middle.5.refs_3_, ...), custom_call_target="tpu_custom_call" | custom-call | flops 2500000000 | tf_op jit(solution)/shard_map/late/pallas_call | solution.py:57
  (114 shorter events, 44.3 us)
Async XLA Ops:
  2.7 6.6 %collective-permute-start.1 = (bf16[16,3072]{1,0:T(8,128)(2,1)}, bf16[16,3072]{1,0:T(8,128)(2,1)S(1)}, u32[]{:S(2)}, u32[]{:S(2)}) collective-permute-start(bf16[16,3072]{1,0:T(8,128)(2,1)} %get-tuple-element.59), channel_id=1, source_target_pairs={{4,8},{12,16},{20,24},{28,0},{8,4},{16,12},{24,20},{0,28},{5,9},{1... | collective-permute-start | bytes 294920 | tf_op jit(solution)/shard_map/ppermute | solution.py:387
  6.2 9.5 %collective-permute-start = (bf16[128,1152]{1,0:T(8,128)(2,1)}, bf16[128,1152]{1,0:T(8,128)(2,1)S(1)}, u32[]{:S(2)}, u32[]{:S(2)}) collective-permute-start(bf16[128,1152]{1,0:T(8,128)(2,1)} %get-tuple-element.58), channel_id=1, source_target_pairs={{0,4},{4,0},{8,12},{12,8},{16,20},{20,16},{24,28},{28,24},{1,5},{5... | collective-permute-start | bytes 884744 | tf_op jit(solution)/shard_map/ppermute | solution.py:359
  7.3 7.4 %collective-permute-start.4 = (bf16[256,384]{1,0:T(8,128)(2,1)S(1)}, bf16[256,384]{1,0:T(8,128)(2,1)S(1)}, u32[]{:S(2)}, u32[]{:S(2)}) collective-permute-start(bf16[256,384]{1,0:T(8,128)(2,1)S(1)} %maximum_select_fusion.refs_0_), channel_id=1, source_target_pairs={{0,8},{4,12},{8,0},{12,4},{16,24},{20,28},{24,16},{28,20},{1,9},{5... | collective-permute-start | bytes 589832 | tf_op jit(solution)/shard_map/ppermute | solution.py:362
  7.9 7.8 %collective-permute-start.5 = (bf16[256,384]{1,0:T(8,128)(2,1)S(1)}, bf16[256,384]{1,0:T(8,128)(2,1)S(1)}, u32[]{:S(2)}, u32[]{:S(2)}) collective-permute-start(bf16[256,384]{1,0:T(8,128)(2,1)S(1)} %maximum_select_fusion.refs_0_), channel_id=1, source_target_pairs={{0,16},{4,20},{8,24},{12,28},{16,0},{20,4},{24,8},{28,12},{1,17},{... | collective-permute-start | bytes 589832 | tf_op jit(solution)/shard_map/ppermute | solution.py:362
  9.3 7.2 %collective-permute-start.6 = (bf16[128,768]{1,0:T(8,128)(2,1)S(1)}, bf16[128,768]{1,0:T(8,128)(2,1)S(1)}, u32[]{:S(2)}, u32[]{:S(2)}) collective-permute-start(bf16[128,768]{1,0:T(8,128)(2,1)S(1)} %bitcast.24), channel_id=1, source_target_pairs={{0,4},{4,0},{8,12},{12,8},{16,20},{20,16},{24,28},{28,24},{1,5},{5... | collective-permute-start | bytes 589832 | tf_op jit(solution)/shard_map/ppermute | solution.py:359
  10.9 17.3 %collective-permute-start.11 = (bf16[384,768]{1,0:T(8,128)(2,1)S(1)}, bf16[384,768]{1,0:T(8,128)(2,1)S(1)}, u32[]{:S(2)}, u32[]{:S(2)}) collective-permute-start(bf16[384,768]{1,0:T(8,128)(2,1)S(1)} %dynamic-slice_bitcast_fusion), channel_id=1, source_target_pairs={{0,1},{1,2},{2,3},{3,0},{4,5},{5,6},{6,7},{7,4},{8,9},{9,10},{10,1... | collective-permute-start | bytes 1769480 | tf_op jit(solution)/shard_map/ppermute | solution.py:411
  14.7 8.7 %collective-permute-start.10 = (bf16[256,384]{1,0:T(8,128)(2,1)S(1)}, bf16[256,384]{1,0:T(8,128)(2,1)S(1)}, u32[]{:S(2)}, u32[]{:S(2)}) collective-permute-start(bf16[256,384]{1,0:T(8,128)(2,1)S(1)} %maximum_select_fusion.refs_0_), channel_id=1, source_target_pairs={{0,24},{4,28},{8,16},{12,20},{16,8},{20,12},{24,0},{28,4},{1,25},{... | collective-permute-start | bytes 589832 | tf_op jit(solution)/shard_map/ppermute | solution.py:362
  17.2 11.0 %collective-permute-start.9 = (bf16[256,384]{1,0:T(8,128)(2,1)S(1)}, bf16[256,384]{1,0:T(8,128)(2,1)S(1)}, u32[]{:S(2)}, u32[]{:S(2)}) collective-permute-start(bf16[256,384]{1,0:T(8,128)(2,1)S(1)} %get-tuple-element.111), channel_id=1, source_target_pairs={{0,8},{4,12},{8,0},{12,4},{16,24},{20,28},{24,16},{28,20},{1,9},{5... | collective-permute-start | bytes 589832 | tf_op jit(solution)/shard_map/ppermute | solution.py:362
  18.2 10.9 %collective-permute-start.7 = (bf16[256,384]{1,0:T(8,128)(2,1)S(1)}, bf16[256,384]{1,0:T(8,128)(2,1)S(1)}, u32[]{:S(2)}, u32[]{:S(2)}) collective-permute-start(bf16[256,384]{1,0:T(8,128)(2,1)S(1)} %get-tuple-element.113), channel_id=1, source_target_pairs={{0,16},{4,20},{8,24},{12,28},{16,0},{20,4},{24,8},{28,12},{1,17},{... | collective-permute-start | bytes 589832 | tf_op jit(solution)/shard_map/ppermute | solution.py:362
  19.7 10.8 %collective-permute-start.8 = (bf16[256,384]{1,0:T(8,128)(2,1)S(1)}, bf16[256,384]{1,0:T(8,128)(2,1)S(1)}, u32[]{:S(2)}, u32[]{:S(2)}) collective-permute-start(bf16[256,384]{1,0:T(8,128)(2,1)S(1)} %get-tuple-element.112), channel_id=1, source_target_pairs={{0,24},{4,28},{8,16},{12,20},{16,8},{20,12},{24,0},{28,4},{1,25},{... | collective-permute-start | bytes 589832 | tf_op jit(solution)/shard_map/ppermute | solution.py:362
  36.2 7.4 %collective-permute-start.16 = (bf16[272,384]{1,0:T(8,128)(2,1)S(1)}, bf16[272,384]{1,0:T(8,128)(2,1)S(1)}, u32[]{:S(2)}, u32[]{:S(2)}) collective-permute-start(bf16[272,384]{1,0:T(8,128)(2,1)S(1)} %add_convert_fusion.5.refs_1_), channel_id=1, source_target_pairs={{0,1},{1,0},{2,3},{3,2},{4,5},{5,4},{6,7},{7,6},{8,9},{9,8},{10,11... | collective-permute-start | bytes 626696 | tf_op jit(solution)/shard_map/ppermute | solution.py:371
  43.7 7.8 %collective-permute-start.20 = (bf16[256,384]{1,0:T(8,128)(2,1)S(1)}, bf16[256,384]{1,0:T(8,128)(2,1)S(1)}, u32[]{:S(2)}, u32[]{:S(2)}) collective-permute-start(bf16[256,384]{1,0:T(8,128)(2,1)S(1)} %get-tuple-element.80.refs_0_.refs_5_), channel_id=1, source_target_pairs={{0,8},{4,12},{8,0},{12,4},{16,24},{20,28},{24,16},{28,20},{1,9},{5... | collective-permute-start | bytes 589832 | tf_op jit(solution)/shard_map/ppermute | solution.py:362
  44.4 10.3 %collective-permute-start.17 = (bf16[256,384]{1,0:T(8,128)(2,1)S(1)}, bf16[256,384]{1,0:T(8,128)(2,1)S(1)}, u32[]{:S(2)}, u32[]{:S(2)}) collective-permute-start(bf16[256,384]{1,0:T(8,128)(2,1)S(1)} %get-tuple-element.80.refs_0_.refs_5_), channel_id=1, source_target_pairs={{0,16},{4,20},{8,24},{12,28},{16,0},{20,4},{24,8},{28,12},{1,17},{... | collective-permute-start | bytes 589832 | tf_op jit(solution)/shard_map/ppermute | solution.py:362
  46.8 6.6 %collective-permute-start.18 = (bf16[128,384]{1,0:T(8,128)(2,1)S(1)}, bf16[128,384]{1,0:T(8,128)(2,1)S(1)}, u32[]{:S(2)}, u32[]{:S(2)}) collective-permute-start(bf16[128,384]{1,0:T(8,128)(2,1)S(1)} %get-tuple-element.81), channel_id=1, source_target_pairs={{0,24},{4,28},{8,16},{12,20},{16,8},{20,12},{24,0},{28,4},{1,25},{... | collective-permute-start | bytes 294920 | tf_op jit(solution)/shard_map/ppermute | solution.py:362
  60.6 7.8 %collective-permute-start.29 = (bf16[256,384]{1,0:T(8,128)(2,1)S(1)}, bf16[256,384]{1,0:T(8,128)(2,1)S(1)}, u32[]{:S(2)}, u32[]{:S(2)}) collective-permute-start(bf16[256,384]{1,0:T(8,128)(2,1)S(1)} %get-tuple-element.92.refs_0_.refs_5_), channel_id=1, source_target_pairs={{0,8},{4,12},{8,0},{12,4},{16,24},{20,28},{24,16},{28,20},{1,9},{5... | collective-permute-start | bytes 589832 | tf_op jit(solution)/shard_map/ppermute | solution.py:362
  62.1 10.9 %collective-permute-start.26 = (bf16[256,384]{1,0:T(8,128)(2,1)S(1)}, bf16[256,384]{1,0:T(8,128)(2,1)S(1)}, u32[]{:S(2)}, u32[]{:S(2)}) collective-permute-start(bf16[256,384]{1,0:T(8,128)(2,1)S(1)} %get-tuple-element.92.refs_0_.refs_5_), channel_id=1, source_target_pairs={{0,16},{4,20},{8,24},{12,28},{16,0},{20,4},{24,8},{28,12},{1,17},{... | collective-permute-start | bytes 589832 | tf_op jit(solution)/shard_map/ppermute | solution.py:362
  62.7 8.5 %collective-permute-start.27 = (bf16[128,384]{1,0:T(8,128)(2,1)S(1)}, bf16[128,384]{1,0:T(8,128)(2,1)S(1)}, u32[]{:S(2)}, u32[]{:S(2)}) collective-permute-start(bf16[128,384]{1,0:T(8,128)(2,1)S(1)} %get-tuple-element.93), channel_id=1, source_target_pairs={{0,24},{4,28},{8,16},{12,20},{16,8},{20,12},{24,0},{28,4},{1,25},{... | collective-permute-start | bytes 294920 | tf_op jit(solution)/shard_map/ppermute | solution.py:362
  64.2 8.4 %collective-permute-start.28 = (bf16[128,384]{1,0:T(8,128)(2,1)S(1)}, bf16[128,384]{1,0:T(8,128)(2,1)S(1)}, u32[]{:S(2)}, u32[]{:S(2)}) collective-permute-start(bf16[128,384]{1,0:T(8,128)(2,1)S(1)} %get-tuple-element.94), channel_id=1, source_target_pairs={{0,24},{4,28},{8,16},{12,20},{16,8},{20,12},{24,0},{28,4},{1,25},{... | collective-permute-start | bytes 294920 | tf_op jit(solution)/shard_map/ppermute | solution.py:362
  69.0 6.7 %collective-permute-start.30 = (bf16[144,768]{1,0:T(8,128)(2,1)S(1)}, bf16[144,768]{1,0:T(8,128)(2,1)S(1)}, u32[]{:S(2)}, u32[]{:S(2)}) collective-permute-start(bf16[144,768]{1,0:T(8,128)(2,1)S(1)} %collective-permute-done.24.refs_0_), channel_id=1, source_target_pairs={{0,4},{4,0},{8,12},{12,8},{16,20},{20,16},{24,28},{28,24},{1,5},{5... | collective-permute-start | bytes 663560 | tf_op jit(solution)/shard_map/ppermute | solution.py:359
  77.2 7.0 %collective-permute-start.32 = (bf16[144,768]{1,0:T(8,128)(2,1)S(1)}, bf16[144,768]{1,0:T(8,128)(2,1)S(1)}, u32[]{:S(2)}, u32[]{:S(2)}) collective-permute-start(bf16[144,768]{1,0:T(8,128)(2,1)S(1)} %get-tuple-element.102), channel_id=1, source_target_pairs={{0,4},{4,0},{8,12},{12,8},{16,20},{20,16},{24,28},{28,24},{1,5},{5... | collective-permute-start | bytes 663560 | tf_op jit(solution)/shard_map/ppermute | solution.py:359
  77.4 12.5 %collective-permute-start.34 = (bf16[272,384]{1,0:T(8,128)(2,1)S(1)}, bf16[272,384]{1,0:T(8,128)(2,1)S(1)}, u32[]{:S(2)}, u32[]{:S(2)}) collective-permute-start(bf16[272,384]{1,0:T(8,128)(2,1)S(1)} %add_convert_fusion.3.refs_1_), channel_id=1, source_target_pairs={{0,1},{1,0},{2,3},{3,2},{4,5},{5,4},{6,7},{7,6},{8,9},{9,8},{10,11... | collective-permute-start | bytes 626696 | tf_op jit(solution)/shard_map/ppermute | solution.py:371
  89.9 7.9 %collective-permute-start.38 = (bf16[256,384]{1,0:T(8,128)(2,1)S(1)}, bf16[256,384]{1,0:T(8,128)(2,1)S(1)}, u32[]{:S(2)}, u32[]{:S(2)}) collective-permute-start(bf16[256,384]{1,0:T(8,128)(2,1)S(1)} %get-tuple-element.103.refs_0_.refs_5_), channel_id=1, source_target_pairs={{0,8},{4,12},{8,0},{12,4},{16,24},{20,28},{24,16},{28,20},{1,9},{5... | collective-permute-start | bytes 589832 | tf_op jit(solution)/shard_map/ppermute | solution.py:362
  90.6 10.5 %collective-permute-start.35 = (bf16[256,384]{1,0:T(8,128)(2,1)S(1)}, bf16[256,384]{1,0:T(8,128)(2,1)S(1)}, u32[]{:S(2)}, u32[]{:S(2)}) collective-permute-start(bf16[256,384]{1,0:T(8,128)(2,1)S(1)} %get-tuple-element.103.refs_0_.refs_5_), channel_id=1, source_target_pairs={{0,16},{4,20},{8,24},{12,28},{16,0},{20,4},{24,8},{28,12},{1,17},{... | collective-permute-start | bytes 589832 | tf_op jit(solution)/shard_map/ppermute | solution.py:362
  91.8 11.7 %collective-permute-start.33 = (bf16[144,768]{1,0:T(8,128)(2,1)S(1)}, bf16[144,768]{1,0:T(8,128)(2,1)S(1)}, u32[]{:S(2)}, u32[]{:S(2)}) collective-permute-start(bf16[144,768]{1,0:T(8,128)(2,1)S(1)} %add_convert_fusion.refs_2_), channel_id=1, source_target_pairs={{0,1},{1,0},{2,3},{3,2},{4,5},{5,4},{6,7},{7,6},{8,9},{9,8},{10,11... | collective-permute-start | bytes 663560 | tf_op jit(solution)/shard_map/ppermute | solution.py:371
  (25 other events, 131.2 us)
